TPU v7x, 32 devices: a whole 2x2x4 slice. The times are simulated.
32 devices in a mesh: dp: 8 (over z, y), mp: 4 (over x, core).
Axes of the slice: x: 2, y: 2, z: 4, core: 2. Of those that a mesh axis runs over, the one named last changes fastest.
Arguments:
- tokens: bfloat16 [24576, 768], P('dp'), may hold values from -6 to 6
- seg_ids: int32 [24576], P('dp'), may hold values from 0 to 180, as said below
- labels: int32 [1440], P('dp'), may hold values from 0 to 999
- w_qkv: float32 [3, 768, 768], P(None, 'dp', 'mp'), may hold values from -0.21875 to 0.21875
- m_qkv: float32 [3, 768, 768], P(None, 'dp', 'mp'), may hold values from -0.0009765625 to 0.0009765625
- v_qkv: float32 [3, 768, 768], P(None, 'dp', 'mp'), may hold values from 1.890432e-09 to 7.561728e-09
- w_out: float32 [768, 768], P('mp', 'dp'), may hold values from -0.4375 to 0.4375
- m_out: float32 [768, 768], P('mp', 'dp'), may hold values from -0.0009765625 to 0.0009765625
- v_out: float32 [768, 768], P('mp', 'dp'), may hold values from 1.890432e-09 to 7.561728e-09
- w_up: float32 [768, 3072], P('dp', 'mp'), may hold values from -0.21875 to 0.21875
- m_up: float32 [768, 3072], P('dp', 'mp'), may hold values from -0.0004272461 to 0.0004272461
- v_up: float32 [768, 3072], P('dp', 'mp'), may hold values from 4.72608e-10 to 1.890432e-09
- w_down: float32 [3072, 768], P('mp', 'dp'), may hold values from -0.109375 to 0.109375
- m_down: float32 [3072, 768], P('mp', 'dp'), may hold values from -0.0004272461 to 0.0004272461
- v_down: float32 [3072, 768], P('mp', 'dp'), may hold values from 4.72608e-10 to 1.890432e-09
- w_cls: float32 [768, 1000], P('dp', 'mp')
- m_cls: float32 [768, 1000], P('dp', 'mp'), may hold values from -0.00030517578 to 0.00030517578
- v_cls: float32 [768, 1000], P('dp', 'mp'), may hold values from 2.5e-10 to 1e-09
- norm_params: float32 [7, 768], P(None, 'dp')
- m_norm: float32 [7, 768], P(None, 'dp'), may hold values from -0.0009765625 to 0.0009765625
- v_norm: float32 [7, 768], P(None, 'dp'), may hold values from 1.890432e-09 to 7.561728e-09
- qk_gain: float32 [2, 12, 64], P(None, 'mp', 'dp'), may hold values from 1.2 to 1.6
- m_qk: float32 [2, 12, 64], P(None, 'mp', 'dp'), may hold values from -0.0009765625 to 0.0009765625
- v_qk: float32 [2, 12, 64], P(None, 'mp', 'dp'), may hold values from 1.890432e-09 to 7.561728e-09
Outputs:
- block_out: bfloat16 [24576, 768], P('dp')
- input_grad: float32 [24576, 768], P('dp')
- mean_loss: float32 [], replicated
- m_qkv_new: float32 [3, 768, 768], P(None, 'dp', 'mp')
- v_qkv_new: float32 [3, 768, 768], P(None, 'dp', 'mp')
- w_qkv_new: float32 [3, 768, 768], P(None, 'dp', 'mp')
- m_out_new: float32 [768, 768], P('mp', 'dp')
- v_out_new: float32 [768, 768], P('mp', 'dp')
- w_out_new: float32 [768, 768], P('mp', 'dp')
- m_up_new: float32 [768, 3072], P('dp', 'mp')
- v_up_new: float32 [768, 3072], P('dp', 'mp')
- w_up_new: float32 [768, 3072], P('dp', 'mp')
- m_down_new: float32 [3072, 768], P('mp', 'dp')
- v_down_new: float32 [3072, 768], P('mp', 'dp')
- w_down_new: float32 [3072, 768], P('mp', 'dp')
- m_cls_new: float32 [768, 1000], P('dp', 'mp')
- v_cls_new: float32 [768, 1000], P('dp', 'mp')
- w_cls_new: float32 [768, 1000], P('dp', 'mp')
- m_norm_new: float32 [7, 768], P(None, 'dp')
- v_norm_new: float32 [6, 768], P(None, 'dp')
- v_probe_new: float32 [768], P('dp')
- norm_new: float32 [7, 768], P(None, 'dp')
- m_qk_new: float32 [2, 12, 64], P(None, 'mp', 'dp')
- v_qk_new: float32 [2, 12, 64], P(None, 'mp', 'dp')
- qk_new: float32 [2, 12, 64], P(None, 'mp', 'dp')
Inputs may be any that keep to these rules, and one draw needn't show every extreme that they name: `seg_ids`: each of the 3 sequences of 1024 positions on a data device holds, from its start, images one after another numbered k * 60 + j for its number k on the device and j = 0, 1, ..., each of one position or more, at least 512 positions in all; the rest, one position or more at its end, holds 180.
All inputs are finite; a program needn't handle non-finite values.
Results may differ from a plain program's by a relative error of at most 0.017.
The roundings to bfloat16 on the way count: a program that leaves them out, or rounds other values in their place, can miss the bound.
Values may be sent and summed in bfloat16 or wider, within the bound.
A program may use at most 256 MiB of HBM per device.

v0:
```python
import functools

import jax
import jax.numpy as jnp
from jax import lax
from jax.experimental import pallas as pl
from jax.experimental.pallas import tpu as pltpu
from jax.sharding import PartitionSpec as P

LEN = 1024
STEP = 10
SEQ_DEV = 3
IMG_DEV = 180
PAD_ID = 180

NORM_EPS = 1e-06
MASK_FILL = -1000000000.0
BETA_ONE = 0.9
BETA_TWO = 0.999
ADAM_EPS = 1e-08
MATRIX_RATE = 0.1
MATRIX_DECAY = 0.1
GAIN_RATE = 0.8

HEAD = 64
QB = 256
QBLOCKS = LEN // QB
WINDOWS = (384, 512, 768, 1024)
ALIGN = 64
LANES = 128
F32 = jnp.float32
BF16 = jnp.bfloat16
VMEM_LIMIT = 56 * 1024 * 1024
IMG_SEQ = 60
SLOTS = 64
ANY = pl.BlockSpec(memory_space=pl.ANY)
PARAMS = pltpu.CompilerParams(vmem_limit_bytes=VMEM_LIMIT)


def dot(a, b, ca, cb):
    return lax.dot_general(a, b, (((ca,), (cb,)), ((), ())), preferred_element_type=F32)


def head_mean(values, ones_block):
    high = values.astype(BF16)
    rest = (values - high.astype(F32)).astype(BF16)
    return dot(high, ones_block, 1, 0) + dot(rest, ones_block, 1, 0)


def norm_parts(values):
    centre = values - jnp.mean(values, axis=-1, keepdims=True)
    spread = jnp.mean(centre * centre, axis=-1, keepdims=True)
    scale = lax.rsqrt(spread + NORM_EPS)
    return centre * scale, scale


def norm_back(grad, normed, scale, gain):
    scaled = grad * gain
    first = jnp.mean(scaled, axis=-1, keepdims=True)
    second = jnp.mean(scaled * normed, axis=-1, keepdims=True)
    return (scaled - first - normed * second) * scale


def head_parts(values, ones_block):
    centre = values - head_mean(values, ones_block)
    scale = lax.rsqrt(head_mean(centre * centre, ones_block) + NORM_EPS)
    return centre * scale, scale


def cost(flops, read, exps=0):
    return pl.CostEstimate(flops=int(flops), bytes_accessed=int(read), transcendentals=int(exps))


def whole(shape):
    return pl.BlockSpec(tuple(shape), lambda *_: (0,) * len(shape))


class Plan:
    def __init__(self, n_dp, n_mp, dim):
        self.n_dp, self.n_mp = n_dp, n_mp
        self.merge = 1 if dim // n_dp % 16 == 0 else 2
        self.groups = n_dp // self.merge
        self.block = dim // self.groups
        self.far = [2 * k for k in range(1, self.groups // 2)]

    def swap(self, value, axis, bits):
        size = self.n_dp if axis == "dp" else self.n_mp
        return lax.ppermute(value, axis, [(i, i ^ bits) for i in range(size)])

    def group_swap(self, value, bits):
        return self.swap(value, "dp", bits * self.merge)

    def merged(self, value, dim):
        if self.merge == 1:
            return value
        other = self.swap(value, "dp", 1)
        even = lax.axis_index("dp") % 2 == 0
        first, second = jnp.where(even, value, other), jnp.where(even, other, value)
        return jnp.concatenate([first, second], axis=dim)

    def unmerged(self, value, dim):
        if self.merge == 1:
            return value
        half = value.shape[dim] // 2
        me = lax.axis_index("dp") % 2
        mine = lax.dynamic_slice_in_dim(value, me * half, half, dim)
        theirs = lax.dynamic_slice_in_dim(value, (1 - me) * half, half, dim)
        return mine + self.swap(theirs, "dp", 1)

    def total(self, value, axis):
        size = self.n_dp if axis == "dp" else self.n_mp
        bits = 1
        while bits < size:
            value = value + self.swap(value, axis, bits)
            bits *= 2
        return value


MESH = pl.DeviceIdType.MESH


def flip(index, bits):
    bit = 1
    while bit <= bits:
        if bits & bit:
            index = index + bit * (1 - 2 * (index // bit % 2))
        bit *= 2
    return index


class Chain:
    def __init__(self, region, order, lines):
        self.region, self.steps = region, order
        self.copies = sum({"z": lines - 1, "c": 2}.get(step, 1) for step in order)


class Gatherer:
    def __init__(self, plan, send_sems, recv_sems):
        self.plan, self.send_sems, self.recv_sems = plan, send_sems, recv_sems
        self.dp, self.mp = lax.axis_index("dp"), lax.axis_index("mp")
        self.pair = self.dp % plan.merge
        group = self.dp // plan.merge
        self.z, self.y = group // 2, group % 2
        self.x, self.core = self.mp // 2, self.mp % 2
        self.lines = plan.groups // 2
        self.used = 0
        self.pending = []

    def device(self, z, y, x, core):
        return ((z * 2 + y) * self.plan.merge + self.pair, x * 2 + core)

    def here(self):
        return self.z, self.y, self.x, self.core

    def meet(self, barrier):
        z, y, x, core = self.here()
        others = [(z, 1 - y, x, core), (z, y, 1 - x, core), (z, y, x, 1 - core)]
        others += [(flip(z, k), y, x, core) for k in range(1, self.lines)]
        for other in others:
            pl.semaphore_signal(barrier, inc=1, device_id=self.device(*other), device_id_type=MESH)
        pl.semaphore_wait(barrier, len(others))

    def start(self, chain, number, source=None):
        step, done = chain.steps[number], chain.steps[:number]
        z, y, x, core = self.here()
        spot = dict(z=None if "z" in done else z, y=None if "y" in done else y, x=None if "x" in done else x, core=core)
        if step == "z":
            copies = [(spot, (flip(z, k), y, x, core)) for k in range(1, self.lines)]
        elif step == "c":
            copies = [({**spot, "x": side}, (z, y, x, 1 - core)) for side in (0, 1)]
        else:
            copies = [(spot, dict(y=(z, 1 - y, x, core), x=(z, y, 1 - x, core))[step])]
        started = []
        for place, other in copies:
            region = chain.region(**place)
            out = pltpu.make_async_remote_copy(
                src_ref=region if source is None else source,
                dst_ref=region,
                send_sem=self.send_sems.at[self.used],
                recv_sem=self.recv_sems.at[self.used],
                device_id=self.device(*other),
                device_id_type=MESH,
            )
            self.used += 1
            out.start()
            started.append(out)
        self.pending += started
        return started

    @staticmethod
    def arrive(copies):
        for out in copies:
            out.wait_recv()

    def finish(self):
        for out in self.pending:
            out.wait_send()


class Loads:
    def __init__(self, sources, targets, sems):
        self.targets = targets
        self.copies = [pltpu.make_async_copy(a, b, sems.at[i]) for i, (a, b) in enumerate(zip(sources, targets))]
        self.done = [False] * len(self.copies)
        for c in self.copies:
            c.start()

    def __getitem__(self, i):
        if not self.done[i]:
            self.copies[i].wait()
            self.done[i] = True
        return self.targets[i]


class Sender:
    def __init__(self, send_sems, recv_sems):
        self.dp, self.mp = lax.axis_index("dp"), lax.axis_index("mp")
        self.send_sems, self.recv_sems = send_sems, recv_sems
        self.started, self.used = [], 0

    def device(self, axis, bits):
        return (flip(self.dp, bits), self.mp) if axis == "dp" else (self.dp, flip(self.mp, bits))

    def meet(self, partners):
        barrier = pltpu.get_barrier_semaphore()
        for axis, bits in partners:
            pl.semaphore_signal(barrier, inc=1, device_id=self.device(axis, bits), device_id_type=MESH)
        pl.semaphore_wait(barrier, len(partners))

    def copy(self, src, dst, axis, bits):
        n = self.used
        self.used += 1
        c = pltpu.make_async_remote_copy(
            src_ref=src,
            dst_ref=dst,
            send_sem=self.send_sems.at[n],
            recv_sem=self.recv_sems.at[n],
            device_id=self.device(axis, bits),
            device_id_type=MESH,
        )
        self.started.append(c)
        c.start()
        return c

    def finish(self):
        for c in self.started:
            c.wait_send()


def gather_project(plan, tokens, qkv_block, up_block, down_block, out_block, cls_block, small_block, ones):
    rows, dim = tokens.shape
    cols = ones.shape[0]
    n_mp, merge, size = plan.n_mp, plan.merge, plan.block
    lines = plan.groups // 2
    width = up_block.shape[1]
    out_cols, class_cols = out_block.shape[1], cls_block.shape[1]
    block = 512
    blocks = rows // block
    dim_part = dim // plan.n_dp
    head_part = HEAD // plan.n_dp

    orders = [("small", "zy"), ("w_qk", "zy"), ("w_v", "zy"), ("out", "zyxc"), ("cls", "zy"), ("up", "zy"), ("down", "zx")]
    sizes = {name: Chain(None, order, lines).copies for name, order in orders}
    n_sems = sum(sizes.values())

    def kernel(x_ref, qkv_in, up_in, down_in, out_in, cls_in, small_in, ones_ref, *refs):
        low_ref, pq_ref, pk_ref, q_ref, k_ref, v_ref, w_ref, up_ref, down_ref, o_ref, c_ref, norm_ref, gain_ref, image_ref = refs[:14]
        w_buf, small_buf, low_buf, pq_buf, pk_buf, q_buf, k_buf, v_buf, send_sems, recv_sems, own_sems, out_sems = refs[14:]
        g = Gatherer(plan, send_sems, recv_sems)
        z, y, x, core = g.here()
        everything = slice(None)

        def at(v):
            return everything if v is None else v

        def wide(ref, first, count):
            columns = pl.ds(first, count)
            return lambda z, y, x, core: ref.at[at(x), core, at(z), at(y), :, columns]

        regions = dict(
            w_qk=lambda z, y, x, core: w_buf.at[pl.ds(0, 2), at(z), at(y)],
            w_v=lambda z, y, x, core: w_buf.at[pl.ds(2, 1), at(z), at(y)],
            small=lambda z, y, x, core: small_buf.at[at(z), at(y)],
            up=lambda z, y, x, core: up_ref.at[at(z), at(y)],
            down=lambda z, y, x, core: down_ref.at[at(x), at(z)],
            out=wide(o_ref, 0, out_cols),
            cls=lambda z, y, x, core: c_ref.at[at(z), at(y)],
        )
        chains = {name: Chain(regions[name], order, lines) for name, order in orders}
        sources = dict(
            w_qk=qkv_in.at[pl.ds(0, 2)],
            w_v=qkv_in.at[pl.ds(2, 1)],
            small=small_in,
            up=up_in,
            down=down_in,
            out=out_in,
            cls=cls_in,
        )
        own = {}
        for i, (name, _) in enumerate(orders):
            own[name] = pltpu.make_async_copy(sources[name], regions[name](z, y, x, core), own_sems.at[i])
            own[name].start()
        live, reached = {}, {}

        def begin(name):
            live[name] = g.start(chains[name], 0, source=sources[name])
            reached[name] = 0

        def advance(*names):
            for name in names:
                if reached[name] == len(chains[name].steps):
                    continue
                if reached[name] == 0:
                    own[name].wait()
                g.arrive(live[name])
                reached[name] += 1
                if reached[name] < len(chains[name].steps):
                    live[name] = g.start(chains[name], reached[name])

        g.meet(pltpu.get_barrier_semaphore())
        for name in ("small", "w_qk", "w_v", "out", "cls"):
            begin(name)
        advance("small", "small")

        lane = lax.broadcasted_iota(jnp.int32, (128, dim), 0)
        column = lax.broadcasted_iota(jnp.int32, (128, dim), 1)
        head_lane = lax.broadcasted_iota(jnp.int32, (128, cols), 0)
        head_column = lax.broadcasted_iota(jnp.int32, (128, cols), 1)
        norm = jnp.zeros((8, dim), F32)
        gain = jnp.zeros((8, cols), F32)
        image = jnp.zeros((8, 128), F32)
        for d in range(plan.n_dp):
            part = small_buf[d // merge // 2, d // merge % 2, d % merge]
            spread = jnp.where((column == d * dim_part + lane) & (lane < dim_part), 1.0, 0.0).astype(BF16)
            norm = norm + dot(part[0:8].astype(BF16), spread, 1, 0)
            same = (head_column // HEAD == head_lane // head_part) & (head_column % HEAD == d * head_part + head_lane % head_part)
            gain = gain + dot(part[8:16].astype(BF16), jnp.where(same, 1.0, 0.0).astype(BF16), 1, 0)
            image = image + part[16:24]
        norm_ref[...] = norm
        gain_ref[...] = gain
        image_ref[...] = image

        def first_norm(i, carry):
            at_rows = pl.ds(pl.multiple_of(i * block, block), block)
            normed, _ = norm_parts(x_ref[at_rows, :].astype(F32))
            low_buf[at_rows, :] = (normed * norm[0:1, :] + norm[1:2, :]).astype(BF16)
            return carry

        third = blocks // 3
        lax.fori_loop(0, third, first_norm, 0)
        advance("w_qk", "w_v")
        begin("up")
        begin("down")
        lax.fori_loop(third, blocks, first_norm, 0)
        outs = [pltpu.make_async_copy(low_buf, low_ref, out_sems.at[0])]
        outs[0].start()
        advance("out", "cls", "w_qk", "w_v")
        outs.append(pltpu.make_async_copy(w_buf, w_ref, out_sems.at[1]))
        outs[1].start()

        def project(i, carry):
            at_rows = pl.ds(pl.multiple_of(i * block, block), block)
            low = low_buf[at_rows, :]
            pq = dot(low, w_buf[0].reshape(dim, cols), 1, 0)
            pk = dot(low, w_buf[1].reshape(dim, cols), 1, 0)
            pq_buf[at_rows, :] = pq
            pk_buf[at_rows, :] = pk
            v_buf[at_rows, :] = dot(low, w_buf[2].reshape(dim, cols), 1, 0).astype(BF16)
            nq, _ = head_parts(pq, ones_ref[...])
            nk, _ = head_parts(pk, ones_ref[...])
            q_buf[at_rows, :] = (nq * gain[0:1, :]).astype(BF16)
            k_buf[at_rows, :] = (nk * gain[1:2, :]).astype(BF16)
            return carry

        lax.fori_loop(0, third, project, 0)
        advance("out", "up", "down")
        lax.fori_loop(third, 2 * third, project, 0)
        lax.fori_loop(2 * third, blocks, project, 0)
        pairs = ((pq_buf, pq_ref), (pk_buf, pk_ref), (q_buf, q_ref), (k_buf, k_ref), (v_buf, v_ref))
        for i, (a, b) in enumerate(pairs):
            outs.append(pltpu.make_async_copy(a, b, out_sems.at[2 + i]))
            outs[-1].start()
        advance("out", "cls", "up", "down", "out")
        g.finish()
        for c in outs:
            c.wait()

    vmem = pl.BlockSpec(memory_space=pltpu.VMEM)
    shape = jax.ShapeDtypeStruct
    wide_shape = lambda c: (n_mp // 2, 2, lines, 2, size, c)
    n_rows = lambda c, t: shape((rows, c), t)
    return pl.pallas_call(
        kernel,
        in_specs=[vmem] + [ANY] * 6 + [vmem],
        out_specs=[ANY] * 11 + [vmem] * 3,
        out_shape=[n_rows(dim, BF16), n_rows(cols, F32), n_rows(cols, F32), n_rows(cols, BF16), n_rows(cols, BF16), n_rows(cols, BF16)]
        + [
            shape((3, lines, 2, size, cols), BF16),
            shape((lines, 2, size, width), BF16),
            shape((n_mp // 2, lines, size, width), BF16),
            shape(wide_shape(out_cols), BF16),
            shape((lines, 2, size, class_cols), BF16),
            shape((8, dim), F32),
            shape((8, cols), F32),
            shape((8, 128), F32),
        ],
        scratch_shapes=[
            pltpu.VMEM((3, lines, 2, size, cols), BF16),
            pltpu.VMEM((lines, 2, merge, 24, 128), F32),
            pltpu.VMEM((rows, dim), BF16),
            pltpu.VMEM((rows, cols), F32),
            pltpu.VMEM((rows, cols), F32),
            pltpu.VMEM((rows, cols), BF16),
            pltpu.VMEM((rows, cols), BF16),
            pltpu.VMEM((rows, cols), BF16),
            pltpu.SemaphoreType.DMA((n_sems,)),
            pltpu.SemaphoreType.DMA((n_sems,)),
            pltpu.SemaphoreType.DMA((len(orders),)),
            pltpu.SemaphoreType.DMA((7,)),
        ],
        compiler_params=pltpu.CompilerParams(vmem_limit_bytes=VMEM_LIMIT, collective_id=0, has_side_effects=True),
        cost_estimate=cost(6 * rows * dim * cols, rows * dim * 8),
        name="gather_project",
    )(tokens, qkv_block, up_block, down_block, out_block, cls_block, small_block, ones)


def head_masks(cols):
    lane = lax.broadcasted_iota(jnp.int32, (1, cols), 1)
    return [(lane >= h * HEAD) & (lane < (h + 1) * HEAD) for h in range(cols // HEAD)]


def spread_heads(block, masks):
    zero = jnp.zeros_like(block)
    return jnp.concatenate([jnp.where(m, block, zero) for m in masks], axis=0)


def join_heads(stacked, masks):
    total = stacked[0:QB]
    for h in range(1, len(masks)):
        total = jnp.where(masks[h], stacked[h * QB : (h + 1) * QB], total)
    return total


def by_window(width_ref, step, body):
    width = width_ref[step]
    for number, window in enumerate(WINDOWS):
        pl.when(width == number)(functools.partial(body, window))


def key_segments(row_ref, start, window):
    at = pl.ds(pl.multiple_of(start // LANES * LANES, LANES), window)
    return jnp.where(start % LANES == 0, row_ref[0, 0:1, at], row_ref[0, 1:2, at])


def seq_specs(seq, cols):
    block = lambda c: pl.BlockSpec((QB, c), lambda b, *_: (seq * QBLOCKS + b, 0))
    all_keys = lambda c: pl.BlockSpec((LEN, c), lambda b, *_: (seq, 0))
    seg_row = pl.BlockSpec((1, 2, LEN), lambda b, *_: (seq, 0, 0))
    return block, all_keys, seg_row


def attend(plan, ids, starts, widths, q, k, v, seg_col, seg_row):
    rows, cols = q.shape
    n_mp = plan.n_mp
    share = LEN // n_mp
    per = share // QB
    seqs = rows // LEN

    def kernel(ids_ref, start_ref, width_ref, q_ref, k_ref, v_ref, col_ref, row_ref, *outs):
        out_refs, log_ref = outs[:n_mp], outs[n_mp]
        seq, block = pl.program_id(0), pl.program_id(1)
        step = seq * QBLOCKS + block
        masks = head_masks(cols)
        heads = len(masks)

        def body(window):
            start = pl.multiple_of(start_ref[step], ALIGN)
            keys = k_ref[pl.ds(start, window), :]
            values = v_ref[pl.ds(start, window), :]
            q3 = spread_heads(q_ref[...], masks)
            s = (dot(q3, keys, 1, 1) * HEAD**-0.5).reshape(heads, QB, window)
            same = col_ref[...] == key_segments(row_ref, start, window)
            s = jnp.where(same[None], s, MASK_FILL)
            top = jnp.max(s, axis=-1, keepdims=True)
            e = jnp.exp(s - top)
            total = jnp.sum(e, axis=-1, keepdims=True)
            p = (e * (1.0 / total)).astype(BF16).reshape(heads * QB, window)
            out = join_heads(dot(p, values, 1, 0), masks).astype(BF16)
            other = (block // per) ^ ids_ref[1]
            at = pl.ds(pl.multiple_of(seq * share + block % per * QB, QB), QB)
            for r in range(n_mp):

                @pl.when(other == r)
                def _():
                    out_refs[r][at, :] = out

            log = top + jnp.log(total)
            lane = lax.broadcasted_iota(jnp.int32, (QB, 128), 1)
            logs = jnp.zeros((QB, 128), F32)
            for h in range(heads):
                logs = jnp.where(lane == h, log[h], logs)
            log_ref[...] = logs

        by_window(width_ref, step, body)

    block = lambda c: pl.BlockSpec((QB, c), lambda s, b, *_: (s * QBLOCKS + b, 0))
    all_keys = lambda c: pl.BlockSpec((LEN, c), lambda s, b, *_: (s, 0))
    return pl.pallas_call(
        kernel,
        grid_spec=pltpu.PrefetchScalarGridSpec(
            num_scalar_prefetch=3,
            grid=(seqs, QBLOCKS),
            in_specs=[block(cols), all_keys(cols), all_keys(cols), block(1), pl.BlockSpec((1, 2, LEN), lambda s, b, *_: (s, 0, 0))],
            out_specs=[whole((seqs * share, cols))] * n_mp + [block(128)],
        ),
        out_shape=[jax.ShapeDtypeStruct((seqs * share, cols), BF16)] * n_mp + [jax.ShapeDtypeStruct((rows, 128), F32)],
        compiler_params=PARAMS,
        cost_estimate=cost(60 * rows * LEN * cols, rows * cols * 8, rows * LEN),
        name="attend",
    )(ids, starts, widths, q, k, v, seg_col, seg_row)


def attend_back(plan, seq, ids, starts, widths, live, q, k, v, pq, pk, gains, ones, grads, logs, seg_col, seg_row):
    rows, cols = q.shape
    n_mp = plan.n_mp
    share = LEN // n_mp
    per = share // QB

    def kernel(ids_ref, start_ref, width_ref, live_ref, q_ref, k_ref, v_ref, pq_ref, pk_ref, gain_ref, ones_ref, col_ref, row_ref, log_ref, *refs):
        grad_refs, (gq_ref, gk_ref, gv_ref, sum_ref, dk_ref, dv_ref) = refs[:n_mp], refs[n_mp:]
        block = pl.program_id(0)
        step = seq * QBLOCKS + block
        masks = head_masks(cols)
        heads = len(masks)

        @pl.when(block == 0)
        def _():
            dk_ref[...] = jnp.zeros_like(dk_ref)
            dv_ref[...] = jnp.zeros_like(dv_ref)
            sum_ref[...] = jnp.zeros_like(sum_ref)

        def back(values, grad, slot):
            ones_block = ones_ref[...]
            normed, scale = head_parts(values, ones_block)
            sum_ref[slot] += jnp.sum((grad * normed).reshape(-1, 8, cols), axis=0)
            scaled = grad * gain_ref[slot : slot + 1, :]
            first = head_mean(scaled, ones_block)
            second = head_mean(scaled * normed, ones_block)
            return ((scaled - first - normed * second) * scale).astype(BF16)

        def body(window):
            start = pl.multiple_of(start_ref[step], ALIGN)
            keys = pl.ds(start, window)
            k_win = k_ref[keys, :]
            v_win = v_ref[keys, :]
            other = (block // per) ^ ids_ref[1]
            at = pl.ds(pl.multiple_of(block % per * QB, QB), QB)
            g = grad_refs[0][at, :]
            for r in range(1, n_mp):
                g = jnp.where(other == r, grad_refs[r][at, :], g)
            q3 = spread_heads(q_ref[...], masks)
            g3 = spread_heads(g, masks)
            s = (dot(q3, k_win, 1, 1) * HEAD**-0.5).reshape(heads, QB, window)
            same = col_ref[...] == key_segments(row_ref, start, window)
            all_logs = log_ref[...]
            log = jnp.stack([all_logs[:, h : h + 1] for h in range(heads)])
            p = jnp.exp(jnp.where(same[None], s - log, MASK_FILL))
            dp = dot(g3, v_win, 1, 1).reshape(heads, QB, window)
            inner = jnp.sum(p * dp, axis=-1, keepdims=True)
            ds = (p * (dp - inner)).astype(BF16).reshape(heads * QB, window)
            p_low = p.astype(BF16).reshape(heads * QB, window)
            dv_ref[keys, :] += dot(p_low, g3, 0, 0)
            dk_ref[keys, :] += dot(ds, q3, 0, 0) * HEAD**-0.5
            dq = join_heads(dot(ds, k_win, 1, 0), masks) * HEAD**-0.5
            gq_ref[...] = back(pq_ref[...], dq, 0)

        alive = live_ref[step]

        @pl.when(alive == 0)
        def _():
            gq_ref[...] = jnp.zeros_like(gq_ref)

        @pl.when(alive != 0)
        def _():
            by_window(width_ref, step, body)

        @pl.when(block == QBLOCKS - 1)
        def _():
            gv_ref[...] = dv_ref[...].astype(BF16)

            def keys_back(i, carry):
                at = pl.ds(pl.multiple_of(i * share, share), share)
                gk_ref[at, :] = back(pk_ref[at, :], dk_ref[at, :], 1)
                return carry

            lax.fori_loop(0, n_mp, keys_back, 0)

    block, all_keys, row_spec = seq_specs(seq, cols)
    grad_spec = pl.BlockSpec((share, cols), lambda b, *_: (seq, 0))
    shape = jax.ShapeDtypeStruct((LEN, cols), BF16)
    return pl.pallas_call(
        kernel,
        grid_spec=pltpu.PrefetchScalarGridSpec(
            num_scalar_prefetch=4,
            grid=(QBLOCKS,),
            in_specs=[block(cols), all_keys(cols), all_keys(cols), block(cols), all_keys(cols), whole(gains.shape), whole(ones.shape)]
            + [block(1), row_spec, block(128)]
            + [grad_spec] * n_mp,
            out_specs=[pl.BlockSpec((QB, cols), lambda b, *_: (b, 0)), whole((LEN, cols)), whole((LEN, cols)), whole((2, 8, cols))],
            scratch_shapes=[pltpu.VMEM((LEN, cols), F32), pltpu.VMEM((LEN, cols), F32)],
        ),
        out_shape=[shape, shape, shape, jax.ShapeDtypeStruct((2, 8, cols), F32)],
        compiler_params=PARAMS,
        cost_estimate=cost(60 * LEN * LEN * cols, LEN * cols * 24, LEN * LEN),
        name="attend_back",
    )(ids, starts, widths, live, q, k, v, pq, pk, gains, ones, seg_col, seg_row, logs, *grads)


def key_windows(seg_ids):
    seg = seg_ids.reshape(-1, LEN)
    first = seg[:, ::QB]
    last = seg[:, QB - 1 :: QB]
    low = jnp.sum((seg[:, None, :] < first[:, :, None]).astype(jnp.int32), axis=2)
    high = jnp.sum((seg[:, None, :] <= last[:, :, None]).astype(jnp.int32), axis=2)
    base = low // ALIGN * ALIGN
    number = jnp.full(base.shape, len(WINDOWS) - 1, jnp.int32)
    start = jnp.zeros_like(base)
    for choice in range(len(WINDOWS) - 2, -1, -1):
        at = jnp.minimum(base, LEN - WINDOWS[choice])
        fits = high <= at + WINDOWS[choice]
        number = jnp.where(fits, choice, number)
        start = jnp.where(fits, at, start)
    live = (first != PAD_ID).astype(jnp.int32)
    return start.reshape(-1), number.reshape(-1), live.reshape(-1)


RELATIVE = (0, 2, 1, 3)


def down_copies(plan, ids_ref, parts, target, sems):
    y = ids_ref[0] % 2
    core = ids_ref[1] % 2
    copies = []
    for i, part in enumerate(parts):
        for side in range(2):
            place = target.at[side * 2 + (core ^ (i // 2)), :, y ^ (i % 2)]
            copies.append(pltpu.make_async_copy(part.at[side], place, sems.at[len(copies)]))
    return copies


def own_rows(source, target, share, n_mp, mp, sems, first):
    copies = []
    for s in range(target.shape[0] // share):
        at = pl.ds(pl.multiple_of((s * n_mp + mp) * share, share), share)
        copies.append(pltpu.make_async_copy(source.at[at], target.at[pl.ds(s * share, share)], sems.at[first + s]))
        copies[-1].start()
    return copies


def feed_up(plan, tokens, attended, params, out_w, up, up_across, down, down_across):
    dim = tokens.shape[1]
    rows, cols = attended[0].shape
    n_mp = plan.n_mp
    width = up.shape[1]
    hidden_size = n_mp * width
    share = LEN // n_mp
    seqs = rows // share
    inputs = [attended[0], out_w, up, up_across]
    shape = lambda c, t: jax.ShapeDtypeStruct((rows, c), t)
    results = [shape(dim, F32), shape(dim, BF16), shape(hidden_size, BF16), shape(hidden_size, F32)]
    n_load, n_store = len(inputs), len(results) * seqs + n_mp + 1 + seqs
    n_sems = 3 * seqs + 4

    def kernel(*refs):
        sources, (norm_ref, *sends), refs = refs[:n_load], refs[n_load : n_load + n_mp], refs[n_load + n_mp :]
        (down_in, down_across_in, tokens_in), refs = refs[:3], refs[3:]
        result_outs, att_outs, up_outs, down_outs, refs = refs[:4], refs[4 : n_mp + 3], refs[n_mp + 3 : n_mp + 5], refs[n_mp + 5 : n_mp + 7], refs[n_mp + 7 :]
        targets, bufs, att_bufs, u_bufs, refs = refs[:n_load], refs[n_load : n_load + 4], refs[n_load + 4 : n_load + n_mp + 3], refs[n_load + n_mp + 3 : n_load + n_mp + 5], refs[n_load + n_mp + 5 :]
        x_ref, load_sems, store_sems, send_sems, recv_sems = refs
        loads = Loads(sources, targets, load_sems)
        net = Sender(send_sems, recv_sems)
        x_copies = own_rows(tokens_in, x_ref, share, n_mp, net.mp, store_sems, n_store - seqs)
        net.meet([("mp", r) for r in range(1, n_mp)])
        at = lambda s: pl.ds(s * share, share)
        fetch = lambda s: [net.copy(sends[r - 1].at[at(s)], att_bufs[r - 1].at[at(s)], "mp", r) for r in range(1, n_mp)]
        rows_copies = [fetch(0)]
        up_copies = [net.copy(sources[2], u_bufs[0], "mp", 1), net.copy(sources[3], u_bufs[1], "mp", 1)]
        rows_copies += [fetch(s) for s in range(1, seqs)]
        down_copies = [net.copy(down_in, down_outs[0], "mp", 1), net.copy(down_across_in, down_outs[1], "mp", 1)]
        stores = []

        def store(src, dst):
            stores.append(pltpu.make_async_copy(src, dst, store_sems.at[len(stores)]))
            stores[-1].start()

        mid_buf, low_buf, act_buf, der_buf = bufs
        for s in range(seqs):
            here = at(s)
            att_ref, o_ref = loads[0], loads[1]
            x_copies[s].wait()
            middle = x_ref[here, :].astype(F32) + dot(att_ref[here, :], o_ref[net.mp, :, :cols], 1, 1)
            for r in range(1, n_mp):
                rows_copies[s][r - 1].wait_recv()
                middle = middle + dot(att_bufs[r - 1][here, :], o_ref[flip(net.mp, r), :, :cols], 1, 1)
            mid_buf[here, :] = middle
            normed, _ = norm_parts(middle)
            low = (normed * norm_ref[2:3, :] + norm_ref[3:4, :]).astype(BF16)
            low_buf[here, :] = low
            for c in range(n_mp):
                if c >= 2 and s == 0:
                    up_copies[c - 2].wait_recv()
                    store(u_bufs[c - 2], up_outs[c - 2])
                u_ref = loads[2 + c] if c < 2 else u_bufs[c - 2]
                columns = pl.ds(pl.multiple_of(flip(net.mp, RELATIVE[c]) * width, 128), width)
                hidden = dot(low, u_ref[...], 1, 0)
                phi = 0.5 * (1.0 + lax.erf(hidden * (0.5**0.5)))
                act_buf[here, columns] = (hidden * phi).astype(BF16)
                der_buf[here, columns] = phi + hidden * (jnp.exp(-0.5 * hidden * hidden) * 0.3989422804014327)
            for src, dst in zip(bufs, result_outs):
                store(src.at[here], dst.at[here])
        for src, dst in zip(att_bufs, att_outs):
            store(src, dst)
        for c in down_copies:
            c.wait_recv()
        net.finish()
        for c in stores:
            c.wait()

    like = lambda a: jax.ShapeDtypeStruct(a.shape, a.dtype)
    out = pl.pallas_call(
        kernel,
        in_specs=[ANY] * n_load + [pl.BlockSpec(memory_space=pltpu.VMEM)] + [ANY] * (n_mp + 2),
        out_specs=[ANY] * (n_mp + 7),
        out_shape=results + [like(a) for a in attended[1:]] + [like(up)] * 2 + [like(down)] * 2,
        scratch_shapes=[pltpu.VMEM(a.shape, a.dtype) for a in inputs + results + list(attended[1:]) + [up, up]]
        + [
            pltpu.VMEM((rows, dim), tokens.dtype),
            pltpu.SemaphoreType.DMA((n_load,)),
            pltpu.SemaphoreType.DMA((n_store,)),
            pltpu.SemaphoreType.DMA((n_sems,)),
            pltpu.SemaphoreType.DMA((n_sems,)),
        ],
        compiler_params=pltpu.CompilerParams(vmem_limit_bytes=VMEM_LIMIT, collective_id=4, has_side_effects=True),
        cost_estimate=cost(2 * rows * dim * (hidden_size + dim), rows * hidden_size * 8, rows * hidden_size * 2),
        name="feed_up",
    )(*inputs, params, *attended[1:], down, down_across, tokens)
    return out[:4], [attended[0]] + list(out[4 : n_mp + 3]), out[n_mp + 3 : n_mp + 5], out[n_mp + 5 :]


def start_all(copies):
    for c in copies:
        c.start()


def wait_all(copies):
    for c in copies:
        c.wait()


def feed_down(plan, ids, middle, active, seg_row, params, down):
    rows, dim = middle.shape
    n_mp = plan.n_mp
    hidden_size = active.shape[1]
    width = hidden_size // n_mp
    block = 256
    seqs = rows // block

    def kernel(ids_ref, mid_ref, act_ref, seg_ref, norm_ref, *refs):
        d_parts, (res_ref, block_ref, pool_ref, d_ref, sems) = refs[:4], refs[4:]
        seq = pl.program_id(0)
        copies = down_copies(plan, ids_ref, d_parts, d_ref, sems)

        @pl.when(seq == 0)
        def _():
            start_all(copies)
            wait_all(copies)

        result = mid_ref[...]
        for c in range(n_mp):
            result = result + dot(act_ref[:, c * width : (c + 1) * width], d_ref[c].reshape(dim, width), 1, 1)
        res_ref[...] = result
        block_ref[...] = result.astype(BF16)
        normed, _ = norm_parts(result)
        final = normed * norm_ref[4:5, :] + norm_ref[5:6, :]
        probe = jnp.broadcast_to(norm_ref[6:7, :], (8, dim))
        score = lax.dot_general(
            probe, final, (((1,), (1,)), ((), ())), precision=lax.Precision.HIGHEST, preferred_element_type=F32
        )[0:1]
        slot = lax.broadcasted_iota(jnp.int32, (SLOTS, block), 0)
        member = (seg_ref[0, 0:1, :] - seq * IMG_SEQ == slot) & (slot < IMG_SEQ)
        top = jnp.max(jnp.where(member, score, MASK_FILL), axis=1, keepdims=True)
        e = jnp.exp(jnp.where(member, score - top, MASK_FILL))
        e = jnp.where(member, e, 0.0)
        total = jnp.sum(e, axis=1, keepdims=True)
        low = final.astype(BF16)
        high = e.astype(BF16)
        rest = (e - high.astype(F32)).astype(BF16)
        pool_ref[:, :dim] = dot(high, low, 1, 0) + dot(rest, low, 1, 0)
        lane = lax.broadcasted_iota(jnp.int32, (SLOTS, 128), 1)
        pool_ref[:, dim:] = jnp.where(lane == 0, top, jnp.where(lane == 1, total, 0.0))

    row = lambda c: pl.BlockSpec((block, c), lambda i, *_: (i, 0))
    return pl.pallas_call(
        kernel,
        grid_spec=pltpu.PrefetchScalarGridSpec(
            num_scalar_prefetch=1,
            grid=(seqs,),
            in_specs=[row(dim), row(hidden_size), pl.BlockSpec((1, 2, block), lambda i, ids_ref: (i, 0, ids_ref[1])), whole(params.shape)] + [ANY] * 4,
            out_specs=[row(dim), row(dim), pl.BlockSpec((SLOTS, dim + 128), lambda i, *_: (i, 0))],
            scratch_shapes=[pltpu.VMEM((n_mp, plan.groups // 2, 2, plan.block, width), BF16), pltpu.SemaphoreType.DMA((8,))],
        ),
        out_shape=[
            jax.ShapeDtypeStruct((rows, dim), F32),
            jax.ShapeDtypeStruct((rows, dim), BF16),
            jax.ShapeDtypeStruct((seqs * SLOTS, dim + 128), F32),
        ],
        compiler_params=PARAMS,
        cost_estimate=cost(2 * rows * dim * hidden_size, rows * hidden_size * 4),
        name="feed_down",
    )(ids, middle, active, seg_row, params, *down)


def classify(plan, pool, labels, images, cls, cls_across, class_count):
    slots, full = pool.shape
    dim = full - 128
    n_mp = plan.n_mp
    class_cols = cls.shape[1]
    wide = n_mp * class_cols

    part = slots // 2

    def combined(mine, other, lower, ref_rows):
        first, second = jnp.where(lower, mine, other), jnp.where(lower, other, mine)
        top_a, top_b = first[:, dim : dim + 1], second[:, dim : dim + 1]
        top = jnp.maximum(top_a, top_b)
        weight_a, weight_b = jnp.exp(top_a - top), jnp.exp(top_b - top)
        total = first[:, dim + 1 : dim + 2] * weight_a + second[:, dim + 1 : dim + 2] * weight_b
        ref_rows[:, :dim] = first[:, :dim] * weight_a + second[:, :dim] * weight_b
        lane = lax.broadcasted_iota(jnp.int32, (first.shape[0], 128), 1)
        ref_rows[:, dim:] = jnp.where(lane == 0, top, jnp.where(lane == 1, total, 0.0))

    def kernel(part_ref, label_ref, images_ref, c_in, c_across, grad_ref, stat_ref, loss_ref, cls_ref, c_ref, l_ref, pool_ref, got_ref, own_sems, send_sems, recv_sems):
        net = Sender(send_sems, recv_sems)
        me, mp = net.dp // plan.merge, net.mp
        side, core = mp // 2, mp % 2
        net.meet([("mp", 1), ("mp", 2)])
        first_copy = net.copy(part_ref, got_ref.at[0], "mp", 1)
        weights = [net.copy(a, c_ref.at[flip(mp, r)], "mp", 1) for a, r in ((c_in, 0), (c_across, 2))]
        own_copies = [pltpu.make_async_copy(a, c_ref.at[flip(mp, r)], own_sems.at[r // 2]) for a, r in ((c_in, 0), (c_across, 2))]
        start_all(own_copies)
        first_copy.wait_recv()
        combined(part_ref[...], got_ref[0], core == 0, pool_ref.at[0])
        own = pl.ds(pl.multiple_of(core * part, 8), part)
        net.copy(pool_ref.at[0, own], got_ref.at[1, pl.ds(0, part)], "mp", 2).wait_recv()
        combined(pool_ref[0, own, :], got_ref[1, 0:part, :], side == 0, pool_ref.at[1, own])
        net.copy(pool_ref.at[1, own], pool_ref.at[1, own], "mp", 1).wait_recv()
        for c in weights:
            c.wait_recv()
        wait_all(own_copies)
        net.finish()
        pool_ref = pool_ref.at[1]
        top = pool_ref[:, dim : dim + 1]
        total = pool_ref[:, dim + 1 : dim + 2]
        present = jnp.where(total > 0, 1.0, 0.0)
        safe = total + (1.0 - present)
        pooled = pool_ref[:, :dim] / safe
        low = pooled.astype(BF16)
        logits = jnp.concatenate([dot(low, c_ref[c], 1, 0) for c in range(n_mp)], axis=1)
        column = lax.broadcasted_iota(jnp.int32, (slots, wide), 1)
        logits = jnp.where(column % class_cols < class_count, logits, MASK_FILL)
        row_top = jnp.max(logits, axis=1, keepdims=True)
        log_total = row_top + jnp.log(jnp.sum(jnp.exp(logits - row_top), axis=1, keepdims=True))
        chosen = jnp.where(column == label_ref[...], 1.0, 0.0)
        label_logit = jnp.sum(chosen * logits, axis=1, keepdims=True)
        loss = jnp.sum(present * (log_total - label_logit), axis=0, keepdims=True)
        loss_ref[...] = jnp.broadcast_to(loss, loss_ref.shape)
        scale = present / images_ref[0:1, 0:1]
        grad = ((jnp.exp(logits - log_total) - chosen) * scale).astype(BF16)
        l_ref[...] = grad
        row_grad = sum(dot(grad[:, c * class_cols : (c + 1) * class_cols], c_ref[c], 1, 1) for c in range(n_mp)).astype(BF16)
        grad_ref[...] = row_grad
        inner = jnp.sum(row_grad.astype(F32) * pooled, axis=1, keepdims=True)
        lane = lax.broadcasted_iota(jnp.int32, (slots, 128), 1)
        stat_ref[...] = jnp.where(lane == 0, top, jnp.where(lane == 1, 1.0 / safe, jnp.where(lane == 2, inner, 0.0)))
        own = l_ref[:, pl.ds(pl.multiple_of(mp * class_cols, 128), class_cols)]
        grad_cls = dot(low, own, 0, 0)
        for g in range(plan.groups):
            at = (g % 2 + me % 2) % 2 * (plan.groups // 2) + g // 2
            cls_ref[at] = grad_cls[g * plan.block : (g + 1) * plan.block].astype(BF16)

    vmem = pl.BlockSpec(memory_space=pltpu.VMEM)
    return pl.pallas_call(
        kernel,
        in_specs=[vmem] * 3 + [ANY] * 2,
        out_specs=[vmem] * 4,
        out_shape=[
            jax.ShapeDtypeStruct((slots, dim), BF16),
            jax.ShapeDtypeStruct((slots, 128), F32),
            jax.ShapeDtypeStruct((8, 128), F32),
            jax.ShapeDtypeStruct((plan.groups, plan.block, class_cols), BF16),
        ],
        scratch_shapes=[
            pltpu.VMEM((n_mp,) + cls.shape, BF16),
            pltpu.VMEM((slots, wide), BF16),
            pltpu.VMEM((2, slots, full), F32),
            pltpu.VMEM((2, slots, full), F32),
            pltpu.SemaphoreType.DMA((2,)),
            pltpu.SemaphoreType.DMA((5,)),
            pltpu.SemaphoreType.DMA((5,)),
        ],
        compiler_params=pltpu.CompilerParams(vmem_limit_bytes=VMEM_LIMIT, collective_id=3, has_side_effects=True),
        cost_estimate=cost(6 * slots * dim * wide, dim * wide * 2),
        name="classify",
    )(pool, labels, images, cls, cls_across)


def split_three(values):
    high = values.astype(BF16)
    rest = values - high.astype(F32)
    middle = rest.astype(BF16)
    low = (rest - middle.astype(F32)).astype(BF16)
    return high, middle, low


def feed_back(plan, ids, result, middle, slope, row_grads, stats, seg_col, params, out_w, up, down, cols):
    rows, dim = result.shape
    n_mp = plan.n_mp
    width = up[0].shape[1]
    hidden_size = n_mp * width
    block = 256

    def kernel(ids_ref, res_ref, mid_ref, der_ref, pg_ref, stat_ref, seg_ref, norm_ref, o_ref, *refs):
        u_refs, d_parts, refs = refs[:n_mp], refs[n_mp : n_mp + 4], refs[n_mp + 4 :]
        rlow_ref, hlow_ref, mlow_ref, mgrad_ref, *refs = refs
        ag_refs, (sums_ref, d_ref, sems) = refs[:n_mp], refs[n_mp:]
        mp = ids_ref[1]
        seq = pl.program_id(0)
        copies = down_copies(plan, ids_ref, d_parts, d_ref, sems)

        @pl.when(seq == 0)
        def _():
            start_all(copies)
            sums_ref[...] = jnp.zeros_like(sums_ref)

        normed, scale = norm_parts(res_ref[...])
        gain, probe = norm_ref[4:5, :], norm_ref[6:7, :]
        final = normed * gain + norm_ref[5:6, :]
        score = jnp.sum(final * probe, axis=1, keepdims=True)
        slot = lax.broadcasted_iota(jnp.int32, (block, SLOTS), 1)
        member = (seg_ref[...] - seq * IMG_SEQ == slot) & (slot < IMG_SEQ)
        held = jnp.max(jnp.where(member, 1.0, 0.0), axis=1, keepdims=True)
        one = jnp.where(member, 1.0, 0.0).astype(BF16)
        row_stat = sum(dot(one, part, 1, 0) for part in split_three(stat_ref[...]))
        top, inverse, inner = row_stat[:, 0:1], row_stat[:, 1:2], row_stat[:, 2:3]
        share = jnp.exp(jnp.where(held > 0, score - top, 0.0)) * inverse * held
        row_grad = dot(one, pg_ref[...], 1, 0)
        share_low = share.astype(BF16).astype(F32)
        share_grad = jnp.sum(row_grad * final.astype(BF16).astype(F32), axis=1, keepdims=True)
        score_grad = share * (share_grad - inner)
        final_grad = share_low * row_grad + score_grad * probe
        add = lambda slot, value: sums_ref.at[slot].__setitem__(
            ..., sums_ref[slot] + jnp.sum(value.reshape(-1, 8, dim), axis=0)
        )
        add(4, score_grad * final)
        add(2, final_grad * normed)
        add(3, final_grad)
        result_grad = norm_back(final_grad, normed, scale, gain)
        result_low = result_grad.astype(BF16)
        rlow_ref[...] = result_low
        pl.when(seq == 0)(lambda: wait_all(copies))
        second = jnp.zeros((block, dim), F32)
        for c in range(n_mp):
            other = mp ^ RELATIVE[c]
            at = pl.ds(pl.multiple_of(other * width, 128), width)
            hidden_low = (der_ref[:, at] * dot(result_low, d_ref[other].reshape(dim, width), 1, 0)).astype(BF16)
            hlow_ref[:, at] = hidden_low
            second = second + dot(hidden_low, u_refs[c][...], 1, 1)
        normed_two, scale_two = norm_parts(mid_ref[...])
        add(0, second * normed_two)
        add(1, second)
        middle_grad = result_grad + norm_back(second, normed_two, scale_two, norm_ref[2:3, :])
        mgrad_ref[...] = middle_grad
        middle_low = middle_grad.astype(BF16)
        mlow_ref[...] = middle_low
        for r in range(n_mp):
            ag_refs[r][...] = dot(middle_low, o_ref[mp ^ r, :, :cols], 1, 0).astype(BF16)

    row = lambda c: pl.BlockSpec((block, c), lambda i, *_: (i, 0))
    shape = lambda c, t: jax.ShapeDtypeStruct((rows, c), t)
    slots = lambda c: pl.BlockSpec((SLOTS, c), lambda i, *_: (i, 0))
    own_row = pl.BlockSpec((block, 1), lambda i, ids_ref: (i * n_mp + ids_ref[1], 0))
    return pl.pallas_call(
        kernel,
        grid_spec=pltpu.PrefetchScalarGridSpec(
            num_scalar_prefetch=1,
            grid=(rows // block,),
            in_specs=[row(dim), row(dim), row(hidden_size), slots(dim), slots(128), own_row, whole(params.shape), whole(out_w.shape)]
            + [whole(up[0].shape)] * n_mp
            + [ANY] * 4,
            out_specs=[row(dim), row(hidden_size), row(dim), row(dim)] + [row(cols)] * n_mp + [whole((5, 8, dim))],
            scratch_shapes=[pltpu.VMEM((n_mp, plan.groups // 2, 2, plan.block, width), BF16), pltpu.SemaphoreType.DMA((8,))],
        ),
        out_shape=[shape(dim, BF16), shape(hidden_size, BF16), shape(dim, BF16), shape(dim, F32)]
        + [shape(cols, BF16)] * n_mp
        + [jax.ShapeDtypeStruct((5, 8, dim), F32)],
        compiler_params=PARAMS,
        cost_estimate=cost(2 * rows * dim * (2 * hidden_size + dim), rows * hidden_size * 8),
        name="feed_back",
    )(ids, result, middle, slope, row_grads, stats, seg_col, params, out_w, *up, *down)


def weight_grads(plan, pairs, out_pair, cls_blocks, sends):
    dim = pairs[0][0].shape[1]
    rows = pairs[0][0].shape[0]
    n_mp, size, merge = plan.n_mp, plan.block, plan.merge
    lines = plan.groups // 2
    width = pairs[0][1].shape[1] // n_mp
    cols = out_pair[1][0].shape[1]
    out_cols = -(-cols // 128) * 128
    inputs = [a for pair in pairs for a in pair] + [out_pair[0]] + list(out_pair[1]) + [cls_blocks]
    n_load = len(inputs)
    widths = [width] * len(pairs) + [out_cols]
    n = len(widths)

    def kernel(*refs):
        sources, ag_in, refs = refs[:n_load], refs[n_load : n_load + n_mp - 1], refs[n_load + n_mp - 1 :]
        keep_out, send_out, cls_out, ag_out, refs = refs[:n], refs[n : 2 * n], refs[2 * n], refs[2 * n + 1 : 2 * n + n_mp], refs[2 * n + n_mp :]
        targets, refs = refs[:n_load], refs[n_load:]
        send_buf, got_buf, own_buf, keep_buf, low_buf = (refs[i * n : (i + 1) * n] for i in range(5))
        cls_got, load_sems, store_sems, send_sems, recv_sems = refs[5 * n :]
        loads = Loads(sources, targets, load_sems)
        net = Sender(send_sems, recv_sems)
        y = net.dp // merge % 2
        side, core = net.mp // 2, net.mp % 2
        net.meet([("mp", 1), ("mp", 2), ("mp", 3), ("dp", merge)])
        ag = [net.copy(a, b, "mp", r) for r, (a, b) in enumerate(zip(ag_in, ag_out), start=1)]
        cls_ref = loads[n_load - 1]
        cls_copy = net.copy(cls_ref.at[1], cls_got, "dp", merge)
        stores = []

        def grad(number, other_side, other_core):
            if number < len(pairs):
                left, right = loads[2 * number], loads[2 * number + 1]
                at = flip(side, other_side) * 2 + flip(core, other_core)
                return dot(left[...], right[:, pl.ds(pl.multiple_of(at * width, 128), width)], 0, 0)
            left = loads[2 * len(pairs)]
            right = loads[2 * len(pairs) + 1 + other_side * 2 + other_core]
            value = dot(left[...], right[...], 0, 0)
            return jnp.concatenate([value, jnp.zeros((dim, out_cols - cols), F32)], axis=1) if out_cols != cols else value

        split = lambda value: value.reshape(lines, 2, size, value.shape[1])
        cores = []
        for i in range(n):
            for other_side in (0, 1):
                send_buf[i][flip(side, other_side)] = split(grad(i, other_side, 1).astype(BF16))
            cores.append(net.copy(send_buf[i], got_buf[i], "mp", 1))
            for other_side in (0, 1):
                own_buf[i][flip(side, other_side)] = split(grad(i, other_side, 0))
        for i in range(n):
            cores[i].wait_recv()
            if i == 0:
                keep_buf[i][...] = own_buf[i][side] + got_buf[i][side].astype(F32)
                low_buf[i][...] = (own_buf[i][1 - side] + got_buf[i][1 - side].astype(F32)).astype(BF16)
            else:
                for x in (0, 1):
                    keep_buf[i][x] = own_buf[i][x, :, y] + got_buf[i][x, :, y].astype(F32)
                    low_buf[i][x] = (own_buf[i][x, :, 1 - y] + got_buf[i][x, :, 1 - y].astype(F32)).astype(BF16)
            for a, b in ((low_buf[i], send_out[i]), (keep_buf[i], keep_out[i])):
                stores.append(pltpu.make_async_copy(a, b, store_sems.at[len(stores)]))
                stores[-1].start()
        cls_copy.wait_recv()
        cls_out[...] = cls_ref[0].astype(F32) + cls_got[...].astype(F32)
        for c in ag:
            c.wait_recv()
        net.finish()
        for c in stores:
            c.wait()

    shape = jax.ShapeDtypeStruct
    vmem = pl.BlockSpec(memory_space=pltpu.VMEM)
    full = [(2, lines, 2, size, w) for w in widths]
    half = [(lines, 2, size, widths[0])] + [(2, lines, size, w) for w in widths[1:]]
    n_sems = n + n_mp
    out = pl.pallas_call(
        kernel,
        in_specs=[ANY] * (n_load + n_mp - 1),
        out_specs=[ANY] * (2 * n) + [vmem] + [ANY] * (n_mp - 1),
        out_shape=[shape(h, F32) for h in half]
        + [shape(h, BF16) for h in half]
        + [shape(cls_blocks.shape[1:], F32)]
        + [shape(a.shape, a.dtype) for a in sends],
        scratch_shapes=[pltpu.VMEM(a.shape, a.dtype) for a in inputs]
        + [pltpu.VMEM(f, BF16) for f in full]
        + [pltpu.VMEM(f, BF16) for f in full]
        + [pltpu.VMEM(f, F32) for f in full]
        + [pltpu.VMEM(h, F32) for h in half]
        + [pltpu.VMEM(h, BF16) for h in half]
        + [
            pltpu.VMEM(cls_blocks.shape[1:], BF16),
            pltpu.SemaphoreType.DMA((n_load,)),
            pltpu.SemaphoreType.DMA((2 * n,)),
            pltpu.SemaphoreType.DMA((n_sems,)),
            pltpu.SemaphoreType.DMA((n_sems,)),
        ],
        compiler_params=pltpu.CompilerParams(vmem_limit_bytes=60 * 1024 * 1024, collective_id=2, has_side_effects=True),
        cost_estimate=cost(2 * rows * dim * n_mp * sum(widths), rows * width * n_mp * 8),
        name="grads",
    )(*inputs, *sends)
    return out[:n], out[n : 2 * n], out[2 * n], out[2 * n + 1 :]


def assemble(plan, ids, parts, dtype, name):
    n_mp = plan.n_mp
    seqs, share, dim = parts[0].shape[-3:]
    joint = len(parts) == 1

    def kernel(ids_ref, *refs):
        part_refs, out_ref = refs[:-1], refs[-1]
        if joint:
            out_ref[...] = part_refs[0][...].astype(dtype)
            return
        for i, ref in enumerate(part_refs):

            @pl.when(pl.program_id(0) == i)
            def _():
                out_ref[...] = ref[...].astype(dtype)

    relative = lambda i: i % 2 * 2 + i // 2
    each = pl.BlockSpec((None, seqs, share, dim), lambda i, *_: (i, 0, 0, 0))
    return pl.pallas_call(
        kernel,
        grid_spec=pltpu.PrefetchScalarGridSpec(
            num_scalar_prefetch=1,
            grid=(n_mp,),
            in_specs=[each] if joint else [whole((seqs, share, dim))] * n_mp,
            out_specs=pl.BlockSpec((seqs, None, share, dim), lambda i, ids_ref: (0, ids_ref[1] ^ relative(i), 0, 0)),
        ),
        out_shape=jax.ShapeDtypeStruct((seqs, n_mp, share, dim), dtype),
        compiler_params=PARAMS,
        cost_estimate=cost(0, seqs * n_mp * share * dim * 8),
        name=name,
    )(ids, *parts).reshape(seqs * n_mp * share, dim)


def finish(plan, low, proj_grads, w, middle_grad, tokens, params, row_sums, gain_sums, loss, zx, yz, z_only):
    seqs = len(proj_grads)
    dim = low.shape[1]
    cols = w.shape[2]
    n_mp = plan.n_mp
    share = LEN // n_mp
    lines, size, merge = plan.groups // 2, plan.block, plan.merge
    dp_bits = [1 << i for i in range(plan.n_dp.bit_length() - 1)]
    far = [2 * k * merge for k in range(1, lines)]
    partners = [("mp", 1), ("mp", 2)] + [("dp", b) for b in sorted(set(dp_bits + far + [merge]))]
    stages = [("mp", 1), ("mp", 2)] + [("dp", b) for b in dp_bits]
    inputs = [w] + [g for seq in proj_grads for g in seq] + [a for pair in zx + yz for a in pair] + list(z_only)
    inputs += [low, middle_grad]
    smalls = [params, row_sums, loss] + list(gain_sums)
    n_in = len(inputs)
    n_zx, n_yz, n_z = len(zx), len(yz), len(z_only)
    n_sems = (lines - 1) * (n_zx + n_yz + n_z + 1) + n_zx + n_yz + 1 + 4 * seqs + len(stages)
    n_out = 3 + n_zx + n_yz + n_z

    def kernel(*refs):
        sources, (norm_ref, row_sum_ref, loss_ref, *gain_refs), refs = refs[:n_in], refs[n_in : n_in + 3 + seqs], refs[n_in + 3 + seqs :]
        tokens_in, refs = refs[0], refs[1:]
        rows_ref, qkv_out, total_ref, *owned = refs[:n_out]
        zx_out, yz_out, z_out = owned[:n_zx], owned[n_zx : n_zx + n_yz], owned[n_zx + n_yz :]
        scratch = list(refs[n_out:])
        take = lambda n: [scratch.pop(0) for _ in range(n)]
        targets = take(n_in)
        t_keep, t_send, t_got, t_mine, x_send, x_got, acc, q_low, q_y, q_send, q_z, got_sums, load_sems, send_sems, recv_sems, x_ref = take(16)
        zx_low, zx_got, zx_send, zx_last = take(n_zx), take(n_zx), take(n_zx), take(n_zx)
        yz_low, yz_got, yz_send, yz_last = take(n_yz), take(n_yz), take(n_yz), take(n_yz)
        z_low, z_got = take(n_z), take(n_z)
        loads = Loads(sources, targets, load_sems)
        net = Sender(send_sems, recv_sems)
        copy = net.copy
        own_copies = own_rows(tokens_in, x_ref, share, n_mp, net.mp, load_sems, n_in)
        group = net.dp // merge
        z, y = group // 2, group % 2
        side, core = net.mp // 2, net.mp % 2
        net.meet(partners)
        others = range(1, lines)
        to_z = lambda src, dst, k: copy(src, dst, "dp", 2 * k * merge)
        pair_from = 1 + 3 * seqs
        pair = lambda i: (loads[pair_from + 2 * i], loads[pair_from + 2 * i + 1])
        both = lambda a, b, *at: a[at].astype(F32) + b[at].astype(F32)
        z_from = pair_from + 2 * (n_zx + n_yz)
        y_copies, z_copies = [], []

        def over_y(i):
            a, b = pair(n_zx + i)
            for line in range(lines):
                yz_low[i][line] = both(a, b, line, 1 - y).astype(BF16)
            y_copies.append(copy(yz_low[i], yz_got[i], "dp", merge))

        def over_z(i):
            a, b = pair(i)
            for k in others:
                for s in (0, 1):
                    zx_low[i][k - 1, s] = both(a, b, s, flip(z, k)).astype(BF16)
                z_copies.append(to_z(zx_low[i].at[k - 1], zx_got[i].at[k - 1], k))

        def only_z(i):
            for k in others:
                z_low[i][k - 1] = loads[z_from + i][flip(z, k)].astype(BF16)
                z_copies.append(to_z(z_low[i].at[k - 1], z_got[i].at[k - 1], k))

        w_ref = loads[0]
        pg = [[loads.targets[1 + 3 * s + p] for p in range(3)] for s in range(seqs)]
        core_copies = []
        x_copies = []

        def over_x(s):
            core_copies[s].wait_recv()
            x_send[s] = (t_keep[s, 1].astype(F32) + t_got[s, 1].astype(F32)).astype(BF16)
            x_copies.append(copy(x_send.at[s], x_got.at[s], "mp", 2))
            t_mine[s] = t_keep[s, 0].astype(F32) + t_got[s, 0].astype(F32)

        for s in range(seqs):
            for p in range(3):
                loads[1 + 3 * s + p]

            def terms(target, i, carry):
                to_other = i // 2
                row_side = side + i % 2 * (1 - 2 * side)
                row_core = core + (1 - to_other) * (1 - 2 * core)
                at = pl.ds(pl.multiple_of((row_side * 2 + row_core) * share, share), share)
                gq, gk, gv = (ref[at, :] for ref in pg[s])
                total = dot(gq, w_ref[0], 1, 1) + dot(gk, w_ref[1], 1, 1) + dot(gv, w_ref[2], 1, 1)
                target[s, i % 2] = total.astype(BF16)
                return carry

            lax.fori_loop(0, 2, functools.partial(terms, t_send), 0)
            core_copies.append(copy(t_send.at[s], t_got.at[s], "mp", 1))
            lax.fori_loop(2, 4, functools.partial(terms, t_keep), 0)
            if s == 0:
                over_z(0)
                over_x(0)
            elif s > 1:
                over_x(s - 1)
            if s == 1:
                for i in range(n_yz):
                    over_y(i)
                for i in range(1, n_zx):
                    over_z(i)
                for i in range(n_z):
                    only_z(i)
        if seqs > 1:
            over_x(seqs - 1)

        low_ref = loads[n_in - 2]
        for s in range(seqs):
            for p in range(3):
                part = dot(low_ref[s * LEN : (s + 1) * LEN, :], pg[s][p][...], 0, 0)
                acc[p] = part if s == 0 else acc[p] + part
        for p in range(3):
            q_low[p] = acc[p].reshape(lines, 2, size, cols).astype(BF16)
        y_copy = copy(q_low.at[:, :, 1 - y], q_y, "dp", merge)

        mid_ref = loads[n_in - 1]
        for c in own_copies:
            c.wait()
        total_ref[...] = jnp.zeros_like(total_ref)
        for n in range(5):
            total_ref[2 + n : 3 + n, :] = jnp.sum(row_sum_ref[n], axis=0, keepdims=True)
        for n in range(2):
            gain_sum = sum(jnp.sum(ref[n], axis=0, keepdims=True) for ref in gain_refs)
            total_ref[8 + n : 9 + n, 0:cols] = gain_sum
        total_ref[10:11, 0:128] = loss_ref[0:1, :]
        row_copies = []
        q_copies = []
        for s in range(seqs):
            at = slice(s * share, (s + 1) * share)
            normed, scale = norm_parts(x_ref[at, :].astype(F32))
            x_copies[s].wait_recv()
            first = t_mine[s] + x_got[s].astype(F32)
            total_ref[0:1, :] += jnp.sum(first * normed, axis=0, keepdims=True)
            total_ref[1:2, :] += jnp.sum(first, axis=0, keepdims=True)
            rows_ref[0, s] = (mid_ref[at, :] + norm_back(first, normed, scale, norm_ref[0:1, :])).astype(BF16)
            row_copies.append(copy(rows_ref.at[0, s], rows_ref.at[1, s], "mp", 2))
            if s == 0:
                y_copy.wait_recv()
                for line in range(lines):
                    for p in range(3):
                        rows_at = pl.ds(pl.multiple_of((line * 2 + y) * size, 8), size)
                        q_send[line, p] = (acc[p, rows_at, :] + q_y[p, line].astype(F32)).astype(BF16)
                q_copies = [to_z(q_send.at[flip(z, k)], q_z.at[k - 1], k) for k in others]
            if s == min(1, seqs - 1):
                for i in range(n_yz):
                    a, b = pair(n_zx + i)
                    y_copies[i].wait_recv()
                    for k in others:
                        at_z = flip(z, k)
                        yz_send[i][k - 1] = (both(a, b, at_z, y) + yz_got[i][at_z].astype(F32)).astype(BF16)
                        z_copies.append(to_z(yz_send[i].at[k - 1], yz_last[i].at[k - 1], k))
        mate_copies, last_copies = [], []

        def zx_last_step(i):
            for c in z_copies[i * (lines - 1) : (i + 1) * (lines - 1)]:
                c.wait_recv()
            a, b = pair(i)
            other = both(a, b, 1 - side, z) + sum(zx_got[i][k - 1, 1 - side].astype(F32) for k in others)
            zx_send[i][...] = other.astype(BF16)
            last_copies.append(copy(zx_send[i], zx_last[i], "mp", 2))
            zx_out[i][...] = both(a, b, side, z) + sum(zx_got[i][k - 1, side].astype(F32) for k in others)

        def mate(n):
            row_copies[n].wait_recv()
            mate_copies.append(copy(rows_ref.at[pl.ds(0, 2), n], rows_ref.at[pl.ds(2, 2), n], "mp", 1))

        between = [functools.partial(zx_last_step, i) for i in range(n_zx)] + [functools.partial(mate, n) for n in range(seqs)]
        for n, (axis, bits) in enumerate(stages):
            count = 8 if axis == "mp" else 16
            stage = copy(total_ref.at[pl.ds(0, count)], got_sums.at[n, pl.ds(0, count)], axis, bits)
            net.started.pop()
            if between:
                between.pop(0)()
            stage.wait()
            total_ref[0:count, :] += got_sums[n, 0:count, :]
        for step in between:
            step()
        for c in z_copies[n_zx * (lines - 1) :]:
            c.wait_recv()
        for i in range(n_yz):
            a, b = pair(n_zx + i)
            own = both(a, b, z, y) + yz_got[i][z].astype(F32)
            yz_out[i][...] = own + sum(yz_last[i][k - 1].astype(F32) for k in others)
        for i in range(n_z):
            z_out[i][...] = loads[z_from + i][z] + sum(z_got[i][k - 1].astype(F32) for k in others)
        for c in q_copies:
            c.wait_recv()
        for p in range(3):
            rows_at = pl.ds(pl.multiple_of((z * 2 + y) * size, 8), size)
            own = acc[p, rows_at, :] + q_y[p, z].astype(F32)
            qkv_out[p] = own + sum(q_z[k - 1, p].astype(F32) for k in others)
        for i, c in enumerate(last_copies):
            c.wait_recv()
            zx_out[i][...] += zx_last[i][...].astype(F32)
        for c in mate_copies:
            c.wait_recv()
        net.finish()

    vmem = pl.BlockSpec(memory_space=pltpu.VMEM)
    shape = jax.ShapeDtypeStruct
    blk = (3, size, cols)
    piece = lambda a: a.shape[-2:]
    buf = lambda a, lead, t=BF16: pltpu.VMEM(tuple(lead) + piece(a), t)
    three = lines - 1
    scratch = [pltpu.VMEM(a.shape, a.dtype) for a in inputs]
    scratch += [
        pltpu.VMEM((seqs, 2, share, dim), BF16),
        pltpu.VMEM((seqs, 2, share, dim), BF16),
        pltpu.VMEM((seqs, 2, share, dim), BF16),
        pltpu.VMEM((seqs, share, dim), F32),
        pltpu.VMEM((seqs, share, dim), BF16),
        pltpu.VMEM((seqs, share, dim), BF16),
        pltpu.VMEM((3, dim, cols), F32),
        pltpu.VMEM((3, lines, 2, size, cols), BF16),
        pltpu.VMEM((3, lines, size, cols), BF16),
        pltpu.VMEM((lines,) + blk, BF16),
        pltpu.VMEM((three,) + blk, BF16),
        pltpu.VMEM((len(stages), 16, dim), F32),
        pltpu.SemaphoreType.DMA((n_in + seqs,)),
        pltpu.SemaphoreType.DMA((n_sems,)),
        pltpu.SemaphoreType.DMA((n_sems,)),
        pltpu.VMEM((seqs * share, dim), tokens.dtype),
    ]
    firsts, seconds = [a for a, _ in zx], [a for a, _ in yz]
    for lead in ((three, 2), (three, 2), (), ()):
        scratch += [buf(a, lead) for a in firsts]
    for lead in ((lines,), (lines,), (three,), (three,)):
        scratch += [buf(a, lead) for a in seconds]
    scratch += [buf(a, (three,)) for a in z_only] + [buf(a, (three,)) for a in z_only]
    out = pl.pallas_call(
        kernel,
        in_specs=[ANY] * n_in + [vmem] * len(smalls) + [ANY],
        out_specs=[vmem] * n_out,
        out_shape=[shape((4, seqs, share, dim), BF16), shape(blk, F32), shape((16, dim), F32)]
        + [shape(piece(a), F32) for a in firsts + seconds + list(z_only)],
        scratch_shapes=scratch,
        compiler_params=pltpu.CompilerParams(vmem_limit_bytes=60 * 1024 * 1024, collective_id=1, has_side_effects=True),
        cost_estimate=cost(12 * seqs * LEN * dim * cols, seqs * LEN * dim * 8),
        name="finish",
    )(*inputs, *smalls, tokens)
    return out[0], out[1], out[2], out[3:]


def adam_update(weight, moment_one, moment_two, gradient, step_rate, decay_rate):
    fresh_one = BETA_ONE * moment_one + (1.0 - BETA_ONE) * gradient
    fresh_two = BETA_TWO * moment_two + (1.0 - BETA_TWO) * gradient * gradient
    one_hat = fresh_one / (1.0 - BETA_ONE**STEP)
    two_hat = fresh_two / (1.0 - BETA_TWO**STEP)
    updated = weight - step_rate * (one_hat / (jnp.sqrt(two_hat) + ADAM_EPS) + decay_rate * weight)
    return (fresh_one, fresh_two, updated)


def shards(
    tokens,
    seg_ids,
    labels,
    w_qkv,
    m_qkv,
    v_qkv,
    w_out,
    m_out,
    v_out,
    w_up,
    m_up,
    v_up,
    w_down,
    m_down,
    v_down,
    w_cls,
    m_cls,
    v_cls,
    norm_params,
    m_norm,
    v_norm,
    qk_gain,
    m_qk,
    v_qk,
    *,
    n_dp,
    n_mp,
):
    dp, mp = lax.axis_index("dp"), lax.axis_index("mp")
    group_rows, dim = tokens.shape
    plan = Plan(n_dp, n_mp, dim)
    seqs = group_rows // LEN
    share = LEN // n_mp
    rows = seqs * share
    cols = w_qkv.shape[2]
    classes = w_cls.shape[1]
    class_cols = -(-classes // 128) * 128
    out_cols = -(-cols // 128) * 128
    ids = jnp.stack([dp // plan.merge, mp]).astype(jnp.int32)

    new_image = seg_ids != jnp.concatenate([jnp.full((1,), -1, jnp.int32), seg_ids[:-1]])
    count = jnp.sum((new_image & (seg_ids != PAD_ID)).astype(F32))
    dim_part, head_part = norm_params.shape[1], qk_gain.shape[2]
    pad = lambda a, r, c: jnp.pad(a, ((0, r - a.shape[0]), (0, c - a.shape[1])))
    low_param = lambda a: lax.reduce_precision(a, 8, 7)
    small = jnp.concatenate(
        [
            pad(low_param(norm_params), 8, 128),
            pad(low_param(qk_gain).reshape(2, cols // HEAD * head_part), 8, 128),
            pad(count.reshape(1, 1), 8, 128),
        ]
    )
    qkv_block = plan.merged(w_qkv.astype(BF16), 1)
    up_block = plan.merged(w_up.astype(BF16), 0)
    down_block = plan.merged(w_down.T.astype(BF16), 0)
    out_block = plan.merged(pad(w_out.T.astype(BF16), dim_part, out_cols), 0)
    cls_block = plan.merged(pad(w_cls.astype(BF16), dim_part, class_cols), 0)
    small_block = plan.merged(small[None], 0)

    tied = lambda value, tie: lax.optimization_barrier((value, tie))[0]

    head_of = jnp.arange(cols) // HEAD
    ones = jnp.where(head_of[:, None] == head_of[None, :], 1.0 / HEAD, 0.0).astype(BF16)
    starts, widths, live = key_windows(seg_ids)
    seg_col = seg_ids.reshape(group_rows, 1)
    seg_row = seg_ids.reshape(-1, LEN)
    seg_row = jnp.stack([seg_row, jnp.roll(seg_row, -ALIGN, axis=1)], axis=1)
    normed_low, pq, pk, q, k, v, w, up, down, out_w, cls, params, gains, images = gather_project(
        plan, tokens, qkv_block, up_block, down_block, out_block, cls_block, small_block, ones
    )
    w = w.reshape(3, dim, cols)
    out_w = out_w.reshape(n_mp, dim, out_cols)
    up = up.reshape(dim, up.shape[-1])
    up_across, down_across = plan.swap(up, "mp", 2), plan.group_swap(down, 1)
    cls = cls.reshape(dim, class_cols)
    cls_across = plan.swap(tied(cls, up_across), "mp", 2)
    image_total = images[0, 0]
    *attended, logs = attend(plan, ids, starts, widths, q, k, v, seg_col, seg_row)

    (middle, second_low, active, slope), attended, up_mates, down_mates = feed_up(
        plan, tokens, attended, params, out_w, up, up_across, down, down_across
    )
    up = [up, up_across, *up_mates]
    down = [down, down_across, *down_mates]
    result, block_rows, pool = feed_down(plan, ids, middle, active, seg_row, params, down)

    block_rows = block_rows.reshape(seqs, share, dim)
    slot_label = labels.reshape(seqs, IMG_SEQ)
    slot_label = slot_label // classes * class_cols + slot_label % classes
    slot_label = jnp.pad(slot_label, ((0, 0), (0, SLOTS - IMG_SEQ)), constant_values=-1).reshape(seqs * SLOTS, 1)
    row_grads, stats, loss, cls_blocks = classify(plan, pool, slot_label, images, cls, cls_across, classes)

    block_rows = lax.optimization_barrier((block_rows, stats))[0]
    block_across = plan.swap(block_rows, "mp", 2)
    block_mate, block_mate_across = plan.swap(block_rows, "mp", 1), plan.swap(block_across, "mp", 1)
    block_out = assemble(plan, ids, [block_rows, block_across, block_mate, block_mate_across], BF16, "block_out")

    result_low, hidden_low, middle_low, middle_grad, *rest = feed_back(
        plan, ids, result, middle, slope, row_grads, stats, seg_col, params, out_w, up, down, cols
    )
    attended_grads, sums = rest[:n_mp], rest[n_mp]
    cls_blocks = cls_blocks.reshape(2, plan.groups // 2, plan.block, class_cols)
    kept, sent, cls_sum, arrived = weight_grads(
        plan, [(result_low, active), (second_low, hidden_low)], (middle_low, attended), cls_blocks, attended_grads[1:]
    )
    grad_parts = [attended_grads[0]] + list(arrived)
    got = [plan.swap(sent[0], "mp", 2)] + [plan.group_swap(part, 1) for part in sent[1:]]

    proj_grads, gain_sums = [], []
    for s in range(seqs):
        *grad, gain_sum = attend_back(
            plan, s, ids, starts, widths, live, q, k, v, pq, pk, gains, ones, grad_parts, logs, seg_col, seg_row
        )
        proj_grads.append(grad)
        gain_sums.append(gain_sum)
    *got, block_out, _ = lax.optimization_barrier((*got, block_out, proj_grads[-1][0]))

    down_pair, up_pair, out_pair = zip(kept, got)
    last_rows, grad_qkv, small_grads, owned = finish(
        plan, normed_low, proj_grads, w, middle_grad, tokens, params, sums, gain_sums, loss, [up_pair, out_pair], [down_pair], [cls_sum]
    )
    mean_loss = small_grads[10, 0] / image_total
    grad_qkv = plan.unmerged(grad_qkv, 1)
    grad_up, grad_out, grad_down, grad_cls = (plan.unmerged(a, 0) for a in owned)
    grad_out, grad_down, grad_cls = grad_out[:, :cols].T, grad_down.T, grad_cls[:, :classes]
    input_grad = assemble(plan, ids, [last_rows], F32, "input_grad")
    norm_part = lax.dynamic_slice(small_grads, (0, dp * dim_part), (7, dim_part))
    qk_part = lax.dynamic_slice_in_dim(small_grads[8:10, :cols].reshape(2, cols // HEAD, HEAD), dp * head_part, head_part, 2)
    reduced = (grad_qkv, grad_out, grad_up, grad_down, grad_cls, norm_part, qk_part)
    groups = (
        (w_qkv, m_qkv, v_qkv, MATRIX_RATE, MATRIX_DECAY),
        (w_out, m_out, v_out, MATRIX_RATE, MATRIX_DECAY),
        (w_up, m_up, v_up, MATRIX_RATE, MATRIX_DECAY),
        (w_down, m_down, v_down, MATRIX_RATE, MATRIX_DECAY),
        (w_cls, m_cls, v_cls, MATRIX_RATE, MATRIX_DECAY),
        (norm_params, m_norm, v_norm, GAIN_RATE, 0.0),
        (qk_gain, m_qk, v_qk, GAIN_RATE, 0.0),
    )
    outputs = [block_out, input_grad, mean_loss]
    for number, group in enumerate(groups):
        fresh_one, fresh_two, updated = adam_update(group[0], group[1], group[2], reduced[number], group[3], group[4])
        if number == 5:
            outputs = outputs + [fresh_one, fresh_two[:6], fresh_two[6], updated]
        else:
            outputs = outputs + [fresh_one, fresh_two, updated]
    return tuple(outputs)


def solution(mesh):
    rows_cols = (P("mp", "dp"),) * 3
    cols_rows = (P("dp", "mp"),) * 3
    qkv_spec = (P(None, "dp", "mp"),) * 3
    qk_spec = (P(None, "mp", "dp"),) * 3
    norm_spec = P(None, "dp")
    in_specs = (
        (P("dp", None), P("dp"), P("dp")) + qkv_spec + rows_cols + cols_rows + rows_cols + cols_rows + (norm_spec,) * 3 + qk_spec
    )
    out_specs = (
        (P("dp", None), P("dp", None), P())
        + qkv_spec
        + rows_cols
        + cols_rows
        + rows_cols
        + cols_rows
        + (norm_spec, norm_spec, P("dp"), norm_spec)
        + qk_spec
    )
    body = functools.partial(shards, n_dp=mesh.shape["dp"], n_mp=mesh.shape["mp"])
    return jax.shard_map(body, mesh=mesh, in_specs=in_specs, out_specs=out_specs, check_vma=False)
```

profile of v0, /device:TPU:0, one launch (start us, length us, event | category | flops | bytes accessed | tf_op | source)
XLA Modules:
  0.0 380.9 jit_solution(11500284793585131723)
XLA Ops:
  0.7 0.7 select_convert_fusion.ones_ref
  1.5 1.0 copy.81
  2.5 1.6 convert_bitcast_fusion.down_in
  4.1 1.6 convert_element_type.51.qkv_in
  5.7 1.6 convert_element_type.52.up_in
  7.4 0.6 pad.24.out_in
  8.0 0.6 pad.25.cls_in
  8.8 0.7 convert_reduce_fusion.2
  9.4 1.2 fusion.7.small_in
  10.7 68.7 %gather_project.1 = (bf16[3072,768]{1,0:T(8,128)(2,1)}, f32[3072,192]{1,0:T(8,128)}, f32[3072,192]{1,0:T(8,128)}, bf16[3072,192]{1,0:T(8,128)(2,1)}, bf16[3072,1...) custom-call(bf16[3072,768]{1,0:T(8,128)(2,1)} %refs_25_.1, ...), custom_call_target="tpu_custom_call" | custom-call | flops 2717908992 | bytes 18874368 | tf_op jit(solution)/shard_map/gather_project/pallas_call | solution.py:392
  79.3 1.8 collective-permute-start.1
  83.3 1.7 copy.83.col_ref.seg_ref
  85.0 0.6 pad_add_fusion.row_ref.seg_ref
  85.6 0.6 pad_add_fusion.2.ids_ref
  86.2 20.8 %attend.1 = (bf16[768,192]{1,0:T(8,128)(2,1)}, bf16[768,192]{1,0:T(8,128)(2,1)}, bf16[768,192]{1,0:T(8,128)(2,1)}, bf16[768,192]{1,0:T(8,128)(2,1)}, f32[3072,128]{1,0:T(8,128)}) custom-call(s32[2]{0:T(128)} %pad_add_fusion.2.ids_ref, s32[12]{0:T(128)} %select_select_fusion.1.start_ref, s32[12]{0:T(128)} %get-tuple-element.285.width_ref, ...), custom_call_target="tpu_custom_call" | custom-call | flops 36238786560 | bytes 4718592 | tf_op jit(solution)/shard_map/attend/pallas_call | solution.py:508
  107.3 0.8 reshape.157.label_ref
  108.1 0.6 reshape.156.live_ref
  108.7 1.2 slice.44
  110.1 1.8 collective-permute-start.2
  111.9 1.1 copy-done.31
  112.9 26.8 %feed_up.1 = (f32[768,768]{1,0:T(8,128)}, bf16[768,768]{1,0:T(8,128)(2,1)}, bf16[768,3072]{1,0:T(8,128)(2,1)}, f32[768,3072]{1,0:T(8,128)}, bf16[768,192]{1,0:T(...) custom-call(bf16[768,192]{1,0:T(8,128)(2,1)} %get-tuple-element.109., ...), custom_call_target="tpu_custom_call" | custom-call | flops 4529848320 | bytes 18874368 | tf_op jit(solution)/shard_map/feed_up/pallas_call | solution.py:730
  139.8 17.7 %feed_down.1 = (f32[768,768]{1,0:T(8,128)}, bf16[768,768]{1,0:T(8,128)(2,1)}, f32[192,896]{1,0:T(8,128)}) custom-call(s32[2]{0:T(128)} %pad_add_fusion.2.ids_ref, f32[768,768]{1,0:T(8,128)} %get-tuple-element.117.mid_ref, bf16[768,3072]{1,0:T(8,128)(2,1)} %get-tuple-element.118.act_ref.refs_1_, s32[3,2,1024]{2,1,0:T(2,128)} %pad_add_fusion.row_ref.seg_ref, ...), custom_call_target="tpu_custom_call" | custom-call | flops 3623878656 | bytes 9437184 | tf_op jit(solution)/shard_map/feed_down/pallas_call | solution.py:803
  157.5 0.8 copy-done.35
  158.3 20.8 %classify.1 = (bf16[192,768]{1,0:T(8,128)(2,1)}, f32[192,128]{1,0:T(8,128)}, f32[8,128]{1,0:T(8,128)}, bf16[8,96,256]{2,1,0:T(8,128)(2,1)}) custom-call(f32[192,896]{1,0:T(8,128)} %get-tuple-element.123.part_ref, s32[192,1]{1,0:T(8,128)} %reshape.157.label_ref, f32[8,128]{1,0:T(8,128)} %get-tuple-element.124.images_ref, bf16[768,256]{1,0:T(8,128)(2,1)} %bitcast.51, ...), custom_call_target="tpu_custom_call" | custom-call | flops 905969664 | bytes 1572864 | tf_op jit(solution)/shard_map/classify/pallas_call | solution.py:892
  179.6 23.7 %feed_back.1 = (bf16[768,768]{1,0:T(8,128)(2,1)}, bf16[768,3072]{1,0:T(8,128)(2,1)}, bf16[768,768]{1,0:T(8,128)(2,1)}, f32[768,768]{1,0:T(8,128)}, bf16[768,192]...) custom-call(s32[2]{0:T(128)} %pad_add_fusion.2.ids_ref, ...), custom_call_target="tpu_custom_call" | custom-call | flops 8153726976 | bytes 18874368 | tf_op jit(solution)/shard_map/feed_back/pallas_call | solution.py:992
  203.3 21.6 %grads.1 = (f32[4,2,96,768]{3,2,1,0:T(8,128)}, f32[2,4,96,768]{3,2,1,0:T(8,128)}, f32[2,4,96,256]{3,2,1,0:T(8,128)}, bf16[4,2,96,768]{3,2,1,0:T(8,128)(2,1)}, bf...) custom-call(bf16[768,768]{1,0:T(8,128)(2,1)} %get-tuple-element.131., ...), custom_call_target="tpu_custom_call" | custom-call | flops 8455716864 | bytes 18874368 | tf_op jit(solution)/shard_map/grads/pallas_call | solution.py:1084
  224.9 1.6 collective-permute-start.3
  226.5 13.7 %attend_back.5 = (bf16[1024,192]{1,0:T(8,128)(2,1)}, bf16[1024,192]{1,0:T(8,128)(2,1)}, bf16[1024,192]{1,0:T(8,128)(2,1)}, f32[2,8,192]{2,1,0:T(8,128)}) custom-call(s32[2]{0:T(128)} %pad_add_fusion.2.ids_ref, s32[12]{0:T(128)} %select_select_fusion.1.start_ref, s32[12]{0:T(128)} %get-tuple-element.285.width_ref, s32[12]{0:T(128)} %reshape.156.live_ref, ...), custom_call_target="tpu_custom_call" | custom-call | flops 12079595520 | bytes 4718592 | tf_op jit(solution)/shard_map/attend_back/pallas_call | solution.py:601
  240.4 14.0 %attend_back.4 = (bf16[1024,192]{1,0:T(8,128)(2,1)}, bf16[1024,192]{1,0:T(8,128)(2,1)}, bf16[1024,192]{1,0:T(8,128)(2,1)}, f32[2,8,192]{2,1,0:T(8,128)}) custom-call(s32[2]{0:T(128)} %pad_add_fusion.2.ids_ref, s32[12]{0:T(128)} %select_select_fusion.1.start_ref, s32[12]{0:T(128)} %get-tuple-element.285.width_ref, s32[12]{0:T(128)} %reshape.156.live_ref, ...), custom_call_target="tpu_custom_call" | custom-call | flops 12079595520 | bytes 4718592 | tf_op jit(solution)/shard_map/attend_back/pallas_call | solution.py:601
  254.4 3.0 collective-permute-start.5
  257.4 14.6 %attend_back.3 = (bf16[1024,192]{1,0:T(8,128)(2,1)}, bf16[1024,192]{1,0:T(8,128)(2,1)}, bf16[1024,192]{1,0:T(8,128)(2,1)}, f32[2,8,192]{2,1,0:T(8,128)}) custom-call(s32[2]{0:T(128)} %pad_add_fusion.2.ids_ref, s32[12]{0:T(128)} %select_select_fusion.1.start_ref, s32[12]{0:T(128)} %get-tuple-element.285.width_ref, s32[12]{0:T(128)} %reshape.156.live_ref, ...), custom_call_target="tpu_custom_call" | custom-call | flops 12079595520 | bytes 4718592 | tf_op jit(solution)/shard_map/attend_back/pallas_call | solution.py:601
  272.1 1.0 copy-done.2
  273.1 1.0 copy-done.3
  274.2 5.6 %block_out.1 = bf16[3,4,256,768]{3,2,1,0:T(8,128)(2,1)} custom-call(s32[2]{0:T(128)} %pad_add_fusion.2.ids_ref, bf16[3,256,768]{2,1,0:T(8,128)(2,1)} %bitcast.41, bf16[3,256,768]{2,1,0:T(8,128)(2,1)} %copy-done.1, bf16[3,256,768]{2,1,0:T(8,128)(2,1)} %copy-done.2, bf16[3,256,768]{2,1,0:T(8,128)(2,1)} %copy-done.3), custom_call_target="tpu_custom_call" | custom-call | bytes 18874368 | tf_op jit(solution)/shard_map/block_out/pallas_call | solution.py:1130
  279.8 77.9 %finish.1 = (bf16[4,3,256,768]{3,2,1,0:T(8,128)(2,1)}, f32[3,96,192]{2,1,0:T(8,128)}, f32[16,768]{1,0:T(8,128)}, f32[96,768]{1,0:T(8,128)}, f32[96,256]{1,0:T(8,...) custom-call(bf16[3,768,192]{2,1,0:T(8,128)(2,1)} %bitcast.40, bf16[1024,192]{1,0:T(8,128)(2,1)} %get-tuple-element.158.refs_1_, ...), custom_call_target="tpu_custom_call" | custom-call | flops 5435817984 | bytes 18874368 | tf_op jit(solution)/shard_map/finish/pallas_call | solution.py:1376
  357.7 1.2 slice.43
  358.9 0.7 slice.49
  359.6 7.3 %input_grad.1 = f32[3,4,256,768]{3,2,1,0:T(8,128)} custom-call(s32[2]{0:T(128)} %pad_add_fusion.2.ids_ref, bf16[4,3,256,768]{3,2,1,0:T(8,128)(2,1)} %get-tuple-element.180.refs_0_), custom_call_target="tpu_custom_call" | custom-call | bytes 18874368 | tf_op jit(solution)/shard_map/input_grad/pallas_call | solution.py:1130
  367.0 0.7 copy.97
  367.8 0.7 copy.98
  368.5 0.7 copy.99
  369.4 0.6 copy.100
  370.6 0.6 copy.102
  371.2 1.4 multiply_subtract_fusion.5
  374.5 2.1 multiply_subtract_fusion
  376.6 1.0 multiply_subtract_fusion.1
  377.7 1.0 multiply_subtract_fusion.2
  378.8 0.7 multiply_subtract_fusion.3
  (116 shorter events, 4.9 us)
Async XLA Ops:
  0.7 6.7 %copy-start.7 = (f32[96,250]{1,0:T(8,128)S(1)}, f32[96,250]{1,0:T(8,128)}, u32[]{:S(2)}) copy-start(f32[96,250]{1,0:T(8,128)} %param.39) | copy-start | bytes 288004
  0.7 8.0 %copy-start.24 = (f32[2,3,8]{2,0,1:T(2,128)S(1)}, f32[2,3,8]{2,0,1:T(2,128)}, u32[]{:S(2)}) copy-start(f32[2,3,8]{2,0,1:T(2,128)} %param.45) | copy-start | bytes 580
  0.7 8.1 %copy-start.23 = (f32[7,96]{1,0:T(8,128)S(1)}, f32[7,96]{1,0:T(8,128)}, u32[]{:S(2)}) copy-start(f32[7,96]{1,0:T(8,128)} %param.42) | copy-start | bytes 8068
  0.7 8.1 %copy-start.8 = (s32[3072]{0:T(1024)S(1)}, s32[3072]{0:T(1024)}, u32[]{:S(2)}) copy-start(s32[3072]{0:T(1024)} %param.25) | copy-start | bytes 36868
  79.3 32.5 %collective-permute-start.1 = (bf16[2,4,96,768]{3,2,1,0:T(8,128)(2,1)}, bf16[2,4,96,768]{3,2,1,0:T(8,128)(2,1)S(1)}, u32[]{:S(2)}, u32[]{:S(2)}) collective-permute-start(bf16[2,4,96,768]{3,2,1,0:T(8,128)(2,1)} %get-tuple-element.116.refs_8_.refs_0_.refs_4_), channel_id=1, source_target_pairs={{0,4},{4,0},{8,12},{12,8},{16,20},{20,16},{24,28},{28,24},{1,5},{5... | collective-permute-start | bytes 3538952 | tf_op jit(solution)/shard_map/ppermute | solution.py:88
  81.2 28.9 %collective-permute-start = (bf16[768,768]{1,0:T(8,128)(2,1)}, bf16[768,768]{1,0:T(8,128)(2,1)S(1)}, u32[]{:S(2)}, u32[]{:S(2)}) collective-permute-start(bf16[768,768]{1,0:T(8,128)(2,1)} %bitcast.48), channel_id=1, source_target_pairs={{0,2},{1,3},{2,0},{3,1},{4,6},{5,7},{6,4},{7,5},{8,10},{9,11},{10,... | collective-permute-start | bytes 3538952 | tf_op jit(solution)/shard_map/ppermute | solution.py:88
  86.2 20.8 %copy-start.30 = (s32[180]{0:T(256)S(1)}, s32[180]{0:T(256)}, u32[]{:S(2)}) copy-start(s32[180]{0:T(256)} %param.26) | copy-start | bytes 2164
  86.2 23.7 %copy-start.17 = (f32[192,96]{1,0:T(8,128)S(1)}, f32[192,96]{1,0:T(8,128)}, u32[]{:S(2)}) copy-start(f32[192,96]{1,0:T(8,128)} %param.31) | copy-start | bytes 221188
  86.2 23.8 %copy-start.18 = (f32[192,96]{1,0:T(8,128)S(1)}, f32[192,96]{1,0:T(8,128)}, u32[]{:S(2)}) copy-start(f32[192,96]{1,0:T(8,128)} %param.32) | copy-start | bytes 221188
  86.2 23.9 %copy-start.33 = (bf16[4,2,96,256]{3,2,1,0:T(8,128)(2,1)S(1)}, bf16[4,2,96,256]{3,2,1,0:T(8,128)(2,1)}, u32[]{:S(2)}) copy-start(bf16[4,2,96,256]{3,2,1,0:T(8,128)(2,1)} %get-tuple-element.125) | copy-start | bytes 1179652
  110.1 1.8 copy-start.32
  110.1 47.4 %collective-permute-start.2 = (bf16[768,256]{1,0:T(8,128)(2,1)S(1)}, bf16[768,256]{1,0:T(8,128)(2,1)S(1)}, u32[]{:S(2)}, u32[]{:S(2)}) collective-permute-start(bf16[768,256]{1,0:T(8,128)(2,1)S(1)} %bitcast.52), channel_id=1, source_target_pairs={{0,2},{1,3},{2,0},{3,1},{4,6},{5,7},{6,4},{7,5},{8,10},{9,11},{10,... | collective-permute-start | bytes 1179656 | tf_op jit(solution)/shard_map/ppermute | solution.py:88
  111.9 1.1 copy-start.31
  157.5 0.8 copy-start.35
  158.3 20.8 %copy-start = (bf16[768,768]{1,0:T(8,128)(2,1)S(1)}, bf16[768,768]{1,0:T(8,128)(2,1)}, u32[]{:S(2)}) copy-start(bf16[768,768]{1,0:T(8,128)(2,1)} %get-tuple-element.145) | copy-start | bytes 3538948
  179.1 61.2 %collective-permute-start.6 = (bf16[3,256,768]{2,1,0:T(8,128)(2,1)S(1)}, bf16[3,256,768]{2,1,0:T(8,128)(2,1)S(1)}, u32[]{:S(2)}, u32[]{:S(2)}) collective-permute-start(bf16[3,256,768]{2,1,0:T(8,128)(2,1)S(1)} %bitcast.42), channel_id=1, source_target_pairs={{0,2},{1,3},{2,0},{3,1},{4,6},{5,7},{6,4},{7,5},{8,10},{9,11},{10,... | collective-permute-start | bytes 3538952 | tf_op jit(solution)/shard_map/ppermute | solution.py:88
  179.2 92.9 %collective-permute-start.7 = (bf16[3,256,768]{2,1,0:T(8,128)(2,1)S(1)}, bf16[3,256,768]{2,1,0:T(8,128)(2,1)S(1)}, u32[]{:S(2)}, u32[]{:S(2)}) collective-permute-start(bf16[3,256,768]{2,1,0:T(8,128)(2,1)S(1)} %bitcast.43), channel_id=1, source_target_pairs={{0,1},{1,0},{2,3},{3,2},{4,5},{5,4},{6,7},{7,6},{8,9},{9,8},{10,11... | collective-permute-start | bytes 3538952 | tf_op jit(solution)/shard_map/ppermute | solution.py:88
  224.9 54.9 %collective-permute-start.3 = (bf16[4,2,96,768]{3,2,1,0:T(8,128)(2,1)}, bf16[4,2,96,768]{3,2,1,0:T(8,128)(2,1)}, u32[]{:S(2)}, u32[]{:S(2)}) collective-permute-start(bf16[4,2,96,768]{3,2,1,0:T(8,128)(2,1)} %get-tuple-element.142), channel_id=1, source_target_pairs={{0,2},{1,3},{2,0},{3,1},{4,6},{5,7},{6,4},{7,5},{8,10},{9,11},{10,... | collective-permute-start | bytes 3538952 | tf_op jit(solution)/shard_map/ppermute | solution.py:88
  226.4 53.4 %collective-permute-start.4 = (bf16[2,4,96,768]{3,2,1,0:T(8,128)(2,1)}, bf16[2,4,96,768]{3,2,1,0:T(8,128)(2,1)}, u32[]{:S(2)}, u32[]{:S(2)}) collective-permute-start(bf16[2,4,96,768]{3,2,1,0:T(8,128)(2,1)} %get-tuple-element.143), channel_id=1, source_target_pairs={{0,4},{4,0},{8,12},{12,8},{16,20},{20,16},{24,28},{28,24},{1,5},{5... | collective-permute-start | bytes 3538952 | tf_op jit(solution)/shard_map/ppermute | solution.py:88
  240.2 14.2 %copy-start.34 = (bf16[2,4,96,256]{3,2,1,0:T(8,128)(2,1)S(1)}, bf16[2,4,96,256]{3,2,1,0:T(8,128)(2,1)}, u32[]{:S(2)}) copy-start(bf16[2,4,96,256]{3,2,1,0:T(8,128)(2,1)} %get-tuple-element.144) | copy-start | bytes 1179652
  240.3 14.1 %copy-start.1 = (bf16[3,256,768]{2,1,0:T(8,128)(2,1)}, bf16[3,256,768]{2,1,0:T(8,128)(2,1)S(1)}, u32[]{:S(2)}) copy-start(bf16[3,256,768]{2,1,0:T(8,128)(2,1)S(1)} %collective-permute-done.6.refs_1_) | copy-start | bytes 3538948
  240.3 31.8 %collective-permute-start.8 = (bf16[3,256,768]{2,1,0:T(8,128)(2,1)S(1)}, bf16[3,256,768]{2,1,0:T(8,128)(2,1)S(1)}, u32[]{:S(2)}, u32[]{:S(2)}) collective-permute-start(bf16[3,256,768]{2,1,0:T(8,128)(2,1)S(1)} %collective-permute-done.6.refs_1_), channel_id=1, source_target_pairs={{0,1},{1,0},{2,3},{3,2},{4,5},{5,4},{6,7},{7,6},{8,9},{9,8},{10,11... | collective-permute-start | bytes 3538952 | tf_op jit(solution)/shard_map/ppermute | solution.py:88
  254.4 25.4 %collective-permute-start.5 = (bf16[2,4,96,256]{3,2,1,0:T(8,128)(2,1)S(1)}, bf16[2,4,96,256]{3,2,1,0:T(8,128)(2,1)}, u32[]{:S(2)}, u32[]{:S(2)}) collective-permute-start(bf16[2,4,96,256]{3,2,1,0:T(8,128)(2,1)S(1)} %copy-done.34), channel_id=1, source_target_pairs={{0,4},{4,0},{8,12},{12,8},{16,20},{20,16},{24,28},{28,24},{1,5},{5... | collective-permute-start | bytes 1179656 | tf_op jit(solution)/shard_map/ppermute | solution.py:88
  272.1 1.1 copy-start.2
  273.1 1.0 copy-start.3
  359.6 7.3 %copy-start.22 = (f32[96,256]{1,0:T(8,128)S(1)}, f32[96,256]{1,0:T(8,128)}, u32[]{:S(2)}) copy-start(f32[96,256]{1,0:T(8,128)} %get-tuple-element.183) | copy-start | bytes 294916
  359.6 9.7 %copy-start.28 = (f32[2,3,8]{2,0,1:T(2,128)S(1)}, f32[2,3,8]{2,0,1:T(2,128)}, u32[]{:S(2)}) copy-start(f32[2,3,8]{2,0,1:T(2,128)} %param.47) | copy-start | bytes 580
  359.6 9.7 %copy-start.29 = (f32[2,3,8]{2,0,1:T(2,128)S(1)}, f32[2,3,8]{2,0,1:T(2,128)}, u32[]{:S(2)}) copy-start(f32[2,3,8]{2,0,1:T(2,128)} %param.46) | copy-start | bytes 580
  359.6 11.6 %copy-start.25 = (f32[7,96]{1,0:T(8,128)S(1)}, f32[7,96]{1,0:T(8,128)}, u32[]{:S(2)}) copy-start(f32[7,96]{1,0:T(8,128)} %param.44) | copy-start | bytes 8068
  359.6 11.6 %copy-start.26 = (f32[7,96]{1,0:T(8,128)S(1)}, f32[7,96]{1,0:T(8,128)}, u32[]{:S(2)}) copy-start(f32[7,96]{1,0:T(8,128)} %param.43) | copy-start | bytes 8068
  366.9 7.5 %copy-start.4 = (f32[768,96]{0,1:T(8,128)S(1)}, f32[768,96]{0,1:T(8,128)}, u32[]{:S(2)}) copy-start(f32[768,96]{0,1:T(8,128)} %param.36) | copy-start | bytes 884740
  366.9 7.6 %copy-start.9 = (f32[768,96]{0,1:T(8,128)S(1)}, f32[768,96]{0,1:T(8,128)}, u32[]{:S(2)}) copy-start(f32[768,96]{0,1:T(8,128)} %param.38) | copy-start | bytes 884740
  366.9 7.6 %copy-start.10 = (f32[768,96]{0,1:T(8,128)S(1)}, f32[768,96]{0,1:T(8,128)}, u32[]{:S(2)}) copy-start(f32[768,96]{0,1:T(8,128)} %param.37) | copy-start | bytes 884740
  366.9 9.7 %copy-start.5 = (f32[96,768]{1,0:T(8,128)S(1)}, f32[96,768]{1,0:T(8,128)}, u32[]{:S(2)}) copy-start(f32[96,768]{1,0:T(8,128)} %param.33) | copy-start | bytes 884740
  366.9 9.7 %copy-start.11 = (f32[96,768]{1,0:T(8,128)S(1)}, f32[96,768]{1,0:T(8,128)}, u32[]{:S(2)}) copy-start(f32[96,768]{1,0:T(8,128)} %param.35) | copy-start | bytes 884740
  366.9 9.7 %copy-start.12 = (f32[96,768]{1,0:T(8,128)S(1)}, f32[96,768]{1,0:T(8,128)}, u32[]{:S(2)}) copy-start(f32[96,768]{1,0:T(8,128)} %param.34) | copy-start | bytes 884740
  366.9 9.7 %copy-start.16 = (f32[96,768]{1,0:T(8,128)S(1)}, f32[96,768]{1,0:T(8,128)}, u32[]{:S(2)}) copy-start(f32[96,768]{1,0:T(8,128)} %get-tuple-element.184) | copy-start | bytes 884740
  372.6 5.1 %copy-start.27 = (f32[7,96]{1,0:T(8,128)}, f32[7,96]{1,0:T(8,128)S(1)}, u32[]{:S(2)}) copy-start(f32[7,96]{1,0:T(8,128)S(1)} %get-tuple-element.268) | copy-start | bytes 8068
  374.4 3.2 copy-start.6
  374.4 3.2 copy-start.13
  374.5 3.2 copy-start.14
  374.5 3.2 copy-start.15
  376.6 2.2 copy-start.19
  376.6 2.1 copy-start.20
  376.6 2.1 copy-start.21
where the time goes:
time: 387 us; the launch traced here: 381 us
  Pallas kernels  333 us (86%)
  local copies, waits for them, and re-layouts  17.9 us (5%)
  other arithmetic  16.7 us (4%)
  starting transfers between devices  9.13 us (2%)
  between operations  3.9 us (1%)
    pallas_call x1, Pallas kernels, finish(): pl.pallas_call(kernel, in_specs=[ANY] * n_in + [vmem] * len(smalls) + [AN...  77.9 us
    pallas_call x1, Pallas kernels, gather_project(): pl.pallas_call(kernel, in_specs=[vmem] + [ANY] * 6 + [vmem], out_specs=[A...  68.7 us
    pallas_call x3, Pallas kernels, attend_back(): pl.pallas_call(kernel, grid_spec=pltpu.PrefetchScalarGridSpec(num_scalar_...  42.4 us
    pallas_call x1, Pallas kernels, feed_up(): pl.pallas_call(kernel, in_specs=[ANY] * n_load + [pl.BlockSpec(memory_spa...  26.8 us
    pallas_call x1, Pallas kernels, feed_back(): pl.pallas_call(kernel, grid_spec=pltpu.PrefetchScalarGridSpec(num_scalar_...  23.7 us
    pallas_call x1, Pallas kernels, weight_grads(): pl.pallas_call(kernel, in_specs=[ANY] * (n_load + n_mp - 1), out_specs=[A...  21.6 us
    pallas_call x1, Pallas kernels, attend(): pl.pallas_call(kernel, grid_spec=pltpu.PrefetchScalarGridSpec(num_scalar_...  20.8 us
    pallas_call x1, Pallas kernels, classify(): pl.pallas_call(kernel, in_specs=[vmem] * 3 + [ANY] * 2, out_specs=[vmem]...  20.8 us
  transfers between devices with their start and end apart: 9, of which 0 were waited for; matrix products, arithmetic and copies ran while one was open for 2% of the time, Pallas kernels for 42%

commit v1 on v0

--- a/solution.py
+++ b/solution.py
@@ -253,7 +253,8 @@
     n_mp, merge, size = plan.n_mp, plan.merge, plan.block
     lines = plan.groups // 2
     width = up_block.shape[1]
-    out_cols, class_cols = out_block.shape[1], cls_block.shape[1]
+    out_cols, classes = out_block.shape[1], cls_block.shape[1]
+    class_cols = -(-classes // 128) * 128
     block = 512
     blocks = rows // block
     dim_part = dim // plan.n_dp
@@ -263,9 +264,13 @@
     sizes = {name: Chain(None, order, lines).copies for name, order in orders}
     n_sems = sum(sizes.values())
 
-    def kernel(x_ref, qkv_in, up_in, down_in, out_in, cls_in, small_in, ones_ref, *refs):
+    def kernel(x_ref, qkv_wide, up_wide, down_in, out_in, cls_wide, small_in, ones_ref, *refs):
         low_ref, pq_ref, pk_ref, q_ref, k_ref, v_ref, w_ref, up_ref, down_ref, o_ref, c_ref, norm_ref, gain_ref, image_ref = refs[:14]
-        w_buf, small_buf, low_buf, pq_buf, pk_buf, q_buf, k_buf, v_buf, send_sems, recv_sems, own_sems, out_sems = refs[14:]
+        w_buf, small_buf, low_buf, pq_buf, pk_buf, q_buf, k_buf, v_buf, send_sems, recv_sems, own_sems, out_sems, *lows = refs[14:]
+        qkv_in, up_in, cls_in = lows
+        qkv_in[...] = qkv_wide[...].astype(BF16)
+        up_in[...] = up_wide[...].astype(BF16)
+        cls_in[...] = jnp.concatenate([cls_wide[...].astype(BF16), jnp.zeros((size, class_cols - classes), BF16)], axis=1)
         g = Gatherer(plan, send_sems, recv_sems)
         z, y, x, core = g.here()
         everything = slice(None)
@@ -391,7 +396,7 @@
     n_rows = lambda c, t: shape((rows, c), t)
     return pl.pallas_call(
         kernel,
-        in_specs=[vmem] + [ANY] * 6 + [vmem],
+        in_specs=[vmem, vmem, vmem, ANY, ANY, vmem, ANY, vmem],
         out_specs=[ANY] * 11 + [vmem] * 3,
         out_shape=[n_rows(dim, BF16), n_rows(cols, F32), n_rows(cols, F32), n_rows(cols, BF16), n_rows(cols, BF16), n_rows(cols, BF16)]
         + [
@@ -417,6 +422,9 @@
             pltpu.SemaphoreType.DMA((n_sems,)),
             pltpu.SemaphoreType.DMA((len(orders),)),
             pltpu.SemaphoreType.DMA((7,)),
+            pltpu.VMEM(qkv_block.shape, BF16),
+            pltpu.VMEM(up_block.shape, BF16),
+            pltpu.VMEM((size, class_cols), BF16),
         ],
         compiler_params=pltpu.CompilerParams(vmem_limit_bytes=VMEM_LIMIT, collective_id=0, has_side_effects=True),
         cost_estimate=cost(6 * rows * dim * cols, rows * dim * 8),
@@ -782,10 +790,8 @@
         block_ref[...] = result.astype(BF16)
         normed, _ = norm_parts(result)
         final = normed * norm_ref[4:5, :] + norm_ref[5:6, :]
-        probe = jnp.broadcast_to(norm_ref[6:7, :], (8, dim))
-        score = lax.dot_general(
-            probe, final, (((1,), (1,)), ((), ())), precision=lax.Precision.HIGHEST, preferred_element_type=F32
-        )[0:1]
+        score = jnp.sum(final * norm_ref[6:7, :], axis=1, keepdims=True)
+        score = jnp.broadcast_to(score, (block, 128)).T[0:1]
         slot = lax.broadcasted_iota(jnp.int32, (SLOTS, block), 0)
         member = (seg_ref[0, 0:1, :] - seq * IMG_SEQ == slot) & (slot < IMG_SEQ)
         top = jnp.max(jnp.where(member, score, MASK_FILL), axis=1, keepdims=True)
@@ -1009,7 +1015,7 @@
     )(ids, result, middle, slope, row_grads, stats, seg_col, params, out_w, *up, *down)
 
 
-def weight_grads(plan, pairs, out_pair, cls_blocks, sends):
+def weight_grads(plan, pairs, out_pair, cls_blocks, sends, blocks):
     dim = pairs[0][0].shape[1]
     rows = pairs[0][0].shape[0]
     n_mp, size, merge = plan.n_mp, plan.block, plan.merge
@@ -1017,7 +1023,7 @@
     width = pairs[0][1].shape[1] // n_mp
     cols = out_pair[1][0].shape[1]
     out_cols = -(-cols // 128) * 128
-    inputs = [a for pair in pairs for a in pair] + [out_pair[0]] + list(out_pair[1]) + [cls_blocks]
+    inputs = [a for pair in pairs for a in pair] + [out_pair[0]] + list(out_pair[1]) + [cls_blocks] + list(blocks)
     n_load = len(inputs)
     widths = [width] * len(pairs) + [out_cols]
     n = len(widths)
@@ -1025,16 +1031,18 @@
     def kernel(*refs):
         sources, ag_in, refs = refs[:n_load], refs[n_load : n_load + n_mp - 1], refs[n_load + n_mp - 1 :]
         keep_out, send_out, cls_out, ag_out, refs = refs[:n], refs[n : 2 * n], refs[2 * n], refs[2 * n + 1 : 2 * n + n_mp], refs[2 * n + n_mp :]
+        block_ref, refs = refs[0], refs[1:]
         targets, refs = refs[:n_load], refs[n_load:]
         send_buf, got_buf, own_buf, keep_buf, low_buf = (refs[i * n : (i + 1) * n] for i in range(5))
-        cls_got, load_sems, store_sems, send_sems, recv_sems = refs[5 * n :]
+        cls_got, load_sems, store_sems, send_sems, recv_sems, block_sems = refs[5 * n :]
         loads = Loads(sources, targets, load_sems)
         net = Sender(send_sems, recv_sems)
         y = net.dp // merge % 2
         side, core = net.mp // 2, net.mp % 2
         net.meet([("mp", 1), ("mp", 2), ("mp", 3), ("dp", merge)])
         ag = [net.copy(a, b, "mp", r) for r, (a, b) in enumerate(zip(ag_in, ag_out), start=1)]
-        cls_ref = loads[n_load - 1]
+        places = [block_ref.at[:, flip(net.mp, r)] for r in (0, 2)]
+        cls_ref = loads[n_load - 3]
         cls_copy = net.copy(cls_ref.at[1], cls_got, "dp", merge)
         stores = []
 
@@ -1049,8 +1057,13 @@
             return jnp.concatenate([value, jnp.zeros((dim, out_cols - cols), F32)], axis=1) if out_cols != cols else value
 
         split = lambda value: value.reshape(lines, 2, size, value.shape[1])
-        cores = []
+        cores, block_copies, block_own = [], [], []
         for i in range(n):
+            if i == 1:
+                rows_in = [loads[n_load - 2], loads[n_load - 1]]
+                block_copies += [net.copy(a, b, "mp", 1) for a, b in zip(rows_in, places)]
+                block_own += [pltpu.make_async_copy(a, b, block_sems.at[j]) for j, (a, b) in enumerate(zip(rows_in, places))]
+                start_all(block_own)
             for other_side in (0, 1):
                 send_buf[i][flip(side, other_side)] = split(grad(i, other_side, 1).astype(BF16))
             cores.append(net.copy(send_buf[i], got_buf[i], "mp", 1))
@@ -1070,8 +1083,9 @@
                 stores[-1].start()
         cls_copy.wait_recv()
         cls_out[...] = cls_ref[0].astype(F32) + cls_got[...].astype(F32)
-        for c in ag:
+        for c in ag + block_copies:
             c.wait_recv()
+        wait_all(block_own)
         net.finish()
         for c in stores:
             c.wait()
@@ -1080,15 +1094,17 @@
     vmem = pl.BlockSpec(memory_space=pltpu.VMEM)
     full = [(2, lines, 2, size, w) for w in widths]
     half = [(lines, 2, size, widths[0])] + [(2, lines, size, w) for w in widths[1:]]
-    n_sems = n + n_mp
+    n_sems = n + n_mp + 2
+    seqs, share = blocks[0].shape[:2]
     out = pl.pallas_call(
         kernel,
         in_specs=[ANY] * (n_load + n_mp - 1),
-        out_specs=[ANY] * (2 * n) + [vmem] + [ANY] * (n_mp - 1),
+        out_specs=[ANY] * (2 * n) + [vmem] + [ANY] * n_mp,
         out_shape=[shape(h, F32) for h in half]
         + [shape(h, BF16) for h in half]
         + [shape(cls_blocks.shape[1:], F32)]
-        + [shape(a.shape, a.dtype) for a in sends],
+        + [shape(a.shape, a.dtype) for a in sends]
+        + [shape((seqs, n_mp, share, dim), BF16)],
         scratch_shapes=[pltpu.VMEM(a.shape, a.dtype) for a in inputs]
         + [pltpu.VMEM(f, BF16) for f in full]
         + [pltpu.VMEM(f, BF16) for f in full]
@@ -1101,45 +1117,13 @@
             pltpu.SemaphoreType.DMA((2 * n,)),
             pltpu.SemaphoreType.DMA((n_sems,)),
             pltpu.SemaphoreType.DMA((n_sems,)),
+            pltpu.SemaphoreType.DMA((2,)),
         ],
         compiler_params=pltpu.CompilerParams(vmem_limit_bytes=60 * 1024 * 1024, collective_id=2, has_side_effects=True),
         cost_estimate=cost(2 * rows * dim * n_mp * sum(widths), rows * width * n_mp * 8),
         name="grads",
     )(*inputs, *sends)
-    return out[:n], out[n : 2 * n], out[2 * n], out[2 * n + 1 :]
-
-
-def assemble(plan, ids, parts, dtype, name):
-    n_mp = plan.n_mp
-    seqs, share, dim = parts[0].shape[-3:]
-    joint = len(parts) == 1
-
-    def kernel(ids_ref, *refs):
-        part_refs, out_ref = refs[:-1], refs[-1]
-        if joint:
-            out_ref[...] = part_refs[0][...].astype(dtype)
-            return
-        for i, ref in enumerate(part_refs):
-
-            @pl.when(pl.program_id(0) == i)
-            def _():
-                out_ref[...] = ref[...].astype(dtype)
-
-    relative = lambda i: i % 2 * 2 + i // 2
-    each = pl.BlockSpec((None, seqs, share, dim), lambda i, *_: (i, 0, 0, 0))
-    return pl.pallas_call(
-        kernel,
-        grid_spec=pltpu.PrefetchScalarGridSpec(
-            num_scalar_prefetch=1,
-            grid=(n_mp,),
-            in_specs=[each] if joint else [whole((seqs, share, dim))] * n_mp,
-            out_specs=pl.BlockSpec((seqs, None, share, dim), lambda i, ids_ref: (0, ids_ref[1] ^ relative(i), 0, 0)),
-        ),
-        out_shape=jax.ShapeDtypeStruct((seqs, n_mp, share, dim), dtype),
-        compiler_params=PARAMS,
-        cost_estimate=cost(0, seqs * n_mp * share * dim * 8),
-        name=name,
-    )(ids, *parts).reshape(seqs * n_mp * share, dim)
+    return out[:n], out[n : 2 * n], out[2 * n], out[2 * n + 1 : 2 * n + n_mp], out[2 * n + n_mp].reshape(-1, dim)
 
 
 def finish(plan, low, proj_grads, w, middle_grad, tokens, params, row_sums, gain_sums, loss, zx, yz, z_only):
@@ -1236,8 +1220,8 @@
             core_copies.append(copy(t_send.at[s], t_got.at[s], "mp", 1))
             lax.fori_loop(2, 4, functools.partial(terms, t_keep), 0)
             if s == 0:
+                over_x(0)
                 over_z(0)
-                over_x(0)
             elif s > 1:
                 over_x(s - 1)
             if s == 1:
@@ -1396,6 +1380,44 @@
     return (fresh_one, fresh_two, updated)
 
 
+def update(plan, ids, parts, groups):
+    n_mp, seqs, share, dim = parts.shape
+    n = len(groups)
+    arrays = [a for group in groups for a in group]
+
+    def kernel(ids_ref, part_ref, *refs):
+        sources, out_ref, results = refs[: 4 * n], refs[4 * n], refs[4 * n + 1 :]
+        out_ref[...] = part_ref[...].astype(F32)
+
+        @pl.when(pl.program_id(0) == 0)
+        def _():
+            for i in range(n):
+                w_ref, m_ref, v_ref, g_ref = sources[4 * i : 4 * i + 4]
+                columns = w_ref.shape[-1]
+                grad = g_ref[...][..., :columns]
+                fresh = adam_update(w_ref[...], m_ref[...], v_ref[...], grad, MATRIX_RATE, MATRIX_DECAY)
+                for ref, value in zip(results[3 * i : 3 * i + 3], fresh):
+                    ref[...] = value
+
+    relative = lambda i: i % 2 * 2 + i // 2
+    shapes = [jax.ShapeDtypeStruct(group[0].shape, F32) for group in groups for _ in range(3)]
+    out = pl.pallas_call(
+        kernel,
+        grid_spec=pltpu.PrefetchScalarGridSpec(
+            num_scalar_prefetch=1,
+            grid=(n_mp,),
+            in_specs=[pl.BlockSpec((None, seqs, share, dim), lambda i, *_: (i, 0, 0, 0))] + [whole(a.shape) for a in arrays],
+            out_specs=[pl.BlockSpec((seqs, None, share, dim), lambda i, ids_ref: (0, ids_ref[1] ^ relative(i), 0, 0))]
+            + [whole(a.shape) for a in shapes],
+        ),
+        out_shape=[jax.ShapeDtypeStruct((seqs, n_mp, share, dim), F32)] + shapes,
+        compiler_params=PARAMS,
+        cost_estimate=cost(0, seqs * n_mp * share * dim * 8),
+        name="update",
+    )(ids, parts, *arrays)
+    return out[0].reshape(seqs * n_mp * share, dim), [out[1 + 3 * i : 4 + 3 * i] for i in range(n)]
+
+
 def shards(
     tokens,
     seg_ids,
@@ -1449,11 +1471,12 @@
             pad(count.reshape(1, 1), 8, 128),
         ]
     )
-    qkv_block = plan.merged(w_qkv.astype(BF16), 1)
-    up_block = plan.merged(w_up.astype(BF16), 0)
+    low = lambda a: a if plan.merge == 1 else a.astype(BF16)
+    qkv_block = plan.merged(low(w_qkv), 1)
+    up_block = plan.merged(low(w_up), 0)
     down_block = plan.merged(w_down.T.astype(BF16), 0)
     out_block = plan.merged(pad(w_out.T.astype(BF16), dim_part, out_cols), 0)
-    cls_block = plan.merged(pad(w_cls.astype(BF16), dim_part, class_cols), 0)
+    cls_block = plan.merged(low(w_cls), 0)
     small_block = plan.merged(small[None], 0)
 
     tied = lambda value, tie: lax.optimization_barrier((value, tie))[0]
@@ -1472,13 +1495,13 @@
     up = up.reshape(dim, up.shape[-1])
     up_across, down_across = plan.swap(up, "mp", 2), plan.group_swap(down, 1)
     cls = cls.reshape(dim, class_cols)
-    cls_across = plan.swap(tied(cls, up_across), "mp", 2)
     image_total = images[0, 0]
     *attended, logs = attend(plan, ids, starts, widths, q, k, v, seg_col, seg_row)
 
     (middle, second_low, active, slope), attended, up_mates, down_mates = feed_up(
         plan, tokens, attended, params, out_w, up, up_across, down, down_across
     )
+    cls_across = plan.swap(tied(cls, middle), "mp", 2)
     up = [up, up_across, *up_mates]
     down = [down, down_across, *down_mates]
     result, block_rows, pool = feed_down(plan, ids, middle, active, seg_row, params, down)
@@ -1491,16 +1514,19 @@
 
     block_rows = lax.optimization_barrier((block_rows, stats))[0]
     block_across = plan.swap(block_rows, "mp", 2)
-    block_mate, block_mate_across = plan.swap(block_rows, "mp", 1), plan.swap(block_across, "mp", 1)
-    block_out = assemble(plan, ids, [block_rows, block_across, block_mate, block_mate_across], BF16, "block_out")
 
     result_low, hidden_low, middle_low, middle_grad, *rest = feed_back(
         plan, ids, result, middle, slope, row_grads, stats, seg_col, params, out_w, up, down, cols
     )
     attended_grads, sums = rest[:n_mp], rest[n_mp]
     cls_blocks = cls_blocks.reshape(2, plan.groups // 2, plan.block, class_cols)
-    kept, sent, cls_sum, arrived = weight_grads(
-        plan, [(result_low, active), (second_low, hidden_low)], (middle_low, attended), cls_blocks, attended_grads[1:]
+    kept, sent, cls_sum, arrived, block_out = weight_grads(
+        plan,
+        [(result_low, active), (second_low, hidden_low)],
+        (middle_low, attended),
+        cls_blocks,
+        attended_grads[1:],
+        (block_rows, block_across),
     )
     grad_parts = [attended_grads[0]] + list(arrived)
     got = [plan.swap(sent[0], "mp", 2)] + [plan.group_swap(part, 1) for part in sent[1:]]
@@ -1512,7 +1538,7 @@
         )
         proj_grads.append(grad)
         gain_sums.append(gain_sum)
-    *got, block_out, _ = lax.optimization_barrier((*got, block_out, proj_grads[-1][0]))
+    *got, _ = lax.optimization_barrier((*got, proj_grads[-1][0]))
 
     down_pair, up_pair, out_pair = zip(kept, got)
     last_rows, grad_qkv, small_grads, owned = finish(
@@ -1521,27 +1547,21 @@
     mean_loss = small_grads[10, 0] / image_total
     grad_qkv = plan.unmerged(grad_qkv, 1)
     grad_up, grad_out, grad_down, grad_cls = (plan.unmerged(a, 0) for a in owned)
-    grad_out, grad_down, grad_cls = grad_out[:, :cols].T, grad_down.T, grad_cls[:, :classes]
-    input_grad = assemble(plan, ids, [last_rows], F32, "input_grad")
+    matrices = [
+        (w_qkv, m_qkv, v_qkv, grad_qkv),
+        (w_out, m_out, v_out, grad_out[:, :cols].T),
+        (w_up, m_up, v_up, grad_up),
+        (w_down.T, m_down.T, v_down.T, grad_down),
+        (w_cls, m_cls, v_cls, grad_cls),
+    ]
+    input_grad, fresh = update(plan, ids, last_rows, matrices)
     norm_part = lax.dynamic_slice(small_grads, (0, dp * dim_part), (7, dim_part))
     qk_part = lax.dynamic_slice_in_dim(small_grads[8:10, :cols].reshape(2, cols // HEAD, HEAD), dp * head_part, head_part, 2)
-    reduced = (grad_qkv, grad_out, grad_up, grad_down, grad_cls, norm_part, qk_part)
-    groups = (
-        (w_qkv, m_qkv, v_qkv, MATRIX_RATE, MATRIX_DECAY),
-        (w_out, m_out, v_out, MATRIX_RATE, MATRIX_DECAY),
-        (w_up, m_up, v_up, MATRIX_RATE, MATRIX_DECAY),
-        (w_down, m_down, v_down, MATRIX_RATE, MATRIX_DECAY),
-        (w_cls, m_cls, v_cls, MATRIX_RATE, MATRIX_DECAY),
-        (norm_params, m_norm, v_norm, GAIN_RATE, 0.0),
-        (qk_gain, m_qk, v_qk, GAIN_RATE, 0.0),
-    )
-    outputs = [block_out, input_grad, mean_loss]
-    for number, group in enumerate(groups):
-        fresh_one, fresh_two, updated = adam_update(group[0], group[1], group[2], reduced[number], group[3], group[4])
-        if number == 5:
-            outputs = outputs + [fresh_one, fresh_two[:6], fresh_two[6], updated]
-        else:
-            outputs = outputs + [fresh_one, fresh_two, updated]
+    fresh[3] = [a.T for a in fresh[3]]
+    outputs = [block_out, input_grad, mean_loss] + [a for group in fresh for a in group]
+    one, two, new = adam_update(norm_params, m_norm, v_norm, norm_part, GAIN_RATE, 0.0)
+    outputs += [one, two[:6], two[6], new]
+    outputs += list(adam_update(qk_gain, m_qk, v_qk, qk_part, GAIN_RATE, 0.0))
     return tuple(outputs)
 
 

time: 387 us -> 376 us (0.972)
  other arithmetic: 16.7 us -> 10.6 us
  Pallas kernels: 333 us -> 327 us
    sub x7 -> x2, other arithmetic: 6.5 us -> 1.49 us  [adam_update(): weight - step_rate * (one_hat / (jnp.sqrt(two_hat) + ADAM_EPS) + decay_ra...]
    pallas_call x1, Pallas kernels: 17.7 us -> 13.2 us  [feed_down(): pl.pallas_call(kernel, grid_spec=pltpu.PrefetchScalarGridSpec(num_scalar_...]
    ppermute x9 -> x7, starting transfers between devices: 9.13 us -> 6.19 us  [swap(): return lax.ppermute(value, axis, [(i, i ^ bits) for i in range(size)])]
    pallas_call x3 -> x2, Pallas kernels: 81.6 us -> 80.2 us  [the longest x1 69 us: gather_project(): pl.pallas_call(kernel, in_specs=[vmem, vmem, vmem, ANY, ANY, vmem, ANY, v...]
    unnamed x81 -> x47, local copies, waits for them, and re-layouts: 9.15 us -> 9.64 us
  transfers between devices with their start and end apart: 9 -> 7, of which waited for: 0 -> 1; matrix products, arithmetic and copies ran while one was open for 2% -> 2% of each run, Pallas kernels for 42% -> 27%
where the time goes in v1:
time: 376 us; the launch traced here: 369 us
  Pallas kernels  327 us (87%)
  local copies, waits for them, and re-layouts  19.4 us (5%)
  other arithmetic  10.6 us (3%)
  starting transfers between devices  6.19 us (2%)
    pallas_call x1, Pallas kernels, finish(): pl.pallas_call(kernel, in_specs=[ANY] * n_in + [vmem] * len(smalls) + [AN...  80.1 us
    pallas_call x1, Pallas kernels, gather_project(): pl.pallas_call(kernel, in_specs=[vmem, vmem, vmem, ANY, ANY, vmem, ANY, v...  69 us
    pallas_call x3, Pallas kernels, attend_back(): pl.pallas_call(kernel, grid_spec=pltpu.PrefetchScalarGridSpec(num_scalar_...  43.7 us
    pallas_call x1, Pallas kernels, feed_up(): pl.pallas_call(kernel, in_specs=[ANY] * n_load + [pl.BlockSpec(memory_spa...  26.3 us
    pallas_call x1, Pallas kernels, feed_back(): pl.pallas_call(kernel, grid_spec=pltpu.PrefetchScalarGridSpec(num_scalar_...  23.7 us
    pallas_call x1, Pallas kernels, weight_grads(): pl.pallas_call(kernel, in_specs=[ANY] * (n_load + n_mp - 1), out_specs=[A...  21.4 us
    pallas_call x1, Pallas kernels, attend(): pl.pallas_call(kernel, grid_spec=pltpu.PrefetchScalarGridSpec(num_scalar_...  20.1 us
    pallas_call x1, Pallas kernels, classify(): pl.pallas_call(kernel, in_specs=[vmem] * 3 + [ANY] * 2, out_specs=[vmem]...  18.7 us
  transfers between devices with their start and end apart: 7, of which 1 were waited for; matrix products, arithmetic and copies ran while one was open for 2% of the time, Pallas kernels for 27%

profile of v1, /device:TPU:0, one launch (start us, length us, event | category | flops | bytes accessed | tf_op | source)
XLA Modules:
  0.0 369.4 jit_solution(5255339721561429816)
XLA Ops:
  0.7 0.7 reduce_precision.7
  1.5 0.7 reduce_precision.6
  2.1 1.0 copy.69
  3.1 0.7 select_convert_fusion.ones_ref
  3.9 1.6 bitcast_convert_fusion.down_in
  5.5 1.5 convert_reduce_fusion.2
  7.0 0.6 pad.20.out_in
  7.6 1.2 fusion.small_in
  8.9 69.0 %gather_project.1 = (bf16[3072,768]{1,0:T(8,128)(2,1)}, f32[3072,192]{1,0:T(8,128)}, f32[3072,192]{1,0:T(8,128)}, bf16[3072,192]{1,0:T(8,128)(2,1)}, bf16[3072,1...) custom-call(bf16[3072,768]{1,0:T(8,128)(2,1)} %refs_25_.1, ...), custom_call_target="tpu_custom_call" | custom-call | flops 2717908992 | bytes 18874368 | tf_op jit(solution)/shard_map/gather_project/pallas_call | solution.py:397
  77.9 0.6 collective-permute-start
  78.5 1.5 collective-permute-start.1
  80.8 0.5 select_select_fusion
  81.4 0.5 select_select_fusion.1.start_ref
  81.9 1.7 copy.71.col_ref.seg_ref
  83.5 0.6 pad_add_fusion.2.ids_ref
  84.1 0.6 pad_add_fusion.row_ref.seg_ref
  84.8 20.1 %attend.1 = (bf16[768,192]{1,0:T(8,128)(2,1)}, bf16[768,192]{1,0:T(8,128)(2,1)}, bf16[768,192]{1,0:T(8,128)(2,1)}, bf16[768,192]{1,0:T(8,128)(2,1)}, f32[3072,128]{1,0:T(8,128)}) custom-call(s32[2]{0:T(128)} %pad_add_fusion.2.ids_ref, s32[12]{0:T(128)} %select_select_fusion.1.start_ref, s32[12]{0:T(128)} %get-tuple-element.277.width_ref, ...), custom_call_target="tpu_custom_call" | custom-call | flops 36238786560 | bytes 4718592 | tf_op jit(solution)/shard_map/attend/pallas_call | solution.py:516
  105.2 1.0 copy-done.12
  106.6 26.3 %feed_up.1 = (f32[768,768]{1,0:T(8,128)}, bf16[768,768]{1,0:T(8,128)(2,1)}, bf16[768,3072]{1,0:T(8,128)(2,1)}, f32[768,3072]{1,0:T(8,128)}, bf16[768,192]{1,0:T(...) custom-call(bf16[768,192]{1,0:T(8,128)(2,1)} %get-tuple-element.125., ...), custom_call_target="tpu_custom_call" | custom-call | flops 4529848320 | bytes 18874368 | tf_op jit(solution)/shard_map/feed_up/pallas_call | solution.py:738
  132.9 1.7 collective-permute-start.2
  134.6 0.8 reshape.157.label_ref
  135.4 13.2 %feed_down.1 = (f32[768,768]{1,0:T(8,128)}, bf16[768,768]{1,0:T(8,128)(2,1)}, f32[192,896]{1,0:T(8,128)}) custom-call(s32[2]{0:T(128)} %pad_add_fusion.2.ids_ref, f32[768,768]{1,0:T(8,128)} %get-tuple-element.133.mid_ref, bf16[768,3072]{1,0:T(8,128)(2,1)} %get-tuple-element.134.act_ref.refs_1_, s32[3,2,1024]{2,1,0:T(2,128)} %pad_add_fusion.row_ref.seg_ref, ...), custom_call_target="tpu_custom_call" | custom-call | flops 3623878656 | bytes 9437184 | tf_op jit(solution)/shard_map/feed_down/pallas_call | solution.py:809
  148.6 0.8 copy-done.18
  149.4 18.7 %classify.1 = (bf16[192,768]{1,0:T(8,128)(2,1)}, f32[192,128]{1,0:T(8,128)}, f32[8,128]{1,0:T(8,128)}, bf16[8,96,256]{2,1,0:T(8,128)(2,1)}) custom-call(f32[192,896]{1,0:T(8,128)} %get-tuple-element.139.part_ref, s32[192,1]{1,0:T(8,128)} %reshape.157.label_ref, f32[8,128]{1,0:T(8,128)} %get-tuple-element.140.images_ref, bf16[768,256]{1,0:T(8,128)(2,1)} %bitcast.50, ...), custom_call_target="tpu_custom_call" | custom-call | flops 905969664 | bytes 1572864 | tf_op jit(solution)/shard_map/classify/pallas_call | solution.py:898
  168.1 0.7 collective-permute-start.3
  168.8 1.2 slice.42
  170.0 0.6 reshape.156.live_ref
  170.6 23.7 %feed_back.1 = (bf16[768,768]{1,0:T(8,128)(2,1)}, bf16[768,3072]{1,0:T(8,128)(2,1)}, bf16[768,768]{1,0:T(8,128)(2,1)}, f32[768,768]{1,0:T(8,128)}, bf16[768,192]...) custom-call(s32[2]{0:T(128)} %pad_add_fusion.2.ids_ref, ...), custom_call_target="tpu_custom_call" | custom-call | flops 8153726976 | bytes 18874368 | tf_op jit(solution)/shard_map/feed_back/pallas_call | solution.py:998
  194.2 2.2 collective-permute-done.3.refs_11_
  196.5 1.0 copy-done.15
  197.5 21.4 %grads.1 = (f32[4,2,96,768]{3,2,1,0:T(8,128)}, f32[2,4,96,768]{3,2,1,0:T(8,128)}, f32[2,4,96,256]{3,2,1,0:T(8,128)}, bf16[4,2,96,768]{3,2,1,0:T(8,128)(2,1)}, bf...) custom-call(bf16[768,768]{1,0:T(8,128)(2,1)} %get-tuple-element.147., ...), custom_call_target="tpu_custom_call" | custom-call | flops 8455716864 | bytes 18874368 | tf_op jit(solution)/shard_map/grads/pallas_call | solution.py:1099
  218.9 0.7 collective-permute-start.4
  219.6 1.0 collective-permute-start.5
  220.5 14.9 %attend_back.5 = (bf16[1024,192]{1,0:T(8,128)(2,1)}, bf16[1024,192]{1,0:T(8,128)(2,1)}, bf16[1024,192]{1,0:T(8,128)(2,1)}, f32[2,8,192]{2,1,0:T(8,128)}) custom-call(s32[2]{0:T(128)} %pad_add_fusion.2.ids_ref, s32[12]{0:T(128)} %select_select_fusion.1.start_ref, s32[12]{0:T(128)} %get-tuple-element.277.width_ref, s32[12]{0:T(128)} %reshape.156.live_ref, ...), custom_call_target="tpu_custom_call" | custom-call | flops 12079595520 | bytes 4718592 | tf_op jit(solution)/shard_map/attend_back/pallas_call | solution.py:609
  235.5 15.1 %attend_back.4 = (bf16[1024,192]{1,0:T(8,128)(2,1)}, bf16[1024,192]{1,0:T(8,128)(2,1)}, bf16[1024,192]{1,0:T(8,128)(2,1)}, f32[2,8,192]{2,1,0:T(8,128)}) custom-call(s32[2]{0:T(128)} %pad_add_fusion.2.ids_ref, s32[12]{0:T(128)} %select_select_fusion.1.start_ref, s32[12]{0:T(128)} %get-tuple-element.277.width_ref, s32[12]{0:T(128)} %reshape.156.live_ref, ...), custom_call_target="tpu_custom_call" | custom-call | flops 12079595520 | bytes 4718592 | tf_op jit(solution)/shard_map/attend_back/pallas_call | solution.py:609
  250.6 13.6 %attend_back.3 = (bf16[1024,192]{1,0:T(8,128)(2,1)}, bf16[1024,192]{1,0:T(8,128)(2,1)}, bf16[1024,192]{1,0:T(8,128)(2,1)}, f32[2,8,192]{2,1,0:T(8,128)}) custom-call(s32[2]{0:T(128)} %pad_add_fusion.2.ids_ref, s32[12]{0:T(128)} %select_select_fusion.1.start_ref, s32[12]{0:T(128)} %get-tuple-element.277.width_ref, s32[12]{0:T(128)} %reshape.156.live_ref, ...), custom_call_target="tpu_custom_call" | custom-call | flops 12079595520 | bytes 4718592 | tf_op jit(solution)/shard_map/attend_back/pallas_call | solution.py:609
  264.3 0.7 copy-done.2
  265.8 80.1 %finish.1 = (bf16[4,3,256,768]{3,2,1,0:T(8,128)(2,1)}, f32[3,96,192]{2,1,0:T(8,128)}, f32[16,768]{1,0:T(8,128)}, f32[96,768]{1,0:T(8,128)}, f32[96,256]{1,0:T(8,...) custom-call(bf16[3,768,192]{2,1,0:T(8,128)(2,1)} %bitcast.35, bf16[1024,192]{1,0:T(8,128)(2,1)} %get-tuple-element.170.refs_1_, ...), custom_call_target="tpu_custom_call" | custom-call | flops 5435817984 | bytes 18874368 | tf_op jit(solution)/shard_map/finish/pallas_call | solution.py:1360
  345.9 1.2 slice.41
  347.1 0.7 slice.45
  347.9 1.4 multiply_subtract_fusion
  350.0 0.6 copy.84
  350.5 0.6 copy.83
  351.1 0.6 copy.82
  351.7 1.0 copy.77
  352.7 0.7 slice_bitcast_fusion.refs_7_
  354.7 11.1 %update.1 = (f32[3,4,256,768]{3,2,1,0:T(8,128)}, f32[3,96,192]{2,1,0:T(8,128)}, f32[3,96,192]{2,1,0:T(8,128)}, f32[3,96,192]{2,1,0:T(8,128)}, f32[192,96]{1,0:T(...) custom-call(s32[2]{0:T(128)} %pad_add_fusion.2.ids_ref, ...), custom_call_target="tpu_custom_call" | custom-call | bytes 18874368 | tf_op jit(solution)/shard_map/update/pallas_call | solution.py:1404
  365.9 2.2 copy.102
  (70 shorter events, 3.2 us)
Async XLA Ops:
  8.8 71.2 %copy-start.3 = (s32[3072]{0:T(1024)S(1)}, s32[3072]{0:T(1024)}, u32[]{:S(2)}) copy-start(s32[3072]{0:T(1024)} %param.25) | copy-start | bytes 36868
  77.9 27.3 %collective-permute-start = (bf16[768,768]{1,0:T(8,128)(2,1)}, bf16[768,768]{1,0:T(8,128)(2,1)S(1)}, u32[]{:S(2)}, u32[]{:S(2)}) collective-permute-start(bf16[768,768]{1,0:T(8,128)(2,1)} %bitcast.45), channel_id=1, source_target_pairs={{0,2},{1,3},{2,0},{3,1},{4,6},{5,7},{6,4},{7,5},{8,10},{9,11},{10,... | collective-permute-start | bytes 3538952 | tf_op jit(solution)/shard_map/ppermute | solution.py:88
  78.5 26.7 %collective-permute-start.1 = (bf16[2,4,96,768]{3,2,1,0:T(8,128)(2,1)}, bf16[2,4,96,768]{3,2,1,0:T(8,128)(2,1)S(1)}, u32[]{:S(2)}, u32[]{:S(2)}) collective-permute-start(bf16[2,4,96,768]{3,2,1,0:T(8,128)(2,1)} %get-tuple-element.132.refs_8_.refs_0_.refs_4_), channel_id=1, source_target_pairs={{0,4},{4,0},{8,12},{12,8},{16,20},{20,16},{24,28},{28,24},{1,5},{5... | collective-permute-start | bytes 3538952 | tf_op jit(solution)/shard_map/ppermute | solution.py:88
  84.8 20.1 %copy-start.11 = (s32[180]{0:T(256)S(1)}, s32[180]{0:T(256)}, u32[]{:S(2)}) copy-start(s32[180]{0:T(256)} %param.26) | copy-start | bytes 2164
  105.1 1.1 copy-start.12
  105.2 1.4 copy-start.13
  106.6 26.3 %copy-start.16 = (bf16[4,2,96,256]{3,2,1,0:T(8,128)(2,1)S(1)}, bf16[4,2,96,256]{3,2,1,0:T(8,128)(2,1)}, u32[]{:S(2)}) copy-start(bf16[4,2,96,256]{3,2,1,0:T(8,128)(2,1)} %get-tuple-element.141) | copy-start | bytes 1179652
  132.9 15.7 %collective-permute-start.2 = (bf16[768,256]{1,0:T(8,128)(2,1)S(1)}, bf16[768,256]{1,0:T(8,128)(2,1)S(1)}, u32[]{:S(2)}, u32[]{:S(2)}) collective-permute-start(bf16[768,256]{1,0:T(8,128)(2,1)S(1)} %bitcast.51), channel_id=1, source_target_pairs={{0,2},{1,3},{2,0},{3,1},{4,6},{5,7},{6,4},{7,5},{8,10},{9,11},{10,... | collective-permute-start | bytes 1179656 | tf_op jit(solution)/shard_map/ppermute | solution.py:88
  148.6 0.8 copy-start.18
  149.4 18.8 %copy-start.14 = (bf16[768,768]{1,0:T(8,128)(2,1)S(1)}, bf16[768,768]{1,0:T(8,128)(2,1)}, u32[]{:S(2)}) copy-start(bf16[768,768]{1,0:T(8,128)(2,1)} %get-tuple-element.155) | copy-start | bytes 3538948
  168.1 28.3 %collective-permute-start.3 = (bf16[3,256,768]{2,1,0:T(8,128)(2,1)S(1)}, bf16[3,256,768]{2,1,0:T(8,128)(2,1)S(1)}, u32[]{:S(2)}, u32[]{:S(2)}) collective-permute-start(bf16[3,256,768]{2,1,0:T(8,128)(2,1)S(1)} %bitcast.49), channel_id=1, source_target_pairs={{0,2},{1,3},{2,0},{3,1},{4,6},{5,7},{6,4},{7,5},{8,10},{9,11},{10,... | collective-permute-start | bytes 3538952 | tf_op jit(solution)/shard_map/ppermute | solution.py:88
  196.5 1.0 copy-start.15
  218.9 45.4 %collective-permute-start.4 = (bf16[4,2,96,768]{3,2,1,0:T(8,128)(2,1)}, bf16[4,2,96,768]{3,2,1,0:T(8,128)(2,1)S(1)}, u32[]{:S(2)}, u32[]{:S(2)}) collective-permute-start(bf16[4,2,96,768]{3,2,1,0:T(8,128)(2,1)} %get-tuple-element.180), channel_id=1, source_target_pairs={{0,2},{1,3},{2,0},{3,1},{4,6},{5,7},{6,4},{7,5},{8,10},{9,11},{10,... | collective-permute-start | bytes 3538952 | tf_op jit(solution)/shard_map/ppermute | solution.py:88
  219.6 44.8 %collective-permute-start.5 = (bf16[2,4,96,768]{3,2,1,0:T(8,128)(2,1)}, bf16[2,4,96,768]{3,2,1,0:T(8,128)(2,1)S(1)}, u32[]{:S(2)}, u32[]{:S(2)}) collective-permute-start(bf16[2,4,96,768]{3,2,1,0:T(8,128)(2,1)} %get-tuple-element.181), channel_id=1, source_target_pairs={{0,4},{4,0},{8,12},{12,8},{16,20},{20,16},{24,28},{28,24},{1,5},{5... | collective-permute-start | bytes 3538952 | tf_op jit(solution)/shard_map/ppermute | solution.py:88
  235.5 15.1 %copy-start.17 = (bf16[2,4,96,256]{3,2,1,0:T(8,128)(2,1)S(1)}, bf16[2,4,96,256]{3,2,1,0:T(8,128)(2,1)}, u32[]{:S(2)}) copy-start(bf16[2,4,96,256]{3,2,1,0:T(8,128)(2,1)} %get-tuple-element.182) | copy-start | bytes 1179652
  250.6 13.7 %collective-permute-start.6 = (bf16[2,4,96,256]{3,2,1,0:T(8,128)(2,1)S(1)}, bf16[2,4,96,256]{3,2,1,0:T(8,128)(2,1)S(1)}, u32[]{:S(2)}, u32[]{:S(2)}) collective-permute-start(bf16[2,4,96,256]{3,2,1,0:T(8,128)(2,1)S(1)} %copy-done.17), channel_id=1, source_target_pairs={{0,4},{4,0},{8,12},{12,8},{16,20},{20,16},{24,28},{28,24},{1,5},{5... | collective-permute-start | bytes 1179656 | tf_op jit(solution)/shard_map/ppermute | solution.py:88
  264.3 0.7 copy-start.2
  264.3 1.1 copy-start
  264.3 1.5 copy-start.1
  265.8 82.0 %copy-start.4 = (f32[7,96]{1,0:T(8,128)S(1)}, f32[7,96]{1,0:T(8,128)}, u32[]{:S(2)}) copy-start(f32[7,96]{1,0:T(8,128)} %param.42) | copy-start | bytes 8068
  265.8 82.0 %copy-start.6 = (f32[7,96]{1,0:T(8,128)S(1)}, f32[7,96]{1,0:T(8,128)}, u32[]{:S(2)}) copy-start(f32[7,96]{1,0:T(8,128)} %param.44) | copy-start | bytes 8068
  265.8 82.0 %copy-start.7 = (f32[7,96]{1,0:T(8,128)S(1)}, f32[7,96]{1,0:T(8,128)}, u32[]{:S(2)}) copy-start(f32[7,96]{1,0:T(8,128)} %param.43) | copy-start | bytes 8068
  265.8 84.0 %copy-start.5 = (f32[2,3,8]{2,0,1:T(2,128)S(1)}, f32[2,3,8]{2,0,1:T(2,128)}, u32[]{:S(2)}) copy-start(f32[2,3,8]{2,0,1:T(2,128)} %param.45) | copy-start | bytes 580
  265.8 84.0 %copy-start.9 = (f32[2,3,8]{2,0,1:T(2,128)S(1)}, f32[2,3,8]{2,0,1:T(2,128)}, u32[]{:S(2)}) copy-start(f32[2,3,8]{2,0,1:T(2,128)} %param.47) | copy-start | bytes 580
  265.8 84.0 %copy-start.10 = (f32[2,3,8]{2,0,1:T(2,128)S(1)}, f32[2,3,8]{2,0,1:T(2,128)}, u32[]{:S(2)}) copy-start(f32[2,3,8]{2,0,1:T(2,128)} %param.46) | copy-start | bytes 580
  349.3 16.6 %copy-start.8 = (f32[7,96]{1,0:T(8,128)}, f32[7,96]{1,0:T(8,128)S(1)}, u32[]{:S(2)}) copy-start(f32[7,96]{1,0:T(8,128)S(1)} %get-tuple-element.275) | copy-start | bytes 8068
  354.7 11.2 %slice-start = ((s8[4718592]{0:T(1024)(128)(4,1)}), s8[4194304]{0:T(1024)(128)(4,1)S(1)}, s32[]{:S(2)}) async-start(s8[4718592]{0:T(1024)(128)(4,1)} %bitcast.32), calls=%async_computation | async-start | bytes 8388608
  354.7 11.2 %slice-start.1 = ((s8[4718592]{0:T(1024)(128)(4,1)}), s8[524288]{0:T(1024)(128)(4,1)S(1)}, s32[]{:S(2)}) async-start(s8[4718592]{0:T(1024)(128)(4,1)} %bitcast.32), calls=%async_computation.1 | async-start | bytes 1048576

commit v2 on v1

--- a/solution.py
+++ b/solution.py
@@ -460,13 +460,6 @@
     return jnp.where(start % LANES == 0, row_ref[0, 0:1, at], row_ref[0, 1:2, at])
 
 
-def seq_specs(seq, cols):
-    block = lambda c: pl.BlockSpec((QB, c), lambda b, *_: (seq * QBLOCKS + b, 0))
-    all_keys = lambda c: pl.BlockSpec((LEN, c), lambda b, *_: (seq, 0))
-    seg_row = pl.BlockSpec((1, 2, LEN), lambda b, *_: (seq, 0, 0))
-    return block, all_keys, seg_row
-
-
 def attend(plan, ids, starts, widths, q, k, v, seg_col, seg_row):
     rows, cols = q.shape
     n_mp = plan.n_mp
@@ -528,7 +521,7 @@
     )(ids, starts, widths, q, k, v, seg_col, seg_row)
 
 
-def attend_back(plan, seq, ids, starts, widths, live, q, k, v, pq, pk, gains, ones, grads, logs, seg_col, seg_row):
+def attend_back(plan, ids, starts, widths, live, q, k, v, pq, pk, gains, ones, grads, logs, seg_col, seg_row):
     rows, cols = q.shape
     n_mp = plan.n_mp
     share = LEN // n_mp
@@ -536,7 +529,7 @@
 
     def kernel(ids_ref, start_ref, width_ref, live_ref, q_ref, k_ref, v_ref, pq_ref, pk_ref, gain_ref, ones_ref, col_ref, row_ref, log_ref, *refs):
         grad_refs, (gq_ref, gk_ref, gv_ref, sum_ref, dk_ref, dv_ref) = refs[:n_mp], refs[n_mp:]
-        block = pl.program_id(0)
+        seq, block = pl.program_id(0), pl.program_id(1)
         step = seq * QBLOCKS + block
         masks = head_masks(cols)
         heads = len(masks)
@@ -545,6 +538,9 @@
         def _():
             dk_ref[...] = jnp.zeros_like(dk_ref)
             dv_ref[...] = jnp.zeros_like(dv_ref)
+
+        @pl.when(step == 0)
+        def _():
             sum_ref[...] = jnp.zeros_like(sum_ref)
 
         def back(values, grad, slot):
@@ -603,23 +599,25 @@
 
             lax.fori_loop(0, n_mp, keys_back, 0)
 
-    block, all_keys, row_spec = seq_specs(seq, cols)
-    grad_spec = pl.BlockSpec((share, cols), lambda b, *_: (seq, 0))
-    shape = jax.ShapeDtypeStruct((LEN, cols), BF16)
+    block = lambda c: pl.BlockSpec((QB, c), lambda s, b, *_: (s * QBLOCKS + b, 0))
+    all_keys = lambda c: pl.BlockSpec((LEN, c), lambda s, b, *_: (s, 0))
+    row_spec = pl.BlockSpec((1, 2, LEN), lambda s, b, *_: (s, 0, 0))
+    grad_spec = pl.BlockSpec((share, cols), lambda s, b, *_: (s, 0))
+    shape = jax.ShapeDtypeStruct((rows, cols), BF16)
     return pl.pallas_call(
         kernel,
         grid_spec=pltpu.PrefetchScalarGridSpec(
             num_scalar_prefetch=4,
-            grid=(QBLOCKS,),
+            grid=(rows // LEN, QBLOCKS),
             in_specs=[block(cols), all_keys(cols), all_keys(cols), block(cols), all_keys(cols), whole(gains.shape), whole(ones.shape)]
             + [block(1), row_spec, block(128)]
             + [grad_spec] * n_mp,
-            out_specs=[pl.BlockSpec((QB, cols), lambda b, *_: (b, 0)), whole((LEN, cols)), whole((LEN, cols)), whole((2, 8, cols))],
+            out_specs=[block(cols), all_keys(cols), all_keys(cols), whole((2, 8, cols))],
             scratch_shapes=[pltpu.VMEM((LEN, cols), F32), pltpu.VMEM((LEN, cols), F32)],
         ),
         out_shape=[shape, shape, shape, jax.ShapeDtypeStruct((2, 8, cols), F32)],
         compiler_params=PARAMS,
-        cost_estimate=cost(60 * LEN * LEN * cols, LEN * cols * 24, LEN * LEN),
+        cost_estimate=cost(60 * rows * LEN * cols, rows * cols * 24, rows * LEN),
         name="attend_back",
     )(ids, starts, widths, live, q, k, v, pq, pk, gains, ones, seg_col, seg_row, logs, *grads)
 
@@ -1127,7 +1125,7 @@
 
 
 def finish(plan, low, proj_grads, w, middle_grad, tokens, params, row_sums, gain_sums, loss, zx, yz, z_only):
-    seqs = len(proj_grads)
+    seqs = low.shape[0] // LEN
     dim = low.shape[1]
     cols = w.shape[2]
     n_mp = plan.n_mp
@@ -1137,16 +1135,16 @@
     far = [2 * k * merge for k in range(1, lines)]
     partners = [("mp", 1), ("mp", 2)] + [("dp", b) for b in sorted(set(dp_bits + far + [merge]))]
     stages = [("mp", 1), ("mp", 2)] + [("dp", b) for b in dp_bits]
-    inputs = [w] + [g for seq in proj_grads for g in seq] + [a for pair in zx + yz for a in pair] + list(z_only)
+    inputs = [w] + list(proj_grads) + [a for pair in zx + yz for a in pair] + list(z_only)
     inputs += [low, middle_grad]
-    smalls = [params, row_sums, loss] + list(gain_sums)
+    smalls = [params, row_sums, loss, gain_sums]
     n_in = len(inputs)
     n_zx, n_yz, n_z = len(zx), len(yz), len(z_only)
     n_sems = (lines - 1) * (n_zx + n_yz + n_z + 1) + n_zx + n_yz + 1 + 4 * seqs + len(stages)
     n_out = 3 + n_zx + n_yz + n_z
 
     def kernel(*refs):
-        sources, (norm_ref, row_sum_ref, loss_ref, *gain_refs), refs = refs[:n_in], refs[n_in : n_in + 3 + seqs], refs[n_in + 3 + seqs :]
+        sources, (norm_ref, row_sum_ref, loss_ref, gain_ref), refs = refs[:n_in], refs[n_in : n_in + 4], refs[n_in + 4 :]
         tokens_in, refs = refs[0], refs[1:]
         rows_ref, qkv_out, total_ref, *owned = refs[:n_out]
         zx_out, yz_out, z_out = owned[:n_zx], owned[n_zx : n_zx + n_yz], owned[n_zx + n_yz :]
@@ -1167,7 +1165,7 @@
         net.meet(partners)
         others = range(1, lines)
         to_z = lambda src, dst, k: copy(src, dst, "dp", 2 * k * merge)
-        pair_from = 1 + 3 * seqs
+        pair_from = 4
         pair = lambda i: (loads[pair_from + 2 * i], loads[pair_from + 2 * i + 1])
         both = lambda a, b, *at: a[at].astype(F32) + b[at].astype(F32)
         z_from = pair_from + 2 * (n_zx + n_yz)
@@ -1192,7 +1190,7 @@
                 z_copies.append(to_z(z_low[i].at[k - 1], z_got[i].at[k - 1], k))
 
         w_ref = loads[0]
-        pg = [[loads.targets[1 + 3 * s + p] for p in range(3)] for s in range(seqs)]
+        pg = [[loads[1 + p].at[pl.ds(s * LEN, LEN)] for p in range(3)] for s in range(seqs)]
         core_copies = []
         x_copies = []
 
@@ -1203,9 +1201,6 @@
             t_mine[s] = t_keep[s, 0].astype(F32) + t_got[s, 0].astype(F32)
 
         for s in range(seqs):
-            for p in range(3):
-                loads[1 + 3 * s + p]
-
             def terms(target, i, carry):
                 to_other = i // 2
                 row_side = side + i % 2 * (1 - 2 * side)
@@ -1250,8 +1245,7 @@
         for n in range(5):
             total_ref[2 + n : 3 + n, :] = jnp.sum(row_sum_ref[n], axis=0, keepdims=True)
         for n in range(2):
-            gain_sum = sum(jnp.sum(ref[n], axis=0, keepdims=True) for ref in gain_refs)
-            total_ref[8 + n : 9 + n, 0:cols] = gain_sum
+            total_ref[8 + n : 9 + n, 0:cols] = jnp.sum(gain_ref[n], axis=0, keepdims=True)
         total_ref[10:11, 0:128] = loss_ref[0:1, :]
         row_copies = []
         q_copies = []
@@ -1531,14 +1525,10 @@
     grad_parts = [attended_grads[0]] + list(arrived)
     got = [plan.swap(sent[0], "mp", 2)] + [plan.group_swap(part, 1) for part in sent[1:]]
 
-    proj_grads, gain_sums = [], []
-    for s in range(seqs):
-        *grad, gain_sum = attend_back(
-            plan, s, ids, starts, widths, live, q, k, v, pq, pk, gains, ones, grad_parts, logs, seg_col, seg_row
-        )
-        proj_grads.append(grad)
-        gain_sums.append(gain_sum)
-    *got, _ = lax.optimization_barrier((*got, proj_grads[-1][0]))
+    *proj_grads, gain_sums = attend_back(
+        plan, ids, starts, widths, live, q, k, v, pq, pk, gains, ones, grad_parts, logs, seg_col, seg_row
+    )
+    *got, _ = lax.optimization_barrier((*got, proj_grads[0]))
 
     down_pair, up_pair, out_pair = zip(kept, got)
     last_rows, grad_qkv, small_grads, owned = finish(

time: 376 us -> 369 us (0.981)
  Pallas kernels: 327 us -> 318 us
    pallas_call x3 -> x1, Pallas kernels: 43.7 us -> 35.4 us  [attend_back(): pl.pallas_call(kernel, grid_spec=pltpu.PrefetchScalarGridSpec(num_scalar_...]
    unnamed x47 -> x45, local copies, waits for them, and re-layouts: 9.64 us -> 9.58 us
  transfers between devices with their start and end apart: 7 -> 7, of which waited for: 1 -> 1; matrix products, arithmetic and copies ran while one was open for 2% -> 2% of each run, Pallas kernels for 27% -> 25%
where the time goes in v2:
time: 369 us; the launch traced here: 362 us
  Pallas kernels  318 us (86%)
  local copies, waits for them, and re-layouts  19.4 us (5%)
  other arithmetic  10.6 us (3%)
  starting transfers between devices  7.29 us (2%)
  between operations  3.9 us (1%)
    pallas_call x1, Pallas kernels, finish(): pl.pallas_call(kernel, in_specs=[ANY] * n_in + [vmem] * len(smalls) + [AN...  79.7 us
    pallas_call x1, Pallas kernels, gather_project(): pl.pallas_call(kernel, in_specs=[vmem, vmem, vmem, ANY, ANY, vmem, ANY, v...  69 us
    pallas_call x1, Pallas kernels, attend_back(): pl.pallas_call(kernel, grid_spec=pltpu.PrefetchScalarGridSpec(num_scalar_...  35.4 us
    pallas_call x1, Pallas kernels, feed_up(): pl.pallas_call(kernel, in_specs=[ANY] * n_load + [pl.BlockSpec(memory_spa...  26.3 us
    pallas_call x1, Pallas kernels, feed_back(): pl.pallas_call(kernel, grid_spec=pltpu.PrefetchScalarGridSpec(num_scalar_...  23.6 us
    pallas_call x1, Pallas kernels, weight_grads(): pl.pallas_call(kernel, in_specs=[ANY] * (n_load + n_mp - 1), out_specs=[A...  21.5 us
    pallas_call x1, Pallas kernels, attend(): pl.pallas_call(kernel, grid_spec=pltpu.PrefetchScalarGridSpec(num_scalar_...  19.5 us
    pallas_call x1, Pallas kernels, classify(): pl.pallas_call(kernel, in_specs=[vmem] * 3 + [ANY] * 2, out_specs=[vmem]...  18.7 us
  transfers between devices with their start and end apart: 7, of which 1 were waited for; matrix products, arithmetic and copies ran while one was open for 2% of the time, Pallas kernels for 25%

profile of v2, /device:TPU:0, one launch (start us, length us, event | category | flops | bytes accessed | tf_op | source)
XLA Modules:
  0.0 361.9 jit_solution(1600051232954865964)
XLA Ops:
  0.7 0.7 reduce_precision.7
  1.5 0.7 reduce_precision.6
  2.1 1.0 copy.67
  3.1 0.7 select_convert_fusion.ones_ref
  3.9 1.6 bitcast_convert_fusion.down_in
  5.5 1.5 convert_reduce_fusion.2
  7.0 0.6 pad.20.out_in
  7.6 1.2 fusion.small_in
  8.9 69.0 %gather_project.1 = (bf16[3072,768]{1,0:T(8,128)(2,1)}, f32[3072,192]{1,0:T(8,128)}, f32[3072,192]{1,0:T(8,128)}, bf16[3072,192]{1,0:T(8,128)(2,1)}, bf16[3072,1...) custom-call(bf16[3072,768]{1,0:T(8,128)(2,1)} %refs_17_.2, ...), custom_call_target="tpu_custom_call" | custom-call | flops 2717908992 | bytes 18874368 | tf_op jit(solution)/shard_map/gather_project/pallas_call | solution.py:397
  77.9 0.6 collective-permute-start
  78.5 1.5 collective-permute-start.1
  80.8 0.5 select_select_fusion
  81.4 0.5 select_select_fusion.1.start_ref
  81.9 1.7 copy.69.col_ref.seg_ref
  83.5 0.6 pad_add_fusion.2.ids_ref
  84.1 0.6 pad_add_fusion.row_ref.seg_ref
  84.8 19.5 %attend.1 = (bf16[768,192]{1,0:T(8,128)(2,1)}, bf16[768,192]{1,0:T(8,128)(2,1)}, bf16[768,192]{1,0:T(8,128)(2,1)}, bf16[768,192]{1,0:T(8,128)(2,1)}, f32[3072,128]{1,0:T(8,128)}) custom-call(s32[2]{0:T(128)} %pad_add_fusion.2.ids_ref, s32[12]{0:T(128)} %select_select_fusion.1.start_ref, s32[12]{0:T(128)} %get-tuple-element.261.width_ref, ...), custom_call_target="tpu_custom_call" | custom-call | flops 36238786560 | bytes 4718592 | tf_op jit(solution)/shard_map/attend/pallas_call | solution.py:509
  104.6 1.0 copy-done.12
  106.0 26.3 %feed_up.1 = (f32[768,768]{1,0:T(8,128)}, bf16[768,768]{1,0:T(8,128)(2,1)}, bf16[768,3072]{1,0:T(8,128)(2,1)}, f32[768,3072]{1,0:T(8,128)}, bf16[768,192]{1,0:T(...) custom-call(bf16[768,192]{1,0:T(8,128)(2,1)} %get-tuple-element.117., ...), custom_call_target="tpu_custom_call" | custom-call | flops 4529848320 | bytes 18874368 | tf_op jit(solution)/shard_map/feed_up/pallas_call | solution.py:736
  132.3 1.7 collective-permute-start.2
  134.0 0.8 reshape.157.label_ref
  134.8 13.5 %feed_down.1 = (f32[768,768]{1,0:T(8,128)}, bf16[768,768]{1,0:T(8,128)(2,1)}, f32[192,896]{1,0:T(8,128)}) custom-call(s32[2]{0:T(128)} %pad_add_fusion.2.ids_ref, f32[768,768]{1,0:T(8,128)} %get-tuple-element.125.mid_ref, bf16[768,3072]{1,0:T(8,128)(2,1)} %get-tuple-element.126.act_ref.refs_1_, s32[3,2,1024]{2,1,0:T(2,128)} %pad_add_fusion.row_ref.seg_ref, ...), custom_call_target="tpu_custom_call" | custom-call | flops 3623878656 | bytes 9437184 | tf_op jit(solution)/shard_map/feed_down/pallas_call | solution.py:807
  148.3 0.8 copy-done.17
  149.1 18.7 %classify.1 = (bf16[192,768]{1,0:T(8,128)(2,1)}, f32[192,128]{1,0:T(8,128)}, f32[8,128]{1,0:T(8,128)}, bf16[8,96,256]{2,1,0:T(8,128)(2,1)}) custom-call(f32[192,896]{1,0:T(8,128)} %get-tuple-element.131.part_ref, s32[192,1]{1,0:T(8,128)} %reshape.157.label_ref, f32[8,128]{1,0:T(8,128)} %get-tuple-element.132.images_ref, bf16[768,256]{1,0:T(8,128)(2,1)} %bitcast.50, ...), custom_call_target="tpu_custom_call" | custom-call | flops 905969664 | bytes 1572864 | tf_op jit(solution)/shard_map/classify/pallas_call | solution.py:896
  167.8 0.6 collective-permute-start.3
  168.5 1.2 slice.42
  169.7 0.6 reshape.156.live_ref
  170.3 23.6 %feed_back.1 = (bf16[768,768]{1,0:T(8,128)(2,1)}, bf16[768,3072]{1,0:T(8,128)(2,1)}, bf16[768,768]{1,0:T(8,128)(2,1)}, f32[768,768]{1,0:T(8,128)}, bf16[768,192]...) custom-call(s32[2]{0:T(128)} %pad_add_fusion.2.ids_ref, ...), custom_call_target="tpu_custom_call" | custom-call | flops 8153726976 | bytes 18874368 | tf_op jit(solution)/shard_map/feed_back/pallas_call | solution.py:996
  193.9 2.3 collective-permute-done.3.refs_11_
  196.2 1.0 copy-done.15
  197.2 21.5 %grads.1 = (f32[4,2,96,768]{3,2,1,0:T(8,128)}, f32[2,4,96,768]{3,2,1,0:T(8,128)}, f32[2,4,96,256]{3,2,1,0:T(8,128)}, bf16[4,2,96,768]{3,2,1,0:T(8,128)(2,1)}, bf...) custom-call(bf16[768,768]{1,0:T(8,128)(2,1)} %get-tuple-element.139., ...), custom_call_target="tpu_custom_call" | custom-call | flops 8455716864 | bytes 18874368 | tf_op jit(solution)/shard_map/grads/pallas_call | solution.py:1097
  218.7 2.0 collective-permute-start.6
  220.7 0.7 collective-permute-start.4
  221.5 35.4 %attend_back.1 = (bf16[3072,192]{1,0:T(8,128)(2,1)}, bf16[3072,192]{1,0:T(8,128)(2,1)}, bf16[3072,192]{1,0:T(8,128)(2,1)}, f32[2,8,192]{2,1,0:T(8,128)}) custom-call(s32[2]{0:T(128)} %pad_add_fusion.2.ids_ref, s32[12]{0:T(128)} %select_select_fusion.1.start_ref, s32[12]{0:T(128)} %get-tuple-element.261.width_ref, s32[12]{0:T(128)} %reshape.156.live_ref, ...), custom_call_target="tpu_custom_call" | custom-call | flops 36238786560 | bytes 14155776 | tf_op jit(solution)/shard_map/attend_back/pallas_call | solution.py:607
  257.0 0.7 copy-done.2
  257.7 0.4 copy-done
  258.5 79.7 %finish.1 = (bf16[4,3,256,768]{3,2,1,0:T(8,128)(2,1)}, f32[3,96,192]{2,1,0:T(8,128)}, f32[16,768]{1,0:T(8,128)}, f32[96,768]{1,0:T(8,128)}, f32[96,256]{1,0:T(8,...) custom-call(bf16[3,768,192]{2,1,0:T(8,128)(2,1)} %bitcast.35, bf16[3072,192]{1,0:T(8,128)(2,1)} %get-tuple-element.162.refs_1_, ...), custom_call_target="tpu_custom_call" | custom-call | flops 5435817984 | bytes 18874368 | tf_op jit(solution)/shard_map/finish/pallas_call | solution.py:1354
  338.2 1.2 slice.41
  339.4 0.7 slice.45
  340.1 1.4 multiply_subtract_fusion
  341.5 0.5 slice_bitcast_fusion.1
  342.2 0.6 copy.80
  342.8 0.6 copy.79
  343.4 0.6 copy.78
  343.9 1.0 copy.73
  344.9 0.7 slice_bitcast_fusion.refs_7_
  346.9 11.1 %update.1 = (f32[3,4,256,768]{3,2,1,0:T(8,128)}, f32[3,96,192]{2,1,0:T(8,128)}, f32[3,96,192]{2,1,0:T(8,128)}, f32[3,96,192]{2,1,0:T(8,128)}, f32[192,96]{1,0:T(...) custom-call(s32[2]{0:T(128)} %pad_add_fusion.2.ids_ref, ...), custom_call_target="tpu_custom_call" | custom-call | bytes 18874368 | tf_op jit(solution)/shard_map/update/pallas_call | solution.py:1398
  358.1 2.2 copy.98
  (66 shorter events, 2.2 us)
Async XLA Ops:
  8.8 71.2 %copy-start.3 = (s32[3072]{0:T(1024)S(1)}, s32[3072]{0:T(1024)}, u32[]{:S(2)}) copy-start(s32[3072]{0:T(1024)} %param.25) | copy-start | bytes 36868
  77.9 26.7 %collective-permute-start = (bf16[768,768]{1,0:T(8,128)(2,1)}, bf16[768,768]{1,0:T(8,128)(2,1)S(1)}, u32[]{:S(2)}, u32[]{:S(2)}) collective-permute-start(bf16[768,768]{1,0:T(8,128)(2,1)} %bitcast.45), channel_id=1, source_target_pairs={{0,2},{1,3},{2,0},{3,1},{4,6},{5,7},{6,4},{7,5},{8,10},{9,11},{10,... | collective-permute-start | bytes 3538952 | tf_op jit(solution)/shard_map/ppermute | solution.py:88
  78.5 26.1 %collective-permute-start.1 = (bf16[2,4,96,768]{3,2,1,0:T(8,128)(2,1)}, bf16[2,4,96,768]{3,2,1,0:T(8,128)(2,1)S(1)}, u32[]{:S(2)}, u32[]{:S(2)}) collective-permute-start(bf16[2,4,96,768]{3,2,1,0:T(8,128)(2,1)} %get-tuple-element.124.refs_8_.refs_0_.refs_4_), channel_id=1, source_target_pairs={{0,4},{4,0},{8,12},{12,8},{16,20},{20,16},{24,28},{28,24},{1,5},{5... | collective-permute-start | bytes 3538952 | tf_op jit(solution)/shard_map/ppermute | solution.py:88
  84.8 19.5 %copy-start.11 = (s32[180]{0:T(256)S(1)}, s32[180]{0:T(256)}, u32[]{:S(2)}) copy-start(s32[180]{0:T(256)} %param.26) | copy-start | bytes 2164
  104.6 1.1 copy-start.12
  104.6 1.4 copy-start.13
  106.0 26.3 %copy-start.16 = (bf16[4,2,96,256]{3,2,1,0:T(8,128)(2,1)S(1)}, bf16[4,2,96,256]{3,2,1,0:T(8,128)(2,1)}, u32[]{:S(2)}) copy-start(bf16[4,2,96,256]{3,2,1,0:T(8,128)(2,1)} %get-tuple-element.133) | copy-start | bytes 1179652
  132.3 16.0 %collective-permute-start.2 = (bf16[768,256]{1,0:T(8,128)(2,1)S(1)}, bf16[768,256]{1,0:T(8,128)(2,1)S(1)}, u32[]{:S(2)}, u32[]{:S(2)}) collective-permute-start(bf16[768,256]{1,0:T(8,128)(2,1)S(1)} %bitcast.51), channel_id=1, source_target_pairs={{0,2},{1,3},{2,0},{3,1},{4,6},{5,7},{6,4},{7,5},{8,10},{9,11},{10,... | collective-permute-start | bytes 1179656 | tf_op jit(solution)/shard_map/ppermute | solution.py:88
  148.3 0.8 copy-start.17
  149.1 18.7 %copy-start.14 = (bf16[768,768]{1,0:T(8,128)(2,1)S(1)}, bf16[768,768]{1,0:T(8,128)(2,1)}, u32[]{:S(2)}) copy-start(bf16[768,768]{1,0:T(8,128)(2,1)} %get-tuple-element.147) | copy-start | bytes 3538948
  167.8 28.4 %collective-permute-start.3 = (bf16[3,256,768]{2,1,0:T(8,128)(2,1)S(1)}, bf16[3,256,768]{2,1,0:T(8,128)(2,1)S(1)}, u32[]{:S(2)}, u32[]{:S(2)}) collective-permute-start(bf16[3,256,768]{2,1,0:T(8,128)(2,1)S(1)} %bitcast.49), channel_id=1, source_target_pairs={{0,2},{1,3},{2,0},{3,1},{4,6},{5,7},{6,4},{7,5},{8,10},{9,11},{10,... | collective-permute-start | bytes 3538952 | tf_op jit(solution)/shard_map/ppermute | solution.py:88
  196.2 1.0 copy-start.15
  218.7 38.3 %collective-permute-start.6 = (bf16[2,4,96,256]{3,2,1,0:T(8,128)(2,1)}, bf16[2,4,96,256]{3,2,1,0:T(8,128)(2,1)S(1)}, u32[]{:S(2)}, u32[]{:S(2)}) collective-permute-start(bf16[2,4,96,256]{3,2,1,0:T(8,128)(2,1)} %get-tuple-element.168), channel_id=1, source_target_pairs={{0,4},{4,0},{8,12},{12,8},{16,20},{20,16},{24,28},{28,24},{1,5},{5... | collective-permute-start | bytes 1179656 | tf_op jit(solution)/shard_map/ppermute | solution.py:88
  220.7 36.3 %collective-permute-start.4 = (bf16[4,2,96,768]{3,2,1,0:T(8,128)(2,1)}, bf16[4,2,96,768]{3,2,1,0:T(8,128)(2,1)S(1)}, u32[]{:S(2)}, u32[]{:S(2)}) collective-permute-start(bf16[4,2,96,768]{3,2,1,0:T(8,128)(2,1)} %get-tuple-element.166), channel_id=1, source_target_pairs={{0,2},{1,3},{2,0},{3,1},{4,6},{5,7},{6,4},{7,5},{8,10},{9,11},{10,... | collective-permute-start | bytes 3538952 | tf_op jit(solution)/shard_map/ppermute | solution.py:88
  221.4 35.6 %collective-permute-start.5 = (bf16[2,4,96,768]{3,2,1,0:T(8,128)(2,1)}, bf16[2,4,96,768]{3,2,1,0:T(8,128)(2,1)S(1)}, u32[]{:S(2)}, u32[]{:S(2)}) collective-permute-start(bf16[2,4,96,768]{3,2,1,0:T(8,128)(2,1)} %get-tuple-element.167), channel_id=1, source_target_pairs={{0,4},{4,0},{8,12},{12,8},{16,20},{20,16},{24,28},{28,24},{1,5},{5... | collective-permute-start | bytes 3538952 | tf_op jit(solution)/shard_map/ppermute | solution.py:88
  256.9 0.8 copy-start.2
  256.9 1.2 copy-start
  257.0 1.5 copy-start.1
  258.4 81.7 %copy-start.4 = (f32[7,96]{1,0:T(8,128)S(1)}, f32[7,96]{1,0:T(8,128)}, u32[]{:S(2)}) copy-start(f32[7,96]{1,0:T(8,128)} %param.42) | copy-start | bytes 8068
  258.4 81.7 %copy-start.6 = (f32[7,96]{1,0:T(8,128)S(1)}, f32[7,96]{1,0:T(8,128)}, u32[]{:S(2)}) copy-start(f32[7,96]{1,0:T(8,128)} %param.44) | copy-start | bytes 8068
  258.4 81.7 %copy-start.7 = (f32[7,96]{1,0:T(8,128)S(1)}, f32[7,96]{1,0:T(8,128)}, u32[]{:S(2)}) copy-start(f32[7,96]{1,0:T(8,128)} %param.43) | copy-start | bytes 8068
  258.4 83.7 %copy-start.5 = (f32[2,3,8]{2,0,1:T(2,128)S(1)}, f32[2,3,8]{2,0,1:T(2,128)}, u32[]{:S(2)}) copy-start(f32[2,3,8]{2,0,1:T(2,128)} %param.45) | copy-start | bytes 580
  258.4 83.7 %copy-start.9 = (f32[2,3,8]{2,0,1:T(2,128)S(1)}, f32[2,3,8]{2,0,1:T(2,128)}, u32[]{:S(2)}) copy-start(f32[2,3,8]{2,0,1:T(2,128)} %param.47) | copy-start | bytes 580
  258.4 83.6 %copy-start.10 = (f32[2,3,8]{2,0,1:T(2,128)S(1)}, f32[2,3,8]{2,0,1:T(2,128)}, u32[]{:S(2)}) copy-start(f32[2,3,8]{2,0,1:T(2,128)} %param.46) | copy-start | bytes 580
  341.5 16.6 %copy-start.8 = (f32[7,96]{1,0:T(8,128)}, f32[7,96]{1,0:T(8,128)S(1)}, u32[]{:S(2)}) copy-start(f32[7,96]{1,0:T(8,128)S(1)} %get-tuple-element.259) | copy-start | bytes 8068
  346.9 11.2 %slice-start = ((s8[4718592]{0:T(1024)(128)(4,1)}), s8[4194304]{0:T(1024)(128)(4,1)S(1)}, s32[]{:S(2)}) async-start(s8[4718592]{0:T(1024)(128)(4,1)} %bitcast.32), calls=%async_computation | async-start | bytes 8388608
  346.9 11.2 %slice-start.1 = ((s8[4718592]{0:T(1024)(128)(4,1)}), s8[524288]{0:T(1024)(128)(4,1)S(1)}, s32[]{:S(2)}) async-start(s8[4718592]{0:T(1024)(128)(4,1)} %bitcast.32), calls=%async_computation.1 | async-start | bytes 1048576

commit v3 on v2

--- a/solution.py
+++ b/solution.py
@@ -1388,7 +1388,10 @@
             for i in range(n):
                 w_ref, m_ref, v_ref, g_ref = sources[4 * i : 4 * i + 4]
                 columns = w_ref.shape[-1]
-                grad = g_ref[...][..., :columns]
+                if w_ref.shape[:-1] == g_ref.shape[:-1]:
+                    grad = g_ref[...][..., :columns]
+                else:
+                    grad = g_ref[...].T[: w_ref.shape[0], :columns]
                 fresh = adam_update(w_ref[...], m_ref[...], v_ref[...], grad, MATRIX_RATE, MATRIX_DECAY)
                 for ref, value in zip(results[3 * i : 3 * i + 3], fresh):
                     ref[...] = value
@@ -1539,7 +1542,7 @@
     grad_up, grad_out, grad_down, grad_cls = (plan.unmerged(a, 0) for a in owned)
     matrices = [
         (w_qkv, m_qkv, v_qkv, grad_qkv),
-        (w_out, m_out, v_out, grad_out[:, :cols].T),
+        (w_out, m_out, v_out, grad_out),
         (w_up, m_up, v_up, grad_up),
         (w_down.T, m_down.T, v_down.T, grad_down),
         (w_cls, m_cls, v_cls, grad_cls),

time: 369 us -> 368 us (level)
  transfers between devices with their start and end apart: 7 -> 7, of which waited for: 1 -> 2; matrix products, arithmetic and copies ran while one was open for 2% -> 2% of each run, Pallas kernels for 25% -> 25%
where the time goes in v3:
time: 368 us; the launch traced here: 362 us
  Pallas kernels  320 us (87%)
  local copies, waits for them, and re-layouts  17.3 us (5%)
  other arithmetic  10.6 us (3%)
  starting transfers between devices  7.16 us (2%)
  between operations  3.88 us (1%)
    pallas_call x1, Pallas kernels, finish(): pl.pallas_call(kernel, in_specs=[ANY] * n_in + [vmem] * len(smalls) + [AN...  81.3 us
    pallas_call x1, Pallas kernels, gather_project(): pl.pallas_call(kernel, in_specs=[vmem, vmem, vmem, ANY, ANY, vmem, ANY, v...  69 us
    pallas_call x1, Pallas kernels, attend_back(): pl.pallas_call(kernel, grid_spec=pltpu.PrefetchScalarGridSpec(num_scalar_...  33.5 us
    pallas_call x1, Pallas kernels, feed_up(): pl.pallas_call(kernel, in_specs=[ANY] * n_load + [pl.BlockSpec(memory_spa...  26.3 us
    pallas_call x1, Pallas kernels, feed_back(): pl.pallas_call(kernel, grid_spec=pltpu.PrefetchScalarGridSpec(num_scalar_...  23.6 us
    pallas_call x1, Pallas kernels, weight_grads(): pl.pallas_call(kernel, in_specs=[ANY] * (n_load + n_mp - 1), out_specs=[A...  21.5 us
    pallas_call x1, Pallas kernels, attend(): pl.pallas_call(kernel, grid_spec=pltpu.PrefetchScalarGridSpec(num_scalar_...  21 us
    pallas_call x1, Pallas kernels, classify(): pl.pallas_call(kernel, in_specs=[vmem] * 3 + [ANY] * 2, out_specs=[vmem]...  18.7 us
  transfers between devices with their start and end apart: 7, of which 2 were waited for; matrix products, arithmetic and copies ran while one was open for 2% of the time, Pallas kernels for 25%

profile of v3, /device:TPU:0, one launch (start us, length us, event | category | flops | bytes accessed | tf_op | source)
XLA Modules:
  0.0 362.2 jit_solution(15242873938109650220)
XLA Ops:
  0.7 0.7 reduce_precision.7
  1.5 0.7 reduce_precision.6
  2.1 1.0 copy.65
  3.1 0.7 select_convert_fusion.ones_ref
  3.9 1.6 bitcast_convert_fusion.down_in
  5.5 1.5 convert_reduce_fusion.2
  7.0 0.6 pad.20.out_in
  7.6 1.2 fusion.small_in
  8.9 69.0 %gather_project.1 = (bf16[3072,768]{1,0:T(8,128)(2,1)}, f32[3072,192]{1,0:T(8,128)}, f32[3072,192]{1,0:T(8,128)}, bf16[3072,192]{1,0:T(8,128)(2,1)}, bf16[3072,1...) custom-call(bf16[3072,768]{1,0:T(8,128)(2,1)} %refs_17_.2, ...), custom_call_target="tpu_custom_call" | custom-call | flops 2717908992 | bytes 18874368 | tf_op jit(solution)/shard_map/gather_project/pallas_call | solution.py:397
  77.9 0.6 collective-permute-start
  78.5 1.5 collective-permute-start.1
  80.4 0.3 convert_reduce_fusion.1
  80.8 0.5 select_select_fusion
  81.4 0.5 select_select_fusion.1.start_ref
  81.9 1.7 copy.67.col_ref.seg_ref
  83.5 0.6 pad_add_fusion.2.ids_ref
  84.1 0.6 pad_add_fusion.row_ref.seg_ref
  84.8 21.0 %attend.1 = (bf16[768,192]{1,0:T(8,128)(2,1)}, bf16[768,192]{1,0:T(8,128)(2,1)}, bf16[768,192]{1,0:T(8,128)(2,1)}, bf16[768,192]{1,0:T(8,128)(2,1)}, f32[3072,128]{1,0:T(8,128)}) custom-call(s32[2]{0:T(128)} %pad_add_fusion.2.ids_ref, s32[12]{0:T(128)} %select_select_fusion.1.start_ref, s32[12]{0:T(128)} %get-tuple-element.261.width_ref, ...), custom_call_target="tpu_custom_call" | custom-call | flops 36238786560 | bytes 4718592 | tf_op jit(solution)/shard_map/attend/pallas_call | solution.py:509
  106.0 1.0 copy-done.12
  107.1 0.3 copy-done.13
  107.4 26.3 %feed_up.1 = (f32[768,768]{1,0:T(8,128)}, bf16[768,768]{1,0:T(8,128)(2,1)}, bf16[768,3072]{1,0:T(8,128)(2,1)}, f32[768,3072]{1,0:T(8,128)}, bf16[768,192]{1,0:T(...) custom-call(bf16[768,192]{1,0:T(8,128)(2,1)} %get-tuple-element.117., ...), custom_call_target="tpu_custom_call" | custom-call | flops 4529848320 | bytes 18874368 | tf_op jit(solution)/shard_map/feed_up/pallas_call | solution.py:736
  133.8 1.7 collective-permute-start.2
  135.5 0.8 reshape.157.label_ref
  136.3 13.5 %feed_down.1 = (f32[768,768]{1,0:T(8,128)}, bf16[768,768]{1,0:T(8,128)(2,1)}, f32[192,896]{1,0:T(8,128)}) custom-call(s32[2]{0:T(128)} %pad_add_fusion.2.ids_ref, f32[768,768]{1,0:T(8,128)} %get-tuple-element.125.mid_ref, bf16[768,3072]{1,0:T(8,128)(2,1)} %get-tuple-element.126.act_ref.refs_1_, s32[3,2,1024]{2,1,0:T(2,128)} %pad_add_fusion.row_ref.seg_ref, ...), custom_call_target="tpu_custom_call" | custom-call | flops 3623878656 | bytes 9437184 | tf_op jit(solution)/shard_map/feed_down/pallas_call | solution.py:807
  149.8 0.8 copy-done.17
  150.5 18.7 %classify.1 = (bf16[192,768]{1,0:T(8,128)(2,1)}, f32[192,128]{1,0:T(8,128)}, f32[8,128]{1,0:T(8,128)}, bf16[8,96,256]{2,1,0:T(8,128)(2,1)}) custom-call(f32[192,896]{1,0:T(8,128)} %get-tuple-element.131.part_ref, s32[192,1]{1,0:T(8,128)} %reshape.157.label_ref, f32[8,128]{1,0:T(8,128)} %get-tuple-element.132.images_ref, bf16[768,256]{1,0:T(8,128)(2,1)} %bitcast.48, ...), custom_call_target="tpu_custom_call" | custom-call | flops 905969664 | bytes 1572864 | tf_op jit(solution)/shard_map/classify/pallas_call | solution.py:896
  169.3 0.7 collective-permute-start.3
  169.9 1.2 slice.38
  171.1 0.6 reshape.156.live_ref
  171.7 23.6 %feed_back.1 = (bf16[768,768]{1,0:T(8,128)(2,1)}, bf16[768,3072]{1,0:T(8,128)(2,1)}, bf16[768,768]{1,0:T(8,128)(2,1)}, f32[768,768]{1,0:T(8,128)}, bf16[768,192]...) custom-call(s32[2]{0:T(128)} %pad_add_fusion.2.ids_ref, ...), custom_call_target="tpu_custom_call" | custom-call | flops 8153726976 | bytes 18874368 | tf_op jit(solution)/shard_map/feed_back/pallas_call | solution.py:996
  195.3 2.3 collective-permute-done.3.refs_11_
  197.6 1.0 copy-done.15
  198.7 21.5 %grads.1 = (f32[4,2,96,768]{3,2,1,0:T(8,128)}, f32[2,4,96,768]{3,2,1,0:T(8,128)}, f32[2,4,96,256]{3,2,1,0:T(8,128)}, bf16[4,2,96,768]{3,2,1,0:T(8,128)(2,1)}, bf...) custom-call(bf16[768,768]{1,0:T(8,128)(2,1)} %get-tuple-element.139., ...), custom_call_target="tpu_custom_call" | custom-call | flops 8455716864 | bytes 18874368 | tf_op jit(solution)/shard_map/grads/pallas_call | solution.py:1097
  220.2 0.6 collective-permute-start.4
  220.8 2.0 collective-permute-start.5
  222.8 33.5 %attend_back.1 = (bf16[3072,192]{1,0:T(8,128)(2,1)}, bf16[3072,192]{1,0:T(8,128)(2,1)}, bf16[3072,192]{1,0:T(8,128)(2,1)}, f32[2,8,192]{2,1,0:T(8,128)}) custom-call(s32[2]{0:T(128)} %pad_add_fusion.2.ids_ref, s32[12]{0:T(128)} %select_select_fusion.1.start_ref, s32[12]{0:T(128)} %get-tuple-element.261.width_ref, s32[12]{0:T(128)} %reshape.156.live_ref, ...), custom_call_target="tpu_custom_call" | custom-call | flops 36238786560 | bytes 14155776 | tf_op jit(solution)/shard_map/attend_back/pallas_call | solution.py:607
  256.3 1.1 collective-permute-done.5.refs_5_
  257.4 1.0 copy-done.1
  258.4 81.3 %finish.1 = (bf16[4,3,256,768]{3,2,1,0:T(8,128)(2,1)}, f32[3,96,192]{2,1,0:T(8,128)}, f32[16,768]{1,0:T(8,128)}, f32[96,768]{1,0:T(8,128)}, f32[96,256]{1,0:T(8,...) custom-call(bf16[3,768,192]{2,1,0:T(8,128)(2,1)} %bitcast.33, bf16[3072,192]{1,0:T(8,128)(2,1)} %get-tuple-element.162.refs_1_, ...), custom_call_target="tpu_custom_call" | custom-call | flops 5435817984 | bytes 18874368 | tf_op jit(solution)/shard_map/finish/pallas_call | solution.py:1354
  339.8 1.2 slice.37
  341.0 0.7 slice.41
  341.7 1.4 multiply_subtract_fusion
  343.1 0.5 slice_bitcast_fusion
  343.8 0.6 copy.77
  344.4 0.6 copy.76
  344.9 0.6 copy.75
  346.9 11.5 %update.1 = (f32[3,4,256,768]{3,2,1,0:T(8,128)}, f32[3,96,192]{2,1,0:T(8,128)}, f32[3,96,192]{2,1,0:T(8,128)}, f32[3,96,192]{2,1,0:T(8,128)}, f32[192,96]{1,0:T(...) custom-call(s32[2]{0:T(128)} %pad_add_fusion.2.ids_ref, ...), custom_call_target="tpu_custom_call" | custom-call | bytes 18874368 | tf_op jit(solution)/shard_map/update/pallas_call | solution.py:1401
  358.5 2.2 copy.95
  (64 shorter events, 1.3 us)
Async XLA Ops:
  8.8 71.2 %copy-start.3 = (s32[3072]{0:T(1024)S(1)}, s32[3072]{0:T(1024)}, u32[]{:S(2)}) copy-start(s32[3072]{0:T(1024)} %param.25) | copy-start | bytes 36868
  77.9 28.1 %collective-permute-start = (bf16[768,768]{1,0:T(8,128)(2,1)}, bf16[768,768]{1,0:T(8,128)(2,1)S(1)}, u32[]{:S(2)}, u32[]{:S(2)}) collective-permute-start(bf16[768,768]{1,0:T(8,128)(2,1)} %bitcast.43), channel_id=1, source_target_pairs={{0,2},{1,3},{2,0},{3,1},{4,6},{5,7},{6,4},{7,5},{8,10},{9,11},{10,... | collective-permute-start | bytes 3538952 | tf_op jit(solution)/shard_map/ppermute | solution.py:88
  78.5 27.5 %collective-permute-start.1 = (bf16[2,4,96,768]{3,2,1,0:T(8,128)(2,1)}, bf16[2,4,96,768]{3,2,1,0:T(8,128)(2,1)S(1)}, u32[]{:S(2)}, u32[]{:S(2)}) collective-permute-start(bf16[2,4,96,768]{3,2,1,0:T(8,128)(2,1)} %get-tuple-element.124.refs_8_.refs_0_.refs_4_), channel_id=1, source_target_pairs={{0,4},{4,0},{8,12},{12,8},{16,20},{20,16},{24,28},{28,24},{1,5},{5... | collective-permute-start | bytes 3538952 | tf_op jit(solution)/shard_map/ppermute | solution.py:88
  84.8 21.0 %copy-start.11 = (s32[180]{0:T(256)S(1)}, s32[180]{0:T(256)}, u32[]{:S(2)}) copy-start(s32[180]{0:T(256)} %param.26) | copy-start | bytes 2164
  106.0 1.1 copy-start.12
  106.0 1.4 copy-start.13
  107.4 26.3 %copy-start.16 = (bf16[4,2,96,256]{3,2,1,0:T(8,128)(2,1)S(1)}, bf16[4,2,96,256]{3,2,1,0:T(8,128)(2,1)}, u32[]{:S(2)}) copy-start(bf16[4,2,96,256]{3,2,1,0:T(8,128)(2,1)} %get-tuple-element.133) | copy-start | bytes 1179652
  133.8 16.0 %collective-permute-start.2 = (bf16[768,256]{1,0:T(8,128)(2,1)S(1)}, bf16[768,256]{1,0:T(8,128)(2,1)S(1)}, u32[]{:S(2)}, u32[]{:S(2)}) collective-permute-start(bf16[768,256]{1,0:T(8,128)(2,1)S(1)} %bitcast.49), channel_id=1, source_target_pairs={{0,2},{1,3},{2,0},{3,1},{4,6},{5,7},{6,4},{7,5},{8,10},{9,11},{10,... | collective-permute-start | bytes 1179656 | tf_op jit(solution)/shard_map/ppermute | solution.py:88
  149.8 0.8 copy-start.17
  150.5 18.7 %copy-start.14 = (bf16[768,768]{1,0:T(8,128)(2,1)S(1)}, bf16[768,768]{1,0:T(8,128)(2,1)}, u32[]{:S(2)}) copy-start(bf16[768,768]{1,0:T(8,128)(2,1)} %get-tuple-element.147) | copy-start | bytes 3538948
  169.3 28.4 %collective-permute-start.3 = (bf16[3,256,768]{2,1,0:T(8,128)(2,1)S(1)}, bf16[3,256,768]{2,1,0:T(8,128)(2,1)S(1)}, u32[]{:S(2)}, u32[]{:S(2)}) collective-permute-start(bf16[3,256,768]{2,1,0:T(8,128)(2,1)S(1)} %bitcast.47), channel_id=1, source_target_pairs={{0,2},{1,3},{2,0},{3,1},{4,6},{5,7},{6,4},{7,5},{8,10},{9,11},{10,... | collective-permute-start | bytes 3538952 | tf_op jit(solution)/shard_map/ppermute | solution.py:88
  197.6 1.0 copy-start.15
  220.1 36.1 %collective-permute-start.6 = (bf16[2,4,96,256]{3,2,1,0:T(8,128)(2,1)}, bf16[2,4,96,256]{3,2,1,0:T(8,128)(2,1)S(1)}, u32[]{:S(2)}, u32[]{:S(2)}) collective-permute-start(bf16[2,4,96,256]{3,2,1,0:T(8,128)(2,1)} %get-tuple-element.168), channel_id=1, source_target_pairs={{0,4},{4,0},{8,12},{12,8},{16,20},{20,16},{24,28},{28,24},{1,5},{5... | collective-permute-start | bytes 1179656 | tf_op jit(solution)/shard_map/ppermute | solution.py:88
  220.2 36.1 %collective-permute-start.4 = (bf16[4,2,96,768]{3,2,1,0:T(8,128)(2,1)}, bf16[4,2,96,768]{3,2,1,0:T(8,128)(2,1)S(1)}, u32[]{:S(2)}, u32[]{:S(2)}) collective-permute-start(bf16[4,2,96,768]{3,2,1,0:T(8,128)(2,1)} %get-tuple-element.166), channel_id=1, source_target_pairs={{0,2},{1,3},{2,0},{3,1},{4,6},{5,7},{6,4},{7,5},{8,10},{9,11},{10,... | collective-permute-start | bytes 3538952 | tf_op jit(solution)/shard_map/ppermute | solution.py:88
  220.8 36.6 %collective-permute-start.5 = (bf16[2,4,96,768]{3,2,1,0:T(8,128)(2,1)}, bf16[2,4,96,768]{3,2,1,0:T(8,128)(2,1)S(1)}, u32[]{:S(2)}, u32[]{:S(2)}) collective-permute-start(bf16[2,4,96,768]{3,2,1,0:T(8,128)(2,1)} %get-tuple-element.167), channel_id=1, source_target_pairs={{0,4},{4,0},{8,12},{12,8},{16,20},{20,16},{24,28},{28,24},{1,5},{5... | collective-permute-start | bytes 3538952 | tf_op jit(solution)/shard_map/ppermute | solution.py:88
  256.3 1.1 copy-start.2
  256.3 1.2 copy-start
  257.4 1.0 copy-start.1
  258.4 83.2 %copy-start.4 = (f32[7,96]{1,0:T(8,128)S(1)}, f32[7,96]{1,0:T(8,128)}, u32[]{:S(2)}) copy-start(f32[7,96]{1,0:T(8,128)} %param.42) | copy-start | bytes 8068
  258.4 83.2 %copy-start.6 = (f32[7,96]{1,0:T(8,128)S(1)}, f32[7,96]{1,0:T(8,128)}, u32[]{:S(2)}) copy-start(f32[7,96]{1,0:T(8,128)} %param.44) | copy-start | bytes 8068
  258.4 83.2 %copy-start.7 = (f32[7,96]{1,0:T(8,128)S(1)}, f32[7,96]{1,0:T(8,128)}, u32[]{:S(2)}) copy-start(f32[7,96]{1,0:T(8,128)} %param.43) | copy-start | bytes 8068
  258.4 85.2 %copy-start.5 = (f32[2,3,8]{2,0,1:T(2,128)S(1)}, f32[2,3,8]{2,0,1:T(2,128)}, u32[]{:S(2)}) copy-start(f32[2,3,8]{2,0,1:T(2,128)} %param.45) | copy-start | bytes 580
  258.4 85.2 %copy-start.9 = (f32[2,3,8]{2,0,1:T(2,128)S(1)}, f32[2,3,8]{2,0,1:T(2,128)}, u32[]{:S(2)}) copy-start(f32[2,3,8]{2,0,1:T(2,128)} %param.47) | copy-start | bytes 580
  258.4 85.2 %copy-start.10 = (f32[2,3,8]{2,0,1:T(2,128)S(1)}, f32[2,3,8]{2,0,1:T(2,128)}, u32[]{:S(2)}) copy-start(f32[2,3,8]{2,0,1:T(2,128)} %param.46) | copy-start | bytes 580
  343.1 15.4 %copy-start.8 = (f32[7,96]{1,0:T(8,128)}, f32[7,96]{1,0:T(8,128)S(1)}, u32[]{:S(2)}) copy-start(f32[7,96]{1,0:T(8,128)S(1)} %get-tuple-element.259) | copy-start | bytes 8068
  346.9 11.6 %slice-start = ((s8[4718592]{0:T(1024)(128)(4,1)}), s8[4194304]{0:T(1024)(128)(4,1)S(1)}, s32[]{:S(2)}) async-start(s8[4718592]{0:T(1024)(128)(4,1)} %bitcast.30), calls=%async_computation | async-start | bytes 8388608
  346.9 11.6 %slice-start.1 = ((s8[4718592]{0:T(1024)(128)(4,1)}), s8[524288]{0:T(1024)(128)(4,1)S(1)}, s32[]{:S(2)}) async-start(s8[4718592]{0:T(1024)(128)(4,1)} %bitcast.30), calls=%async_computation.1 | async-start | bytes 1048576
